TPU v7x, 32 devices: a whole 2x2x4 slice. The times are simulated.
32 devices in a mesh: dp: 16 (over z, y, x), tensor: 2 (over core).
Axes of the slice: x: 2, y: 2, z: 4, core: 2. Of those that a mesh axis runs over, the one named last changes fastest.
Arguments:
- layer_input: bfloat16 [10240, 1536], P(('dp', 'tensor')), may hold values from -6 to 6
- out_cotangent: bfloat16 [10240, 1536], P(('dp', 'tensor')), may hold values from -6 to 6
- positions: int32 [10240], P('dp'), may hold values from 0 to 2559, as said below
- segment_ids: int32 [10240], replicated, may hold values from 0 to 25, as said below
- parent_ids: int32 [26], replicated, may hold values from 0 to 17, as said below
- attention_gain: bfloat16 [1536], P('dp'), may hold values from 0.25 to 1.75
- query_weight: bfloat16 [1536, 1536], P('dp', 'tensor'), may hold values from -0.21875 to 0.21875
- query_bias: bfloat16 [12, 128], P('tensor', 'dp'), may hold values from -3 to 3
- key_weight: bfloat16 [1536, 256], P('dp', 'tensor'), may hold values from -0.15625 to 0.15625
- key_bias: bfloat16 [2, 128], P('tensor', 'dp'), may hold values from -3 to 3
- value_weight: bfloat16 [1536, 256], P('dp', 'tensor'), may hold values from -0.15625 to 0.15625
- value_bias: bfloat16 [2, 128], P('tensor', 'dp'), may hold values from -3 to 3
- output_weight: bfloat16 [1536, 1536], P('tensor', 'dp'), may hold values from -1.75 to 1.75
- feedforward_gain: bfloat16 [1536], P('dp'), may hold values from 0.25 to 1.75
- gate_weight: bfloat16 [1536, 8960], P('dp', 'tensor'), may hold values from -0.15625 to 0.15625
- up_weight: bfloat16 [1536, 8960], P('dp', 'tensor'), may hold values from -0.15625 to 0.15625
- down_weight: bfloat16 [8960, 1536], P('tensor', 'dp'), may hold values from -0.125 to 0.125
Outputs:
- layer_output: bfloat16 [10240, 1536], P(('dp', 'tensor'))
- input_grad: bfloat16 [10240, 1536], P(('dp', 'tensor'))
- attention_gain_grad: float32 [1536], P('dp')
- query_weight_grad: float32 [1536, 1536], P('dp', 'tensor')
- query_bias_grad: float32 [12, 128], P('tensor', 'dp')
- key_weight_grad: float32 [1536, 256], P('dp', 'tensor')
- key_bias_grad: float32 [2, 128], P('tensor', 'dp')
- value_weight_grad: float32 [1536, 256], P('dp', 'tensor')
- value_bias_grad: float32 [2, 128], P('tensor', 'dp')
- output_weight_grad: float32 [1536, 1536], P('tensor', 'dp')
- feedforward_gain_grad: float32 [1536], P('dp')
- gate_weight_grad: float32 [1536, 8960], P('dp', 'tensor')
- up_weight_grad: float32 [1536, 8960], P('dp', 'tensor')
- down_weight_grad: float32 [8960, 1536], P('tensor', 'dp')
Inputs may be any that keep to these rules, and one draw needn't show every extreme that they name: `segment_ids`: the tokens form 2 trees of 5120 consecutive tokens; tree t holds segments 13 t to 13 t + 12: its trunk of 2048 tokens comes first, then its 4 branches of 256 tokens and 8 leaves of 256 tokens in any order, each segment's tokens consecutive. `parent_ids`: A trunk is its own parent; a branch's parent is its tree's trunk; a leaf's parent is a branch of its tree, two leaves to each branch. `positions`: A trunk token's place in its trunk; 2048 plus a branch token's place in its branch; 2304 plus a leaf token's place in its leaf.
All inputs are finite; a program needn't handle non-finite values.
Results may differ from a plain program's by a relative error of at most 0.023.
Values may be sent and summed in bfloat16 or wider, within the bound.
A program may use at most 256 MiB of HBM per device.

v0:
```python
import jax
import jax.numpy as jnp
from jax import lax
from jax.sharding import PartitionSpec as P

SPAN = 8


EPS = 1e-06
NEG = -1e30
THETA = 10000.0


def from_partner(block, axis, apart):
    count = lax.axis_size(axis)
    route = []
    for low in range(count):
        high = low | 1 << apart
        if high != low and high < count:
            route += [(low, high), (high, low)]
    return lax.ppermute(block, axis, route)


def rms_scale(values):
    return lax.rsqrt(jnp.mean(values * values, axis=1, keepdims=True) + EPS)


def norm_apply(values, gain):
    return values * rms_scale(values) * gain


def rotate(values, cosines, sines):
    midpoint = values.shape[-1] // 2
    leading = values[..., :midpoint]
    trailing = values[..., midpoint:]
    return jnp.concatenate(
        [leading * cosines - trailing * sines, trailing * cosines + leading * sines], axis=-1
    )


def rope_tables(positions, head_dim):
    exponents = jnp.arange(head_dim // 2, dtype=jnp.float32) * (2.0 / head_dim)
    frequency = jnp.power(THETA, -exponents)
    angles = positions.astype(jnp.float32)[:, None] * frequency[None, :]
    return (jnp.cos(angles)[:, None, :], jnp.sin(angles)[:, None, :])


def visibility(query_segs, up_one, up_two, query_rows, key_segs, key_rows):
    above = (key_segs[None, :] == up_one[:, None]) | (key_segs[None, :] == up_two[:, None])
    above = above & (key_segs[None, :] != query_segs[:, None])
    same = (key_segs[None, :] == query_segs[:, None]) & (key_rows[None, :] <= query_rows[:, None])
    return above | same


def contract_rows(left, right):
    return lax.dot_general(
        left, right, (((0,), (0,)), ((), ())), preferred_element_type=jnp.float32
    )


def contract_cols(left, right):
    return lax.dot_general(
        left, right, (((1,), (1,)), ((), ())), preferred_element_type=jnp.float32
    )


def tile_scores(query_rot, keys_part, score_scale):
    return (
        jnp.einsum("icgd,jcd->cgij", query_rot, keys_part, preferred_element_type=jnp.float32)
        * score_scale
    )


def tile_probs(query_rot, keys_part, mask, log_total, score_scale):
    scores = tile_scores(query_rot, keys_part, score_scale)
    return jnp.where(mask, jnp.exp(scores - log_total[..., None]), 0.0)


def stats_step(carry, tile, query_rot, score_scale):
    keys_part, values_part, mask, active = tile

    def stats_compute(state):
        top, total = state
        masked = jnp.where(mask, tile_scores(query_rot, keys_part, score_scale), NEG)
        new_top = jnp.maximum(top, jnp.max(masked, axis=-1))
        weights = jnp.where(mask, jnp.exp(masked - new_top[..., None]), 0.0)
        return (new_top, total * jnp.exp(top - new_top) + jnp.sum(weights, axis=-1))

    return lax.cond(active, stats_compute, lambda state: state, carry)


def output_step(carry, tile, query_rot, log_total, score_scale):
    keys_part, values_part, mask, active = tile

    def output_compute(state):
        probs = tile_probs(query_rot, keys_part, mask, log_total, score_scale)
        return state + jnp.einsum(
            "cgij,jcd->icgd",
            probs.astype(jnp.bfloat16),
            values_part,
            preferred_element_type=jnp.float32,
        )

    return lax.cond(active, output_compute, lambda state: state, carry)


def delta_step(carry, tile, query_rot, attended_grad, log_total, score_scale):
    keys_part, values_part, mask, active = tile

    def delta_compute(state):
        probs = tile_probs(query_rot, keys_part, mask, log_total, score_scale)
        prob_grad = jnp.einsum(
            "icgd,jcd->cgij", attended_grad, values_part, preferred_element_type=jnp.float32
        )
        return state + jnp.sum(probs * prob_grad, axis=-1)

    return lax.cond(active, delta_compute, lambda state: state, carry)


def grad_step(carry, tile, query_rot, attended_grad, log_total, delta, score_scale):
    keys_part, values_part, mask, active = tile
    tokens = keys_part.shape[0]
    width = keys_part.shape[1] * keys_part.shape[2]

    def grad_compute(state):
        probs = tile_probs(query_rot, keys_part, mask, log_total, score_scale)
        prob_grad = jnp.einsum(
            "icgd,jcd->cgij", attended_grad, values_part, preferred_element_type=jnp.float32
        )
        score_grad = (probs * (prob_grad - delta[..., None])).astype(jnp.bfloat16)
        state = state + jnp.einsum(
            "cgij,jcd->icgd", score_grad, keys_part, preferred_element_type=jnp.float32
        )
        key_part_grad = (
            jnp.einsum("cgij,icgd->jcd", score_grad, query_rot, preferred_element_type=jnp.float32)
            * score_scale
        )
        value_part_grad = jnp.einsum(
            "cgij,icgd->jcd",
            probs.astype(jnp.bfloat16),
            attended_grad,
            preferred_element_type=jnp.float32,
        )
        joined = jnp.concatenate(
            [key_part_grad.reshape(tokens, width), value_part_grad.reshape(tokens, width)], axis=1
        )
        return (state, joined)

    def skipped(state):
        return (state, jnp.zeros((tokens, 2 * width), jnp.float32))

    return lax.cond(active, grad_compute, skipped, carry)


def on_device(
    layer_input,
    out_cotangent,
    positions,
    segment_ids,
    parent_ids,
    attention_gain,
    query_weight,
    query_bias,
    key_weight,
    key_bias,
    value_weight,
    value_bias,
    output_weight,
    feedforward_gain,
    gate_weight,
    up_weight,
    down_weight,
):

    def fetch_attention():
        return (
            lax.all_gather(attention_gain, "dp", axis=0, tiled=True),
            lax.all_gather(query_weight, "dp", axis=0, tiled=True),
            lax.all_gather(query_bias, "dp", axis=1, tiled=True),
            lax.all_gather(key_weight, "dp", axis=0, tiled=True),
            lax.all_gather(key_bias, "dp", axis=1, tiled=True),
            lax.all_gather(value_weight, "dp", axis=0, tiled=True),
            lax.all_gather(value_bias, "dp", axis=1, tiled=True),
            lax.all_gather(output_weight, "dp", axis=1, tiled=True),
        )

    def fetch_feedforward():
        return (
            lax.all_gather(feedforward_gain, "dp", axis=0, tiled=True),
            lax.all_gather(gate_weight, "dp", axis=0, tiled=True),
            lax.all_gather(up_weight, "dp", axis=0, tiled=True),
            lax.all_gather(down_weight, "dp", axis=1, tiled=True),
        )

    def to_heads(values):
        return lax.all_gather(values, "tensor", axis=0, tiled=True)

    def to_tokens(values):
        return lax.psum_scatter(
            values.astype(jnp.bfloat16), "tensor", scatter_dimension=0, tiled=True
        ).astype(jnp.float32)

    local_tok = positions.shape[0]
    dp_index = lax.axis_index("dp")
    first_row = dp_index * local_tok
    token_ids = jnp.arange(local_tok, dtype=jnp.int32)
    query_rows = first_row + token_ids
    query_segs = lax.dynamic_slice_in_dim(segment_ids, first_row, local_tok)
    seg_numbers = jnp.arange(parent_ids.shape[0], dtype=jnp.int32)
    up_one = jnp.sum(
        jnp.where(query_segs[:, None] == seg_numbers[None, :], parent_ids[None, :], 0), axis=1
    )
    up_two = jnp.sum(
        jnp.where(up_one[:, None] == seg_numbers[None, :], parent_ids[None, :], 0), axis=1
    )
    first_gain, query_mat, query_add, key_mat, key_add, value_mat, value_add, out_mat = (
        fetch_attention()
    )
    heads_here = query_add.shape[0]
    key_heads = key_add.shape[0]
    head_dim = query_add.shape[1]
    groups = heads_here // key_heads
    score_scale = head_dim ** (-0.5)
    key_width = key_heads * head_dim
    input_wide = layer_input.astype(jnp.float32)
    gain_one = first_gain.astype(jnp.float32)
    normed_full = to_heads(norm_apply(input_wide, gain_one).astype(jnp.bfloat16))
    query_pre = jnp.dot(
        normed_full, query_mat, preferred_element_type=jnp.float32
    ) + query_add.reshape(-1).astype(jnp.float32)
    key_pre = jnp.dot(normed_full, key_mat, preferred_element_type=jnp.float32) + key_add.reshape(
        -1
    ).astype(jnp.float32)
    value_all = (
        jnp.dot(normed_full, value_mat, preferred_element_type=jnp.float32)
        + value_add.reshape(-1).astype(jnp.float32)
    ).astype(jnp.bfloat16)
    cosines, sines = rope_tables(positions, head_dim)
    query_flat = query_pre.reshape(local_tok, heads_here, head_dim)
    key_flat = key_pre.reshape(local_tok, key_heads, head_dim)
    query_rot = (
        rotate(query_flat, cosines, sines)
        .astype(jnp.bfloat16)
        .reshape(local_tok, key_heads, groups, head_dim)
    )
    key_rot = rotate(key_flat, cosines, sines).astype(jnp.bfloat16)
    pair_local = jnp.concatenate([key_rot.reshape(local_tok, key_width), value_all], axis=1)
    group_bits = SPAN.bit_length() - 1
    pieces = []
    group_start = dp_index // SPAN * SPAN
    collected = pair_local
    for bit in range(group_bits):
        arrived = from_partner(collected, "dp", bit)
        high_side = (dp_index >> bit) % 2 == 1
        lower = jnp.where(high_side, arrived, collected)
        upper = jnp.where(high_side, collected, arrived)
        collected = jnp.concatenate([lower, upper], axis=0)
    for member in range(SPAN):
        owner = group_start + member
        pieces.append(
            (collected[member * local_tok : (member + 1) * local_tok], owner, jnp.asarray(True))
        )
    tiles = []
    for arrived, owner, valid in pieces:
        key_rows = owner * local_tok + token_ids
        key_segs = lax.dynamic_slice_in_dim(segment_ids, owner * local_tok, local_tok)
        mask = visibility(query_segs, up_one, up_two, query_rows, key_segs, key_rows)
        keys_part = arrived[:, :key_width].reshape(local_tok, key_heads, head_dim)
        values_part = arrived[:, key_width:].reshape(local_tok, key_heads, head_dim)
        tiles.append((keys_part, values_part, mask, jnp.logical_and(valid, jnp.any(mask))))
    stat_shape = (key_heads, groups, local_tok)
    stats = (jnp.full(stat_shape, NEG, jnp.float32), jnp.zeros(stat_shape, jnp.float32))
    for tile in tiles:
        stats = stats_step(stats, tile, query_rot, score_scale)
    log_total = stats[0] + jnp.log(stats[1])
    gathered_out = jnp.zeros((local_tok, key_heads, groups, head_dim), jnp.float32)
    for tile in tiles:
        gathered_out = output_step(gathered_out, tile, query_rot, log_total, score_scale)
    attended = gathered_out.astype(jnp.bfloat16).reshape(local_tok, heads_here * head_dim)
    middle = input_wide + to_tokens(jnp.dot(attended, out_mat, preferred_element_type=jnp.float32))
    second_gain, gate_mat, up_mat, down_mat = fetch_feedforward()
    gain_two = second_gain.astype(jnp.float32)
    normed_two_full = to_heads(norm_apply(middle, gain_two).astype(jnp.bfloat16))
    gate_val = jnp.dot(normed_two_full, gate_mat, preferred_element_type=jnp.float32)
    up_val = jnp.dot(normed_two_full, up_mat, preferred_element_type=jnp.float32)
    product = (jax.nn.silu(gate_val) * up_val).astype(jnp.bfloat16)
    down_part = jnp.dot(product, down_mat, preferred_element_type=jnp.float32)
    layer_output = (middle + to_tokens(down_part)).astype(jnp.bfloat16)
    second_gain, gate_mat, up_mat, down_mat = fetch_feedforward()
    gain_two = second_gain.astype(jnp.float32)
    cotangent_full = to_heads(out_cotangent)
    down_mat_grad = contract_rows(product, cotangent_full)
    product_grad = contract_cols(cotangent_full, down_mat)
    silu_pull = jax.vjp(lambda gate_in, up_in: jax.nn.silu(gate_in) * up_in, gate_val, up_val)[1]
    gate_grad_wide, up_grad_wide = silu_pull(product_grad)
    gate_grad = gate_grad_wide.astype(jnp.bfloat16)
    up_grad = up_grad_wide.astype(jnp.bfloat16)
    gate_mat_grad = contract_rows(normed_two_full, gate_grad)
    up_mat_grad = contract_rows(normed_two_full, up_grad)
    normed_two_grad = to_tokens(contract_cols(gate_grad, gate_mat) + contract_cols(up_grad, up_mat))
    norm_pull = jax.vjp(norm_apply, middle, gain_two)[1]
    middle_norm_grad, gain_two_grad = norm_pull(normed_two_grad)
    middle_grad = out_cotangent.astype(jnp.float32) + middle_norm_grad
    feedforward_grads = (
        lax.psum_scatter(gain_two_grad, "dp", scatter_dimension=0, tiled=True),
        lax.psum_scatter(gate_mat_grad, "dp", scatter_dimension=0, tiled=True),
        lax.psum_scatter(up_mat_grad, "dp", scatter_dimension=0, tiled=True),
        lax.psum_scatter(down_mat_grad, "dp", scatter_dimension=1, tiled=True),
    )
    first_gain, query_mat, query_add, key_mat, key_add, value_mat, value_add, out_mat = (
        fetch_attention()
    )
    gain_one = first_gain.astype(jnp.float32)
    branch_grad = to_heads(middle_grad.astype(jnp.bfloat16))
    out_mat_grad = contract_rows(attended, branch_grad)
    attended_grad = (
        contract_cols(branch_grad, out_mat)
        .astype(jnp.bfloat16)
        .reshape(local_tok, key_heads, groups, head_dim)
    )
    delta = jnp.zeros(stat_shape, jnp.float32)
    for tile in tiles:
        delta = delta_step(delta, tile, query_rot, attended_grad, log_total, score_scale)
    query_rot_grad = jnp.zeros((local_tok, key_heads, groups, head_dim), jnp.float32)
    piece_grads = []
    for tile in tiles:
        query_rot_grad, joined = grad_step(
            query_rot_grad, tile, query_rot, attended_grad, log_total, delta, score_scale
        )
        piece_grads.append(joined)
    remaining = jnp.concatenate(piece_grads, axis=0)
    for bit in reversed(range(group_bits)):
        half_rows = remaining.shape[0] // 2
        lower = remaining[:half_rows]
        upper = remaining[half_rows:]
        high_side = (dp_index >> bit) % 2 == 1
        outgoing = jnp.where(high_side, lower, upper)
        keeping = jnp.where(high_side, upper, lower)
        remaining = keeping + from_partner(outgoing.astype(jnp.bfloat16), "dp", bit).astype(
            outgoing.dtype
        )
    query_rot_grad = (query_rot_grad * score_scale).reshape(local_tok, heads_here, head_dim)
    key_rot_grad = remaining[:, :key_width].reshape(local_tok, key_heads, head_dim)
    value_grad = remaining[:, key_width:].astype(jnp.bfloat16)
    query_turn = jax.vjp(lambda values: rotate(values, cosines, sines), query_flat)[1]
    key_turn = jax.vjp(lambda values: rotate(values, cosines, sines), key_flat)[1]
    query_grad = (
        query_turn(query_rot_grad)[0].reshape(local_tok, heads_here * head_dim).astype(jnp.bfloat16)
    )
    key_grad = key_turn(key_rot_grad)[0].reshape(local_tok, key_width).astype(jnp.bfloat16)
    query_mat_grad = contract_rows(normed_full, query_grad)
    key_mat_grad = contract_rows(normed_full, key_grad)
    value_mat_grad = contract_rows(normed_full, value_grad)
    query_add_grad = jnp.sum(query_grad, axis=0, dtype=jnp.float32).reshape(heads_here, head_dim)
    key_add_grad = jnp.sum(key_grad, axis=0, dtype=jnp.float32).reshape(key_heads, head_dim)
    value_add_grad = jnp.sum(value_grad, axis=0, dtype=jnp.float32).reshape(key_heads, head_dim)
    normed_one_grad = (
        contract_cols(query_grad, query_mat)
        + contract_cols(key_grad, key_mat)
        + contract_cols(value_grad, value_mat)
    )
    normed_one_grad = to_tokens(normed_one_grad)
    first_pull = jax.vjp(norm_apply, input_wide, gain_one)[1]
    input_norm_grad, gain_one_grad = first_pull(normed_one_grad)
    input_grad = (middle_grad + input_norm_grad).astype(jnp.bfloat16)
    attention_grads = (
        lax.psum_scatter(gain_one_grad, "dp", scatter_dimension=0, tiled=True),
        lax.psum_scatter(query_mat_grad, "dp", scatter_dimension=0, tiled=True),
        lax.psum_scatter(query_add_grad, "dp", scatter_dimension=1, tiled=True),
        lax.psum_scatter(key_mat_grad, "dp", scatter_dimension=0, tiled=True),
        lax.psum_scatter(key_add_grad, "dp", scatter_dimension=1, tiled=True),
        lax.psum_scatter(value_mat_grad, "dp", scatter_dimension=0, tiled=True),
        lax.psum_scatter(value_add_grad, "dp", scatter_dimension=1, tiled=True),
        lax.psum_scatter(out_mat_grad, "dp", scatter_dimension=1, tiled=True),
    )
    gain_totals = lax.psum((attention_grads[0], feedforward_grads[0]), "tensor")
    return (
        layer_output,
        input_grad,
        gain_totals[0],
        attention_grads[1],
        attention_grads[2],
        attention_grads[3],
        attention_grads[4],
        attention_grads[5],
        attention_grads[6],
        attention_grads[7],
        gain_totals[1],
        feedforward_grads[1],
        feedforward_grads[2],
        feedforward_grads[3],
    )


def solution(mesh):
    placed = (
        P(("dp", "tensor"), None),
        P(("dp", "tensor"), None),
        P("dp"),
        P(),
        P(),
        P("dp"),
        P("dp", "tensor"),
        P("tensor", "dp"),
        P("dp", "tensor"),
        P("tensor", "dp"),
        P("dp", "tensor"),
        P("tensor", "dp"),
        P("tensor", "dp"),
        P("dp"),
        P("dp", "tensor"),
        P("dp", "tensor"),
        P("tensor", "dp"),
    )
    return jax.shard_map(
        on_device,
        mesh=mesh,
        in_specs=placed,
        out_specs=(
            P(("dp", "tensor"), None),
            P(("dp", "tensor"), None),
            P("dp"),
            P("dp", "tensor"),
            P("tensor", "dp"),
            P("dp", "tensor"),
            P("tensor", "dp"),
            P("dp", "tensor"),
            P("tensor", "dp"),
            P("tensor", "dp"),
            P("dp"),
            P("dp", "tensor"),
            P("dp", "tensor"),
            P("tensor", "dp"),
        ),
        check_vma=False,
    )
```

profile of v0, /device:TPU:0, one launch (start us, length us, event | category | flops | bytes accessed | tf_op | source)
XLA Modules:
  0.0 2916.2 jit_solution(11846835829616408356)
XLA Ops:
  13.3 44.5 %all-reduce.15 = (bf16[1536]{0:T(1024)(128)(2,1)S(1)}, bf16[128]{0:T(256)(128)(2,1)S(1)}, bf16[128]{0:T(256)(128)(2,1)S(1)}, bf16[1536]{0:T(1024)(128)(2,1)S(1)}) all-reduce(bf16[1536]{0:T(1024)(128)(2,1)S(1)} %dynamic-update-slice, bf16[128]{0:T(256)(128)(2,1)S(1)} %dynamic-update-slice.2, ...), channel_id=1, replica_groups=mesh['dp'=16,'tensor'=2] {'dp'}, use_global_device_ids=true, to_apply=%add.4 | all-reduce | flops 3328 | bytes 13312
  63.3 38.6 %all_gather.59 = bf16[1536,128]{1,0:T(8,128)(2,1)S(1)} all-gather(bf16[96,128]{1,0:T(8,128)(2,1)} %param.89), channel_id=1, replica_groups=mesh['dp'=16,'tensor'=2] {'dp'}, dimensions={0}, use_global_device_ids=true | all-gather | bytes 417792 | tf_op jit(solution)/shard_map/all_gather | solution.py:180
  101.9 41.8 %all_gather.61 = bf16[1536,128]{1,0:T(8,128)(2,1)S(1)} all-gather(bf16[96,128]{1,0:T(8,128)(2,1)} %param.91), channel_id=1, replica_groups=mesh['dp'=16,'tensor'=2] {'dp'}, dimensions={0}, use_global_device_ids=true | all-gather | bytes 417792 | tf_op jit(solution)/shard_map/all_gather | solution.py:182
  176.8 47.8 %all_gather.64 = bf16[6,128]{0,1:T(8,128)(2,1)S(1)} all-gather(bf16[6,8]{0,1:T(8,128)(2,1)S(1)} %copy.632), channel_id=1, replica_groups=mesh['dp'=16,'tensor'=2] {'dp'}, dimensions={1}, use_global_device_ids=true | all-gather | bytes 1632 | tf_op jit(solution)/shard_map/all_gather | solution.py:179
  294.6 36.4 %reduce-scatter.15.cloned.1.call-done = bf16[320,1536]{1,0:T(8,128)(2,1)} async-done(((bf16[640,1536]{1,0:T(8,128)(2,1)}), bf16[320,1536]{1,0:T(8,128)(2,1)}) %reduce-scatter.15.cloned.1.call-update) | async-done | bytes 983056 | tf_op jit(solution)/shard_map/reduce_scatter | solution.py:199
  346.9 167.4 %all-gather.18.cloned.1.call-done = bf16[1536,4480]{1,0:T(8,128)(2,1)} async-done(((bf16[96,4480]{1,0:T(8,128)(2,1)}), bf16[1536,4480]{1,0:T(8,128)(2,1)}) %all-gather.18.cloned.1.call-update) | async-done | bytes 13762576 | tf_op jit(solution)/shard_map/all_gather | solution.py:190
  529.7 149.1 %all-gather.20.cloned.1.call-done = bf16[1536,4480]{1,0:T(8,128)(2,1)} async-done(((bf16[96,4480]{1,0:T(8,128)(2,1)}), bf16[1536,4480]{1,0:T(8,128)(2,1)}) %all-gather.20.cloned.1.call-update) | async-done | bytes 13762576 | tf_op jit(solution)/shard_map/all_gather | solution.py:191
  694.3 162.3 %all-gather.22.cloned.1.call-done = bf16[4480,1536]{0,1:T(8,128)(2,1)} async-done(((bf16[4480,96]{0,1:T(8,128)(2,1)}), bf16[4480,1536]{0,1:T(8,128)(2,1)}) %all-gather.22.cloned.1.call-update) | async-done | bytes 13762576 | tf_op jit(solution)/shard_map/all_gather | solution.py:192
  856.6 22.6 multiply_convert_fusion
  879.2 17.6 fusion.493
  957.1 16.2 conditional.56
  1027.5 43.1 %collective-permute-start.3 = (bf16[2560,256]{0,1:T(8,128)(2,1)}, bf16[2560,256]{0,1:T(8,128)(2,1)}, u32[]{:S(2)}, u32[]{:S(2)}) collective-permute-start(bf16[2560,256]{0,1:T(8,128)(2,1)} %select_convert_fusion), channel_id=1, source_target_pairs={{0,8},{8,0},{2,10},{10,2},{4,12},{12,4},{6,14},{14,6},{16,24},{24,... | collective-permute-start | bytes 3932168 | tf_op jit(solution)/shard_map/ppermute | solution.py:21
  1072.4 27.7 collective-permute-done.3
  1103.0 20.1 collective-permute-start.4
  1188.2 19.2 fusion.497
  1208.9 17.2 fusion.498
  1227.7 17.4 fusion.499
  1248.8 76.3 %all-reduce.13 = (f32[1536]{0:T(1024)S(1)}, f32[6,128]{1,0:T(8,128)S(1)}, f32[1,128]{1,0:T(1,128)S(1)}, f32[1,128]{1,0:T(1,128)S(1)}, f32[1536]{0:T(1024)S(1)}) all-reduce(f32[1536]{0:T(1024)S(1)} %get-tuple-element.1822, f32[6,128]{1,0:T(8,128)S(1)} %get-tuple-element.1837, ...), channel_id=6, replica_groups=mesh['dp'=16,'tensor'=2] {'dp'}, use_global_device_ids=true, to_apply=%region_107.108.clone | all-reduce | flops 4096 | bytes 32768
  1334.7 104.1 %reduce-scatter.27.cloned.1.call-done = f32[96,128]{1,0:T(8,128)} async-done(((f32[1536,128]{1,0:T(8,128)}), f32[96,128]{1,0:T(8,128)}) %reduce-scatter.27.cloned.1.call-update) | async-done | bytes 49168 | tf_op jit(solution)/shard_map/reduce_scatter | solution.py:372
  1438.7 141.6 %reduce-scatter.29.cloned.1.call-done = f32[768,96]{0,1:T(8,128)} async-done(((f32[768,1536]{0,1:T(8,128)}), f32[768,96]{0,1:T(8,128)}) %reduce-scatter.29.cloned.1.call-update) | async-done | bytes 294928 | tf_op jit(solution)/shard_map/reduce_scatter | solution.py:374
  1580.3 142.5 %reduce-scatter.23.cloned.1.call-done = f32[96,768]{1,0:T(8,128)} async-done(((f32[1536,768]{1,0:T(8,128)}), f32[96,768]{1,0:T(8,128)}) %reduce-scatter.23.cloned.1.call-update) | async-done | bytes 294928 | tf_op jit(solution)/shard_map/reduce_scatter | solution.py:368
  1722.9 395.0 %reduce-scatter.31.cloned.1.call-done = f32[96,4480]{1,0:T(8,128)} async-done(((f32[1536,4480]{1,0:T(8,128)}), f32[96,4480]{1,0:T(8,128)}) %reduce-scatter.31.cloned.1.call-update) | async-done | bytes 1720336 | tf_op jit(solution)/shard_map/reduce_scatter | solution.py:306
  2117.9 396.1 %reduce-scatter.33.cloned.1.call-done = f32[96,4480]{1,0:T(8,128)} async-done(((f32[1536,4480]{1,0:T(8,128)}), f32[96,4480]{1,0:T(8,128)}) %reduce-scatter.33.cloned.1.call-update) | async-done | bytes 1720336 | tf_op jit(solution)/shard_map/reduce_scatter | solution.py:307
  2514.1 394.9 %reduce-scatter.35.cloned.1.call-done = f32[4480,96]{0,1:T(8,128)} async-done(((f32[4480,1536]{0,1:T(8,128)}), f32[4480,96]{0,1:T(8,128)}) %reduce-scatter.35.cloned.1.call-update) | async-done | bytes 1720336 | tf_op jit(solution)/shard_map/reduce_scatter | solution.py:308
  (405 shorter events, 379.4 us)
Async XLA Ops:
  7.2 136.5 %all-gather.10.cloned.1.call-start = ((), (), s32[]{:S(2)}) async-start(), calls=%async_computation.11 | async-start | bytes 2949120 | tf_op jit(solution)/shard_map/all_gather | solution.py:196
  61.8 174.6 %all-gather.12.cloned.1.call-start = ((), (), s32[]{:S(2)}) async-start(), calls=%async_computation.12 | async-start | bytes 2506752 | tf_op jit(solution)/shard_map/all_gather | solution.py:178
  62.5 226.9 %all-gather.14.cloned.1.call-start = ((), (), s32[]{:S(2)}) async-start(), calls=%async_computation.13 | async-start | bytes 2506752 | tf_op jit(solution)/shard_map/all_gather | solution.py:184
  149.3 181.7 %reduce-scatter.15.cloned.1.call-start = ((), (), s32[]{:S(2)}) async-start(), calls=%async_computation.14 | async-start | bytes 2949120 | tf_op jit(solution)/shard_map/reduce_scatter | solution.py:199
  168.6 64.3 %collective-permute-start.2 = (bf16[2560,256]{0,1:T(8,128)(2,1)}, bf16[2560,256]{0,1:T(8,128)(2,1)}, u32[]{:S(2)}, u32[]{:S(2)}) collective-permute-start(bf16[2560,256]{0,1:T(8,128)(2,1)} %pad_maximum_fusion.8), channel_id=1, source_target_pairs={{0,8},{8,0},{2,10},{10,2},{4,12},{12,4},{6,14},{14,6},{16,24},{24,... | collective-permute-start | bytes 3932168 | tf_op jit(solution)/shard_map/ppermute | solution.py:21
  294.5 52.4 %all-gather.16.cloned.1.call-start = ((), (), s32[]{:S(2)}) async-start(), calls=%async_computation.15 | async-start | bytes 2949120 | tf_op jit(solution)/shard_map/all_gather | solution.py:196
  335.2 179.1 %all-gather.18.cloned.1.call-start = ((), (), s32[]{:S(2)}) async-start(), calls=%async_computation.16 | async-start | bytes 14622720 | tf_op jit(solution)/shard_map/all_gather | solution.py:190
  335.7 343.1 %all-gather.20.cloned.1.call-start = ((), (), s32[]{:S(2)}) async-start(), calls=%async_computation.17 | async-start | bytes 14622720 | tf_op jit(solution)/shard_map/all_gather | solution.py:191
  336.5 357.8 %all-gather.24.cloned.1.call-start = ((), (), s32[]{:S(2)}) async-start(), calls=%async_computation.20 | async-start | bytes 2949120 | tf_op jit(solution)/shard_map/all_gather | solution.py:196
  337.2 519.4 %all-gather.22.cloned.1.call-start = ((), (), s32[]{:S(2)}) async-start(), calls=%async_computation.18 | async-start | bytes 14622720 | tf_op jit(solution)/shard_map/all_gather | solution.py:192
  338.0 580.8 %reduce-scatter.19.cloned.1.call-start = ((), (), s32[]{:S(2)}) async-start(), calls=%async_computation.21 | async-start | bytes 2949120 | tf_op jit(solution)/shard_map/reduce_scatter | solution.py:199
  911.0 25.9 all-gather.26.cloned.1.call-start
  925.2 321.6 %reduce-scatter.21.cloned.1.call-start = ((), (), s32[]{:S(2)}) async-start(), calls=%async_computation.23 | async-start | bytes 2949120 | tf_op jit(solution)/shard_map/reduce_scatter | solution.py:199
  1027.5 72.6 %collective-permute-start.3 = (bf16[2560,256]{0,1:T(8,128)(2,1)}, bf16[2560,256]{0,1:T(8,128)(2,1)}, u32[]{:S(2)}, u32[]{:S(2)}) collective-permute-start(bf16[2560,256]{0,1:T(8,128)(2,1)} %select_convert_fusion), channel_id=1, source_target_pairs={{0,8},{8,0},{2,10},{10,2},{4,12},{12,4},{6,14},{14,6},{16,24},{24,... | collective-permute-start | bytes 3932168 | tf_op jit(solution)/shard_map/ppermute | solution.py:21
  1103.0 34.8 %collective-permute-start.4 = (bf16[1280,256]{0,1:T(8,128)(2,1)S(1)}, bf16[1280,256]{0,1:T(8,128)(2,1)S(1)}, u32[]{:S(2)}, u32[]{:S(2)}) collective-permute-start(bf16[1280,256]{0,1:T(8,128)(2,1)S(1)} %select_convert_fusion.1), channel_id=1, source_target_pairs={{0,4},{4,0},{2,6},{6,2},{8,12},{12,8},{10,14},{14,10},{16,20},{20,... | collective-permute-start | bytes 1966088 | tf_op jit(solution)/shard_map/ppermute | solution.py:21
  1138.0 16.8 collective-permute-start.5
  1158.6 171.5 %reduce-scatter.17.cloned.1.call-start = ((), (), s32[]{:S(2)}) async-start(), calls=%async_computation.19 | async-start | bytes 2949120 | tf_op jit(solution)/shard_map/reduce_scatter | solution.py:199
  1173.9 160.7 %reduce-scatter.25.cloned.1.call-start = ((), (), s32[]{:S(2)}) async-start(), calls=%async_computation.25 | async-start | bytes 835584 | tf_op jit(solution)/shard_map/reduce_scatter | solution.py:370
  1175.7 263.1 %reduce-scatter.27.cloned.1.call-start = ((), (), s32[]{:S(2)}) async-start(), calls=%async_computation.26 | async-start | bytes 835584 | tf_op jit(solution)/shard_map/reduce_scatter | solution.py:372
  1177.4 403.0 %reduce-scatter.29.cloned.1.call-start = ((), (), s32[]{:S(2)}) async-start(), calls=%async_computation.27 | async-start | bytes 5013504 | tf_op jit(solution)/shard_map/reduce_scatter | solution.py:374
  1183.7 539.2 %reduce-scatter.23.cloned.1.call-start = ((), (), s32[]{:S(2)}) async-start(), calls=%async_computation.24 | async-start | bytes 5013504 | tf_op jit(solution)/shard_map/reduce_scatter | solution.py:368
  1188.1 929.8 %reduce-scatter.31.cloned.1.call-start = ((), (), s32[]{:S(2)}) async-start(), calls=%async_computation.28 | async-start | bytes 29245440 | tf_op jit(solution)/shard_map/reduce_scatter | solution.py:306
  1207.4 1306.6 %reduce-scatter.33.cloned.1.call-start = ((), (), s32[]{:S(2)}) async-start(), calls=%async_computation.29 | async-start | bytes 29245440 | tf_op jit(solution)/shard_map/reduce_scatter | solution.py:307
  1226.2 1682.8 %reduce-scatter.35.cloned.1.call-start = ((), (), s32[]{:S(2)}) async-start(), calls=%async_computation.30 | async-start | bytes 29245440 | tf_op jit(solution)/shard_map/reduce_scatter | solution.py:308
  (101 other events, 3174.8 us)
Sparse Core Ops, SparseCore 0:
  61.9 6.2 all-gather.9
  71.0 69.0 all-gather.11
  149.5 60.1 all-gather.13
  294.6 36.3 reduce-scatter.14
  335.3 11.5 all-gather.15
  349.9 164.3 all-gather.17
  517.5 161.3 all-gather.19
  680.5 8.5 all-gather.23
  692.3 164.3 all-gather.21
  911.1 7.6 reduce-scatter.18
  925.4 11.5 all-gather.25
  1158.7 9.7 reduce-scatter.20
  1174.1 9.7 reduce-scatter.16
  1188.9 123.3 reduce-scatter.24
  1317.4 121.2 reduce-scatter.26
  1444.3 135.9 reduce-scatter.28
  1586.8 136.0 reduce-scatter.22
  1729.3 388.5 reduce-scatter.30
  2125.5 388.4 reduce-scatter.32
  2520.5 388.4 reduce-scatter.34
where the time goes:
time: 2920 us
  waiting for transfers between devices  2180 us (75%)
  blocking collectives  252 us (9%)
  matrix products  216 us (7%)
  starting transfers between devices  75.1 us (3%)
  loops' own time  74.5 us (3%)
  other arithmetic  45.8 us (2%)
  local copies, waits for them, and re-layouts  43.6 us (1%)
    reduce_scatter x1, waiting for transfers between devices, on_device(): lax.psum_scatter(up_mat_grad, 'dp', scatter_dimension=0, tiled=True)  396 us
    reduce_scatter x1, waiting for transfers between devices, on_device(): lax.psum_scatter(gate_mat_grad, 'dp', scatter_dimension=0, tiled=True)  395 us
    reduce_scatter x1, waiting for transfers between devices, on_device(): lax.psum_scatter(down_mat_grad, 'dp', scatter_dimension=1, tiled=True)  395 us
    all_gather x1, waiting for transfers between devices, fetch_feedforward(): lax.all_gather(gate_weight, 'dp', axis=0, tiled=True)  167 us
    all_gather x1, waiting for transfers between devices, fetch_feedforward(): lax.all_gather(down_weight, 'dp', axis=1, tiled=True)  162 us
    all_gather x1, waiting for transfers between devices, fetch_feedforward(): lax.all_gather(up_weight, 'dp', axis=0, tiled=True)  149 us
    reduce_scatter x1, waiting for transfers between devices, on_device(): lax.psum_scatter(query_mat_grad, 'dp', scatter_dimension=0, tiled=True)  143 us
    reduce_scatter x1, waiting for transfers between devices, on_device(): lax.psum_scatter(out_mat_grad, 'dp', scatter_dimension=1, tiled=True)  142 us
  transfers between devices with their start and end apart: 26, of which 18 were waited for; matrix products, arithmetic and copies ran while one was open for 6% of the time, Pallas kernels for 0%

commit v1 on v0

v1 whole, which is shorter than its diff:
```python
import jax, functools
import jax.numpy as jnp
from jax import lax
from jax.experimental import pallas as pl
from jax.experimental.pallas import tpu as pltpu
from jax.sharding import PartitionSpec as P
NEG=-1e30
QB=128; KC=512; KB=256
LOG2E=1.4426950408889634

def dot_nt(a,b): return lax.dot_general(a,b,(((1,),(1,)),((),())),preferred_element_type=jnp.float32)
def dot_nn(a,b): return lax.dot_general(a,b,(((1,),(0,)),((),())),preferred_element_type=jnp.float32)

def fwd_kernel(info, q_ref, k_ref, v_ref, o_ref, l_ref, *, heads, scale):
    blk = pl.program_id(0)
    nfull = info[blk*8]
    rows = heads*QB
    q = jnp.concatenate([q_ref[:, h*128:(h+1)*128] for h in range(heads)], axis=0)
    c2 = scale*LOG2E
    def step(carry, s, v):
        m,l,acc = carry
        mt = s[:, :128]
        for j in range(1, KC//128): mt = jnp.maximum(mt, s[:, j*128:(j+1)*128])
        mn = jnp.maximum(m, jnp.max(mt, axis=1, keepdims=True))
        p = jnp.exp2((s-mn)*c2)
        ps = p[:, :128]
        for j in range(1, KC//128): ps = ps + p[:, j*128:(j+1)*128]
        a = jnp.exp2((m-mn)*c2)
        l = l*a + ps
        acc = acc*a + dot_nn(p.astype(jnp.bfloat16), v)
        return mn,l,acc
    def body(c, carry):
        k = k_ref[pl.ds(pl.multiple_of(c*KC,KC),KC),:]
        v = v_ref[pl.ds(pl.multiple_of(c*KC,KC),KC),:]
        return step(carry, dot_nt(q,k), v)
    init = (jnp.full((rows,1),NEG,jnp.float32), jnp.zeros((rows,128),jnp.float32), jnp.zeros((rows,128),jnp.float32))
    b0 = pl.multiple_of(info[blk*8+1]*KB,KB); b1 = pl.multiple_of(info[blk*8+2]*KB,KB)
    k = jnp.concatenate([k_ref[pl.ds(b0,KB),:], k_ref[pl.ds(b1,KB),:]],axis=0)
    v = jnp.concatenate([v_ref[pl.ds(b0,KB),:], v_ref[pl.ds(b1,KB),:]],axis=0)
    s = dot_nt(q,k)
    col = lax.broadcasted_iota(jnp.int32,(QB,KC),1)
    row = lax.broadcasted_iota(jnp.int32,(QB,KC),0)
    base = jnp.where(col<KB, info[blk*8+3], info[blk*8+4]-KB)
    ok = col+base <= row
    s = jnp.concatenate([jnp.where(ok, s[h*QB:(h+1)*QB], NEG) for h in range(heads)],axis=0)
    carry = step(init, s, v)
    m,l,acc = lax.fori_loop(0,nfull,body,carry)
    lsum = jnp.sum(l,axis=1,keepdims=True)
    out = (acc/lsum).astype(jnp.bfloat16)
    o_ref[...] = jnp.concatenate([out[h*QB:(h+1)*QB] for h in range(heads)],axis=1)
    lse2 = m*c2+jnp.log2(lsum)
    t = jnp.broadcast_to(lse2,(rows,128)).T
    l_ref[...] = t[:8,:].reshape(1,8,rows)

def attn_fwd(info, q, k, v, scale):
    T=q.shape[0]; heads=q.shape[1]//128; nb=T//QB; rows=heads*QB
    return pl.pallas_call(functools.partial(fwd_kernel,heads=heads,scale=scale),
        grid_spec=pltpu.PrefetchScalarGridSpec(num_scalar_prefetch=1,grid=(nb,),
            in_specs=[pl.BlockSpec((QB,heads*128),lambda i,s:(i,0)),
                      pl.BlockSpec(k.shape,lambda i,s:(0,0)),pl.BlockSpec(v.shape,lambda i,s:(0,0))],
            out_specs=[pl.BlockSpec((QB,heads*128),lambda i,s:(i,0)),pl.BlockSpec((1,8,rows),lambda i,s:(i,0,0))]),
        out_shape=[jax.ShapeDtypeStruct((T,heads*128),jnp.bfloat16),jax.ShapeDtypeStruct((nb,8,rows),jnp.float32)],
        compiler_params=pltpu.CompilerParams(vmem_limit_bytes=56<<20),
        name="attention_forward",
        cost_estimate=pl.CostEstimate(flops=4*T*heads*128*2304,bytes_accessed=6<<20,transcendentals=T*heads*2304),
    )(info,q,k,v)

def bwd_kernel(info, q_ref, do_ref, o_ref, l_ref, k_ref, v_ref, dq_ref, dk_ref, dv_ref, *, heads, scale):
    blk = pl.program_id(0)
    @pl.when(blk==0)
    def _():
        dk_ref[...] = jnp.zeros_like(dk_ref)
        dv_ref[...] = jnp.zeros_like(dv_ref)
    nfull = info[blk*8]
    rows = heads*QB
    cat = lambda ref: jnp.concatenate([ref[:, h*128:(h+1)*128] for h in range(heads)], axis=0)
    q = cat(q_ref); do = cat(do_ref); o = cat(o_ref)
    c2 = scale*LOG2E
    delta = jnp.sum((do.astype(jnp.float32)*o.astype(jnp.float32)).T, axis=0, keepdims=True)
    lse2 = l_ref[0,0:1,:]
    def tile(k, v, ok):
        s = dot_nt(k,q)
        p = jnp.exp2(s*c2-lse2)
        if ok is not None:
            p = jnp.concatenate([jnp.where(ok, p[:, h*QB:(h+1)*QB], 0.0) for h in range(heads)],axis=1)
        dp = dot_nt(v,do)
        ds = (p*(dp-delta)).astype(jnp.bfloat16)
        dv = dot_nn(p.astype(jnp.bfloat16), do)
        dk = dot_nn(ds, q)
        dq = lax.dot_general(ds,k,(((0,),(0,)),((),())),preferred_element_type=jnp.float32)
        return dq,dk,dv
    def body(c, acc):
        at = pl.ds(pl.multiple_of(c*KC,KC),KC)
        dq,dk,dv = tile(k_ref[at,:], v_ref[at,:], None)
        dk_ref[at,:] += dk
        dv_ref[at,:] += dv
        return acc+dq
    b0 = pl.multiple_of(info[blk*8+1]*KB,KB); b1 = pl.multiple_of(info[blk*8+2]*KB,KB)
    k = jnp.concatenate([k_ref[pl.ds(b0,KB),:], k_ref[pl.ds(b1,KB),:]],axis=0)
    v = jnp.concatenate([v_ref[pl.ds(b0,KB),:], v_ref[pl.ds(b1,KB),:]],axis=0)
    col = lax.broadcasted_iota(jnp.int32,(KC,QB),0)
    row = lax.broadcasted_iota(jnp.int32,(KC,QB),1)
    base = jnp.where(col<KB, info[blk*8+3], info[blk*8+4]-KB)
    dq,dk,dv = tile(k,v,col+base<=row)
    dk_ref[pl.ds(b0,KB),:] += dk[:KB]
    dv_ref[pl.ds(b0,KB),:] += dv[:KB]
    dk_ref[pl.ds(b1,KB),:] += dk[KB:]
    dv_ref[pl.ds(b1,KB),:] += dv[KB:]
    dq = lax.fori_loop(0,nfull,body,dq)
    dq = dq*scale
    dq_ref[...] = jnp.concatenate([dq[h*QB:(h+1)*QB] for h in range(heads)],axis=1)

def attn_bwd(info,q,do,o,lse,k,v,scale):
    T=q.shape[0]; heads=q.shape[1]//128; nb=T//QB; rows=heads*QB
    qspec=pl.BlockSpec((QB,heads*128),lambda i,s:(i,0))
    full=pl.BlockSpec(k.shape,lambda i,s:(0,0))
    return pl.pallas_call(functools.partial(bwd_kernel,heads=heads,scale=scale),
        grid_spec=pltpu.PrefetchScalarGridSpec(num_scalar_prefetch=1,grid=(nb,),
            in_specs=[qspec,qspec,qspec,pl.BlockSpec((1,8,rows),lambda i,s:(i,0,0)),full,full],
            out_specs=[qspec,full,full]),
        out_shape=[jax.ShapeDtypeStruct((T,heads*128),jnp.float32),jax.ShapeDtypeStruct(k.shape,jnp.float32),jax.ShapeDtypeStruct(v.shape,jnp.float32)],
        compiler_params=pltpu.CompilerParams(vmem_limit_bytes=56<<20),
        name="attention_backward",
        cost_estimate=pl.CostEstimate(flops=10*T*heads*128*2304,bytes_accessed=12<<20,transcendentals=T*heads*2304),
    )(info,q,do,o,lse,k,v)
EPS = 1e-06
THETA = 10000.0
TREE_TOK = 5120
TRUNK = 2048
PLANE = 4


def swap(block, axis, count, bits):
    return lax.ppermute(block, axis, [(i, i ^ bits) for i in range(count)])


def rms_scale(values):
    return lax.rsqrt(jnp.mean(values * values, axis=1, keepdims=True) + EPS)


def norm_back(grad, values, gain):
    scale = rms_scale(values)
    z = values * scale
    w = grad * gain
    gain_grad = jnp.sum(grad * z, axis=0)
    return scale * (w - z * jnp.mean(w * z, axis=1, keepdims=True)), gain_grad


def turn(values, cosines, sines):
    swapped = jnp.concatenate([values[..., 64:], values[..., :64]], axis=-1)
    return values * cosines + swapped * sines


def rope_tables(positions):
    exponents = jnp.arange(64, dtype=jnp.float32) * (2.0 / 128)
    frequency = jnp.power(THETA, -exponents)
    angles = positions.astype(jnp.float32)[:, None] * frequency[None, :]
    cosines, sines = jnp.cos(angles), jnp.sin(angles)
    return (
        jnp.concatenate([cosines, cosines], axis=1)[:, None, :],
        jnp.concatenate([-sines, sines], axis=1)[:, None, :],
    )


def contract_rows(left, right):
    return lax.dot_general(
        left, right, (((0,), (0,)), ((), ())), preferred_element_type=jnp.float32
    )


def contract_cols(left, right):
    return lax.dot_general(
        left, right, (((1,), (1,)), ((), ())), preferred_element_type=jnp.float32
    )


def matmul(left, right):
    return jnp.dot(left, right, preferred_element_type=jnp.float32)


def attention_plan(segment_ids, parent_ids, dp_index, local_tok):
    members = TREE_TOK // local_tok
    first = dp_index // members * TREE_TOK
    slots = lax.dynamic_slice_in_dim(segment_ids, first, TREE_TOK)[::KB]
    numbers = jnp.arange(parent_ids.shape[0], dtype=jnp.int32)
    parents = jnp.sum(jnp.where(slots[:, None] == numbers[None, :], parent_ids[None, :], 0), axis=1)
    places = jnp.arange(slots.shape[0], dtype=jnp.int32)
    holder = jnp.sum(jnp.where(parents[:, None] == slots[None, :], places[None, :], 0), axis=1)
    starts = dp_index % members * local_tok + QB * jnp.arange(local_tok // QB, dtype=jnp.int32)
    slot = starts // KB
    chosen = slot[:, None] == places[None, :]
    pick = lambda table: jnp.sum(jnp.where(chosen, table[None, :], 0), axis=1)
    in_trunk = starts < TRUNK
    is_leaf = pick(parents) != slots[0]
    chunk = jnp.minimum(starts, TRUNK) // KC
    far = jnp.int32(1 << 20)
    block0 = jnp.where(in_trunk, 2 * chunk, jnp.where(is_leaf, pick(holder), TRUNK // KB))
    block1 = jnp.where(in_trunk, 2 * chunk + 1, slot)
    shift0 = jnp.where(in_trunk, block0 * KB - starts, jnp.where(is_leaf, -far, far))
    shift1 = block1 * KB - starts
    zero = jnp.zeros_like(chunk)
    return jnp.stack([chunk, block0, block1, shift0, shift1, zero, zero, zero], axis=1).reshape(-1)


def on_device(
    dp_size,
    layer_input,
    out_cotangent,
    positions,
    segment_ids,
    parent_ids,
    attention_gain,
    query_weight,
    query_bias,
    key_weight,
    key_bias,
    value_weight,
    value_bias,
    output_weight,
    feedforward_gain,
    gate_weight,
    up_weight,
    down_weight,
):
    bf16, f32 = jnp.bfloat16, jnp.float32
    local_tok = positions.shape[0]
    half_tok = layer_input.shape[0]
    width = layer_input.shape[1]
    shard = attention_gain.shape[0]
    heads, head_dim = query_bias.shape[0], 128
    q_width = heads * head_dim
    hidden = gate_weight.shape[1]
    block = -(-hidden // (PLANE * 128)) * 128
    lines = dp_size // PLANE
    members = TREE_TOK // local_tok
    dp_index = lax.axis_index("dp")
    core = lax.axis_index("tensor")
    plane_at = dp_index % PLANE
    member = dp_index % members
    z_at = dp_index // PLANE
    scale = head_dim ** (-0.5)
    line_groups = [[j + PLANE * z for z in range(lines)] for j in range(PLANE)]

    def by_core(mine):
        other = swap(mine, "tensor", 2, 1)
        first = jnp.where(core == 0, mine, other)
        second = jnp.where(core == 0, other, mine)
        return jnp.concatenate([first, second], axis=0)

    def to_tokens(values):
        halves = values.reshape(2, half_tok, width)
        mine = lax.dynamic_index_in_dim(halves, core, 0, keepdims=False)
        theirs = lax.dynamic_index_in_dim(halves, 1 - core, 0, keepdims=False)
        return mine + swap(theirs.astype(bf16), "tensor", 2, 1).astype(f32)

    extra = jnp.zeros((shard, 128), bf16)
    extra = extra.at[:, 0].set(attention_gain).at[:, 1].set(feedforward_gain)
    biases = jnp.concatenate([query_bias.reshape(-1), key_bias.reshape(-1), value_bias.reshape(-1)])
    per = biases.shape[0]
    pad_to = -(-per // shard)
    biases = jnp.pad(biases, (0, pad_to * shard - per)).reshape(pad_to, shard)
    extra = extra.at[:, 2 : 2 + pad_to].set(biases.T)
    first_stack = jnp.concatenate([query_weight, key_weight, value_weight, extra], axis=1)
    first_all = lax.all_gather(first_stack, "dp", axis=0, tiled=True)
    out_t = lax.all_gather(output_weight.T, "dp", axis=0, tiled=True)

    def spread(weight):
        padded = jnp.pad(weight, ((0, 0), (0, PLANE * block - hidden)))
        result = jnp.zeros((PLANE * shard, block), bf16)
        for bits in range(PLANE):
            there = plane_at ^ bits
            piece = lax.dynamic_slice_in_dim(padded, there * block, block, axis=1)
            if bits:
                piece = swap(piece, "dp", dp_size, bits)
            result = lax.dynamic_update_slice_in_dim(result, piece, there * shard, axis=0)
        return lax.all_gather(result, "dp", axis=0, tiled=True, axis_index_groups=line_groups)

    gate_mat = spread(gate_weight)
    up_mat = spread(up_weight)
    down_t = spread(down_weight.T)

    input_wide = layer_input.astype(f32)
    input_all = by_core(layer_input).astype(f32)
    z_all = input_all * rms_scale(input_all)
    gain_one = first_all[:, q_width + 256].astype(f32)
    gain_two = first_all[:, q_width + 257].astype(f32)
    bias_all = first_all[:, q_width + 258 : q_width + 258 + pad_to].astype(f32)
    bias_all = bias_all.reshape(dp_size, shard, pad_to).transpose(0, 2, 1).reshape(dp_size, -1)
    per_head = query_bias.shape[1]
    bias_all = bias_all[:, :per].reshape(dp_size, heads + 2, per_head)
    bias_all = bias_all.transpose(1, 0, 2).reshape((heads + 2) * head_dim)
    normed = (z_all * gain_one).astype(bf16)
    qkv = matmul(normed, first_all[:, : q_width + 256]) + bias_all
    cosines, sines = rope_tables(positions)
    q_rot = turn(qkv[:, :q_width].reshape(local_tok, heads, head_dim), cosines, sines)
    q_rot = q_rot.astype(bf16).reshape(local_tok, q_width)
    k_rot = turn(qkv[:, None, q_width : q_width + 128], cosines, sines).astype(bf16)[:, 0]
    pair = jnp.concatenate([k_rot, qkv[:, q_width + 128 :].astype(bf16)], axis=1)
    tree = jnp.zeros((TREE_TOK, 256), bf16)
    for bits in range(members):
        piece = swap(pair, "dp", dp_size, bits) if bits else pair
        tree = lax.dynamic_update_slice_in_dim(tree, piece, (member ^ bits) * local_tok, axis=0)
    k_tree, v_tree = tree[:, :128], tree[:, 128:]
    plan = attention_plan(segment_ids, parent_ids, dp_index, local_tok)
    attended, lse = attn_fwd(plan, q_rot, k_tree, v_tree, scale)
    middle = input_wide + to_tokens(contract_cols(attended, out_t))
    normed_two = (middle * rms_scale(middle) * gain_two).astype(bf16)

    def to_plane(mine):
        parts = [mine] + [swap(mine, "dp", dp_size, bits) for bits in range(1, PLANE)]
        parts = jnp.concatenate(parts, axis=0)
        return jnp.concatenate([parts, swap(parts, "tensor", 2, 1)], axis=0)

    def from_plane(partial):
        both = partial.astype(bf16).reshape(2, PLANE * half_tok, width)
        sums = both[0].astype(f32) + swap(both[1], "tensor", 2, 1).astype(f32)
        sums = sums.reshape(PLANE, half_tok, width)
        total = sums[0]
        for bits in range(1, PLANE):
            total = total + swap(sums[bits].astype(bf16), "dp", dp_size, bits).astype(f32)
        return total

    cot = to_plane(out_cotangent)
    x = to_plane(normed_two)
    gate = matmul(x, gate_mat)
    up = matmul(x, up_mat)
    product_grad = matmul(cot, down_t)
    sig = jax.nn.sigmoid(gate)
    silu = gate * sig
    product = (silu * up).astype(bf16)
    gate_grad = (product_grad * up * sig * (1 + gate * (1 - sig))).astype(bf16)
    up_grad = (product_grad * silu).astype(bf16)
    normed_two_grad = from_plane(contract_cols(gate_grad, gate_mat) + contract_cols(up_grad, up_mat))

    def collect(grad):
        rows = PLANE * shard
        if lines == 4:
            chunks = grad.astype(bf16)
            take = lambda d: lax.dynamic_slice_in_dim(chunks, jnp.clip(d, 0, lines - 1) * rows, rows)
            total = take(z_at).astype(f32)
            for sign in (1, -1):
                carried = None
                for step in range(lines - 1):
                    place = z_at if sign == 1 else lines - 1 - z_at
                    target = lines - 1 - step + place
                    send = take(target if sign == 1 else lines - 1 - target).astype(f32)
                    if carried is not None:
                        send = send + jnp.where(place > 0, carried.astype(f32), 0)
                    route = []
                    for z in range(step + 1):
                        for j in range(PLANE):
                            a = z if sign == 1 else lines - 1 - z
                            route.append((a * PLANE + j, (a + sign) * PLANE + j))
                    carried = lax.ppermute(send.astype(bf16), "dp", route)
                total = total + jnp.where(place > 0, carried.astype(f32), 0)
        else:
            total = lax.psum_scatter(
                grad.astype(bf16), "dp", scatter_dimension=0, tiled=True, axis_index_groups=line_groups
            )
        total = total.astype(bf16)
        result = jnp.zeros((shard, PLANE * block), bf16)
        for bits in range(PLANE):
            there = plane_at ^ bits
            piece = lax.dynamic_slice_in_dim(total, there * shard, shard, axis=0)
            if bits:
                piece = swap(piece, "dp", dp_size, bits)
            result = lax.dynamic_update_slice_in_dim(result, piece, there * block, axis=1)
        return result[:, :hidden].astype(f32)

    gate_out = collect(contract_rows(x, gate_grad))
    up_out = collect(contract_rows(x, up_grad))
    down_out = collect(contract_rows(cot, product)).T
    layer_output = (middle + from_plane(contract_cols(product, down_t))).astype(bf16)

    norm_grad, gain_two_grad = norm_back(normed_two_grad, middle, gain_two)
    middle_grad = out_cotangent.astype(f32) + norm_grad

    branch_grad = by_core(middle_grad.astype(bf16))
    out_grad = contract_rows(branch_grad, attended)
    gain_column = jnp.pad(gain_two_grad[:, None], ((0, 0), (0, 127)))
    out_sum = lax.psum_scatter(
        jnp.concatenate([out_grad, gain_column], axis=1).astype(bf16), "dp", scatter_dimension=0, tiled=True
    )
    attended_grad = matmul(branch_grad, out_t).astype(bf16)
    dq, dk, dv = attn_bwd(plan, q_rot, attended_grad, attended, lse, k_tree, v_tree, scale)
    pair_grads = jnp.concatenate([dk, dv], axis=1)
    total = lax.dynamic_slice_in_dim(pair_grads, member * local_tok, local_tok)
    for bits in range(1, members):
        piece = lax.dynamic_slice_in_dim(pair_grads, (member ^ bits) * local_tok, local_tok)
        total = total + swap(piece.astype(bf16), "dp", dp_size, bits).astype(f32)
    q_grad = turn(dq.reshape(local_tok, heads, head_dim), cosines, -sines).astype(bf16)
    q_grad = q_grad.reshape(local_tok, q_width)
    k_grad = turn((total[:, :128] * scale)[:, None], cosines, -sines).astype(bf16)[:, 0]
    grads = jnp.concatenate([q_grad, k_grad, total[:, 128:].astype(bf16)], axis=1)
    first_grad = contract_rows(normed, grads)
    bias_grad = jnp.sum(grads.astype(f32), axis=0)
    normed_grad = to_tokens(contract_cols(grads, first_all[:, : q_width + 256]))
    input_norm_grad, gain_one_grad = norm_back(normed_grad, input_wide, gain_one)
    input_grad = (middle_grad + input_norm_grad).astype(bf16)
    bias_grad = bias_grad.reshape(heads + 2, dp_size, per_head).transpose(1, 0, 2).reshape(dp_size, per)
    bias_grad = jnp.pad(bias_grad, ((0, 0), (0, pad_to * shard - per)))
    bias_grad = bias_grad.reshape(dp_size, pad_to, shard).transpose(0, 2, 1).reshape(width, pad_to)
    tail = jnp.concatenate([gain_one_grad[:, None], bias_grad], axis=1)
    tail = jnp.pad(tail, ((0, 0), (0, 127 - pad_to)))
    first_sum = lax.psum_scatter(
        jnp.concatenate([first_grad, tail], axis=1).astype(bf16), "dp", scatter_dimension=0, tiled=True
    ).astype(f32)
    out_sum = out_sum.astype(f32)
    gains = jnp.stack([first_sum[:, q_width + 256], out_sum[:, q_width]])
    gains = gains + swap(gains, "tensor", 2, 1)
    bias_sum = first_sum[:, q_width + 257 : q_width + 257 + pad_to].T.reshape(-1)[:per]
    return (
        layer_output,
        input_grad,
        gains[0],
        first_sum[:, :q_width],
        bias_sum[: heads * per_head].reshape(heads, per_head),
        first_sum[:, q_width : q_width + 128],
        bias_sum[heads * per_head : (heads + 1) * per_head].reshape(1, per_head),
        first_sum[:, q_width + 128 : q_width + 256],
        bias_sum[(heads + 1) * per_head :].reshape(1, per_head),
        out_sum[:, :q_width].T,
        gains[1],
        gate_out,
        up_out,
        down_out,
    )


def solution(mesh):
    placed = (
        P(("dp", "tensor"), None),
        P(("dp", "tensor"), None),
        P("dp"),
        P(),
        P(),
        P("dp"),
        P("dp", "tensor"),
        P("tensor", "dp"),
        P("dp", "tensor"),
        P("tensor", "dp"),
        P("dp", "tensor"),
        P("tensor", "dp"),
        P("tensor", "dp"),
        P("dp"),
        P("dp", "tensor"),
        P("dp", "tensor"),
        P("tensor", "dp"),
    )
    return jax.shard_map(
        functools.partial(on_device, mesh.shape["dp"]),
        mesh=mesh,
        in_specs=placed,
        out_specs=(
            P(("dp", "tensor"), None),
            P(("dp", "tensor"), None),
            P("dp"),
            P("dp", "tensor"),
            P("tensor", "dp"),
            P("dp", "tensor"),
            P("tensor", "dp"),
            P("dp", "tensor"),
            P("tensor", "dp"),
            P("tensor", "dp"),
            P("dp"),
            P("dp", "tensor"),
            P("dp", "tensor"),
            P("tensor", "dp"),
        ),
        check_vma=False,
    )
```

time: 2920 us -> 1150 us (0.39)
  waiting for transfers between devices: 2180 us -> 562 us
  blocking collectives: 252 us -> 0 us
  local copies, waits for them, and re-layouts: 43.6 us -> 137 us
  starting transfers between devices: 75.1 us -> 164 us
  loops' own time: 74.5 us -> 0 us
  matrix products: 216 us -> 164 us
    reduce_scatter x11 -> x0, waiting for transfers between devices: 1620 us -> none  [the longest x1 396 us: on_device(): lax.psum_scatter(up_mat_grad, 'dp', scatter_dimension=0, tiled=True)]
    all_gather x9 -> x5, waiting for transfers between devices: 499 us -> 52.8 us  [the longest x3 52.8 us: spread(): lax.all_gather(result, 'dp', axis=0, tiled=True, axis_index_groups=line_g...]
    ppermute x6 -> x71, waiting for transfers between devices: 63.7 us -> 334 us  [the longest x53 244 us: swap(): return lax.ppermute(block, axis, [(i, i ^ bits) for i in range(count)])]
    unnamed x20 -> x9, waiting for transfers between devices: 3.54 us -> 175 us
    all_gather x3 -> x0, blocking collectives: 128 us -> none  [the longest x1 47.8 us: fetch_attention(): lax.all_gather(query_bias, 'dp', axis=1, tiled=True)]
    unnamed x2 -> x0, blocking collectives: 121 us -> none
    ppermute x6 -> x71, starting transfers between devices: 73.5 us -> 164 us  [the longest x53 114 us: swap(): return lax.ppermute(block, axis, [(i, i ^ bits) for i in range(count)])]
    another operation x32 -> x0, loops' own time: 74.5 us -> none  [the longest x8 40.9 us: grad_step(): return lax.cond(active, grad_compute, skipped, carry)]
  transfers between devices with their start and end apart: 26 -> 78, of which waited for: 18 -> 33; matrix products, arithmetic and copies ran while one was open for 6% -> 22% of each run, Pallas kernels for 0% -> 1%
where the time goes in v1:
time: 1150 us; the launch traced here: 1140 us
  waiting for transfers between devices  562 us (49%)
  starting transfers between devices  164 us (14%)
  matrix products  164 us (14%)
  local copies, waits for them, and re-layouts  137 us (12%)
  other arithmetic  73.3 us (6%)
  Pallas kernels  23.5 us (2%)
  between operations  15.8 us (1%)
    ppermute x53, waiting for transfers between devices, swap(): return lax.ppermute(block, axis, [(i, i ^ bits) for i in range(count)])  244 us
    unnamed x9, waiting for transfers between devices  175 us
    ppermute x53, starting transfers between devices, swap(): return lax.ppermute(block, axis, [(i, i ^ bits) for i in range(count)])  114 us
    ppermute x18, waiting for transfers between devices, collect(): carried = lax.ppermute(send.astype(bf16), 'dp', route)  90.6 us
    dot_general x5, matrix products, matmul(): return jnp.dot(left, right, preferred_element_type=jnp.float32)  66.3 us
    all_gather x3, waiting for transfers between devices, spread(): lax.all_gather(result, 'dp', axis=0, tiled=True, axis_index_groups=line_g...  52.8 us
    dot_general x5, matrix products, contract_cols(): lax.dot_general(left, right, (((1,), (1,)), ((), ())), preferred_element_...  50.1 us
    ppermute x18, starting transfers between devices, collect(): carried = lax.ppermute(send.astype(bf16), 'dp', route)  49.6 us
  transfers between devices with their start and end apart: 78, of which 33 were waited for; matrix products, arithmetic and copies ran while one was open for 22% of the time, Pallas kernels for 1%

profile of v1, /device:TPU:0, one launch (start us, length us, event | category | flops | bytes accessed | tf_op | source)
XLA Modules:
  0.0 1139.6 jit_solution(17906779488742073211)
XLA Ops:
  51.3 52.0 %collective-permute-done.16 = bf16[96,1152]{1,0:T(8,128)(2,1)} collective-permute-done((bf16[96,1152]{1,0:T(8,128)(2,1)}, bf16[96,1152]{1,0:T(8,128)(2,1)}, u32[]{:S(2)}, u32[]{:S(2)}) %collective-permute-start.16) | collective-permute-done | bytes 221216 | tf_op jit(solution)/shard_map/ppermute | solution.py:134
  261.7 14.2 %collective-permute-done.9 = bf16[320,1536]{1,0:T(8,128)(2,1)S(1)} collective-permute-done((bf16[320,1536]{1,0:T(8,128)(2,1)}, bf16[320,1536]{1,0:T(8,128)(2,1)S(1)}, u32[]{:S(2)}, u32[]{:S(2)}) %collective-permute-start.9) | collective-permute-done | bytes 983072 | tf_op jit(solution)/shard_map/ppermute | solution.py:134
  275.8 18.7 %collective-permute-done.10 = bf16[320,1536]{1,0:T(8,128)(2,1)S(1)} collective-permute-done((bf16[320,1536]{1,0:T(8,128)(2,1)}, bf16[320,1536]{1,0:T(8,128)(2,1)S(1)}, u32[]{:S(2)}, u32[]{:S(2)}) %collective-permute-start.10) | collective-permute-done | bytes 983072 | tf_op jit(solution)/shard_map/ppermute | solution.py:134
  304.0 16.4 %fusion.70 = f32[2560,1152]{1,0:T(8,128)} fusion(bf16[2560,1536]{1,0:T(8,128)(2,1)} %constant_dynamic-update-slice_fusion.5, bf16[1536,1152]{1,0:T(8,128)(2,1)} %all-gather.14.cloned.1.call-done), kind=kOutput, calls=%fused_computation.273 | convolution fusion | flops 9059696640 | bytes 23199744 | tf_op jit(solution)/shard_map/dot_general | solution.py:178
  329.5 16.3 %fusion.69 = f32[2560,1152]{1,0:T(8,128)} fusion(bf16[2560,1536]{1,0:T(8,128)(2,1)} %constant_dynamic-update-slice_fusion, bf16[1536,1152]{1,0:T(8,128)(2,1)} %all-gather.12.cloned.1.call-done), kind=kOutput, calls=%fused_computation.272 | convolution fusion | flops 9059696640 | bytes 23199744 | tf_op jit(solution)/shard_map/dot_general | solution.py:178
  345.8 52.8 %all-gather.10.cloned.1.call-done = bf16[1536,1152]{1,0:T(8,128)(2,1)} async-done(((bf16[384,1152]{1,0:T(8,128)(2,1)}), bf16[1536,1152]{1,0:T(8,128)(2,1)}) %all-gather.10.cloned.1.call-update) | async-done | bytes 3538960 | tf_op jit(solution)/shard_map/all_gather | solution.py:276
  398.5 26.6 %multiply_convert_fusion.1 = (bf16[2560,1152]{1,0:T(8,128)(2,1)}, bf16[2560,1152]{1,0:T(8,128)(2,1)}, bf16[2560,1152]{1,0:T(8,128)(2,1)}) fusion(f32[2560,1152]{1,0:T(8,128)} %fusion.70, f32[2560,1152]{1,0:T(8,128)} %fusion.69, bf16[2560,1536]{1,0:T(8,128)(2,1)} %constant_dynamic-update-slice_fusion, bf16[1536,1152]{1,0:T(8,128)(2,1)} %all-gather.10.cloned.1.call-done), kind=kOutput, calls=%fused_computation.2 | convolution fusion | flops 9103933440 | bytes 52690944 | tf_op jit(solution)/shard_map/dot_general | solution.py:178
  425.1 14.5 %convolution_convert_fusion.3 = bf16[1536,1152]{1,0:T(8,128)(2,1)S(1)} fusion(bf16[2560,1536]{1,0:T(8,128)(2,1)} %constant_dynamic-update-slice_fusion, bf16[2560,1152]{1,0:T(8,128)(2,1)} %get-tuple-element.131), kind=kOutput, calls=%fused_computation.11 | convolution fusion | flops 9061466112 | bytes 17301504 | tf_op jit(solution)/shard_map/dot_general | solution.py:166
  451.1 13.8 %fusion.71 = f32[2560,1536]{1,0:T(8,128)} fusion(bf16[2560,1152]{1,0:T(8,128)(2,1)S(1)} %copy-done.58, bf16[1536,1152]{1,0:T(8,128)(2,1)S(1)} %copy-done.53), kind=kOutput, calls=%fused_computation.274 | convolution fusion | flops 9059696640 | bytes 25165824 | tf_op jit(solution)/shard_map/dot_general | solution.py:172
  464.9 16.9 %add_convert_fusion = bf16[2560,1536]{1,0:T(8,128)(2,1)} fusion(f32[2560,1536]{1,0:T(8,128)} %fusion.71, bf16[2560,1152]{1,0:T(8,128)(2,1)} %get-tuple-element.131, bf16[1536,1152]{1,0:T(8,128)(2,1)S(1)} %copy-done.54), kind=kOutput, calls=%fused_computation | convolution fusion | flops 9067560960 | bytes 33030144 | tf_op jit(solution)/shard_map/dot_general | solution.py:172
  491.2 14.4 %convolution_convert_fusion.1 = bf16[1536,1152]{1,0:T(8,128)(2,1)S(1)} fusion(bf16[2560,1536]{1,0:T(8,128)(2,1)} %constant_dynamic-update-slice_fusion.5, bf16[2560,1152]{1,0:T(8,128)(2,1)} %get-tuple-element.133), kind=kOutput, calls=%fused_computation.9 | convolution fusion | flops 9061466112 | bytes 17301504 | tf_op jit(solution)/shard_map/dot_general | solution.py:166
  505.5 13.5 %convolution_convert_fusion = bf16[2560,1536]{1,0:T(8,128)(2,1)S(1)} fusion(bf16[2560,1152]{1,0:T(8,128)(2,1)} %get-tuple-element.133, bf16[1536,1152]{1,0:T(8,128)(2,1)} %all-gather.14.cloned.1.call-done), kind=kOutput, calls=%fused_computation.6 | convolution fusion | flops 9063628800 | bytes 17301504 | tf_op jit(solution)/shard_map/dot_general | solution.py:172
  531.9 14.5 %collective-permute-done.62 = bf16[384,1152]{1,0:T(8,128)(2,1)S(1)} collective-permute-done((bf16[384,1152]{1,0:T(8,128)(2,1)S(1)}, bf16[384,1152]{1,0:T(8,128)(2,1)S(1)}, u32[]{:S(2)}, u32[]{:S(2)}) %collective-permute-start.62) | collective-permute-done | bytes 884768 | tf_op jit(solution)/shard_map/ppermute | solution.py:354
  551.8 13.5 %collective-permute-done.45 = bf16[384,1152]{1,0:T(8,128)(2,1)S(1)} collective-permute-done((bf16[384,1152]{1,0:T(8,128)(2,1)S(1)}, bf16[384,1152]{1,0:T(8,128)(2,1)S(1)}, u32[]{:S(2)}, u32[]{:S(2)}) %collective-permute-start.45) | collective-permute-done | bytes 884768 | tf_op jit(solution)/shard_map/ppermute | solution.py:354
  571.1 13.2 %collective-permute-done.54 = bf16[384,1152]{1,0:T(8,128)(2,1)S(1)} collective-permute-done((bf16[384,1152]{1,0:T(8,128)(2,1)S(1)}, bf16[384,1152]{1,0:T(8,128)(2,1)S(1)}, u32[]{:S(2)}, u32[]{:S(2)}) %collective-permute-start.54) | collective-permute-done | bytes 884768 | tf_op jit(solution)/shard_map/ppermute | solution.py:354
  590.0 13.2 %collective-permute-done.63 = bf16[384,1152]{1,0:T(8,128)(2,1)S(1)} collective-permute-done((bf16[384,1152]{1,0:T(8,128)(2,1)S(1)}, bf16[384,1152]{1,0:T(8,128)(2,1)S(1)}, u32[]{:S(2)}, u32[]{:S(2)}) %collective-permute-start.63) | collective-permute-done | bytes 884768 | tf_op jit(solution)/shard_map/ppermute | solution.py:354
  622.2 15.0 %collective-permute-start.64 = (bf16[384,1152]{1,0:T(8,128)(2,1)S(1)}, bf16[384,1152]{1,0:T(8,128)(2,1)S(1)}, u32[]{:S(2)}, u32[]{:S(2)}) collective-permute-start(bf16[384,1152]{1,0:T(8,128)(2,1)S(1)} %get-tuple-element.151), channel_id=1, source_target_pairs={{0,8},{2,10},{4,12},{6,14},{8,16},{10,18},{12,20},{14,22},{16,24},... | collective-permute-start | bytes 2654216 | tf_op jit(solution)/shard_map/ppermute | solution.py:354
  685.3 40.3 %collective-permute-done.52 = bf16[96,1152]{1,0:T(8,128)(2,1)S(1)} collective-permute-done((bf16[96,1152]{1,0:T(8,128)(2,1)S(1)}, bf16[96,1152]{1,0:T(8,128)(2,1)S(1)}, u32[]{:S(2)}, u32[]{:S(2)}) %collective-permute-start.52) | collective-permute-done | bytes 221216 | tf_op jit(solution)/shard_map/ppermute | solution.py:134
  738.5 13.9 %attention_backward.1 = (f32[640,768]{1,0:T(8,128)}, f32[5120,128]{1,0:T(8,128)}, f32[5120,128]{1,0:T(8,128)}) custom-call(s32[40]{0:T(128)} %reshape.478.info, bf16[640,768]{1,0:T(8,128)(2,1)} %add_convert_fusion.2.q_ref, bf16[640,768]{1,0:T(8,128)(2,1)} %convolution_convert_fusion.6.do_ref, bf16[640,768]{1,0:T(8,128)(2,1)} %get-tuple-element.55.o_ref, ...), custom_call_target="tpu_custom_call" | custom-call | flops 11324620800 | bytes 12582912 | tf_op jit(solution)/shard_map/attention_backward/pallas_call | solution.py:117
  769.2 43.5 %collective-permute-start.41 = (bf16[640,256]{1,0:T(8,128)(2,1)}, bf16[640,256]{1,0:T(8,128)(2,1)}, u32[]{:S(2)}, u32[]{:S(2)}) collective-permute-start(bf16[640,256]{1,0:T(8,128)(2,1)} %get-tuple-element.139), channel_id=1, source_target_pairs={{0,14},{2,12},{4,10},{6,8},{8,6},{10,4},{12,2},{14,0},{16,30},{18,... | collective-permute-start | bytes 983048 | tf_op jit(solution)/shard_map/ppermute | solution.py:134
  903.9 21.9 %collective-permute-done.25 = bf16[320,1536]{1,0:T(8,128)(2,1)S(1)} collective-permute-done((bf16[320,1536]{1,0:T(8,128)(2,1)S(1)}, bf16[320,1536]{1,0:T(8,128)(2,1)S(1)}, u32[]{:S(2)}, u32[]{:S(2)}) %collective-permute-start.25) | collective-permute-done | bytes 983072 | tf_op jit(solution)/shard_map/ppermute | solution.py:134
  925.8 21.2 %collective-permute-done.24 = bf16[320,1536]{1,0:T(8,128)(2,1)S(1)} collective-permute-done((bf16[320,1536]{1,0:T(8,128)(2,1)S(1)}, bf16[320,1536]{1,0:T(8,128)(2,1)S(1)}, u32[]{:S(2)}, u32[]{:S(2)}) %collective-permute-start.24) | collective-permute-done | bytes 983072 | tf_op jit(solution)/shard_map/ppermute | solution.py:134
  950.9 36.9 %reduce-scatter.9.cloned.1.call-done = bf16[96,896]{1,0:T(8,128)(2,1)} async-done(((bf16[1536,896]{1,0:T(8,128)(2,1)}), bf16[96,896]{1,0:T(8,128)(2,1)}) %reduce-scatter.9.cloned.1.call-update) | async-done | bytes 172048
  989.9 137.2 %reduce-scatter.7.cloned.1.call-done = bf16[96,1152]{1,0:T(8,128)(2,1)} async-done(((bf16[1536,1152]{1,0:T(8,128)(2,1)}), bf16[96,1152]{1,0:T(8,128)(2,1)}) %reduce-scatter.7.cloned.1.call-update) | async-done | bytes 221200
  (466 shorter events, 469.3 us)
Async XLA Ops:
  7.2 119.8 %all-gather.6.cloned.1.call-start = ((), (), s32[]{:S(2)}) async-start(), calls=%async_computation.2 | async-start | bytes 3760128 | tf_op jit(solution)/shard_map/all_gather | solution.py:264
  15.8 192.4 %all-gather.8.cloned.1.call-start = ((), (), s32[]{:S(2)}) async-start(), calls=%async_computation.3 | async-start | bytes 2506752 | tf_op jit(solution)/shard_map/all_gather | solution.py:265
  16.5 287.5 %all-gather.14.cloned.1.call-start = ((), (), s32[]{:S(2)}) async-start(), calls=%async_computation.6 | async-start | bytes 4423680 | tf_op jit(solution)/shard_map/all_gather | solution.py:276
  36.3 293.2 %all-gather.12.cloned.1.call-start = ((), (), s32[]{:S(2)}) async-start(), calls=%async_computation.5 | async-start | bytes 4423680 | tf_op jit(solution)/shard_map/all_gather | solution.py:276
  36.3 83.0 %collective-permute-start.26 = (bf16[320,1536]{1,0:T(8,128)(2,1)S(1)}, bf16[320,1536]{1,0:T(8,128)(2,1)S(1)}, u32[]{:S(2)}, u32[]{:S(2)}) collective-permute-start(bf16[320,1536]{1,0:T(8,128)(2,1)S(1)} %copy-done.5), channel_id=1, source_target_pairs={{0,2},{2,0},{4,6},{6,4},{8,10},{10,8},{12,14},{14,12},{16,18},{18,... | collective-permute-start | bytes 2949128 | tf_op jit(solution)/shard_map/ppermute | solution.py:134
  37.7 81.7 %collective-permute-start.27 = (bf16[320,1536]{1,0:T(8,128)(2,1)S(1)}, bf16[320,1536]{1,0:T(8,128)(2,1)}, u32[]{:S(2)}, u32[]{:S(2)}) collective-permute-start(bf16[320,1536]{1,0:T(8,128)(2,1)S(1)} %copy-done.5), channel_id=1, source_target_pairs={{0,4},{2,6},{4,0},{6,2},{8,12},{10,14},{12,8},{14,10},{16,20},{18,... | collective-permute-start | bytes 2949128 | tf_op jit(solution)/shard_map/ppermute | solution.py:134
  39.0 81.1 %collective-permute-start.28 = (bf16[320,1536]{1,0:T(8,128)(2,1)S(1)}, bf16[320,1536]{1,0:T(8,128)(2,1)}, u32[]{:S(2)}, u32[]{:S(2)}) collective-permute-start(bf16[320,1536]{1,0:T(8,128)(2,1)S(1)} %copy-done.5), channel_id=1, source_target_pairs={{0,6},{2,4},{4,2},{6,0},{8,14},{10,12},{12,10},{14,8},{16,22},{18,... | collective-permute-start | bytes 2949128 | tf_op jit(solution)/shard_map/ppermute | solution.py:134
  40.4 77.1 %collective-permute-start = (bf16[320,1536]{1,0:T(8,128)(2,1)S(1)}, bf16[320,1536]{1,0:T(8,128)(2,1)}, u32[]{:S(2)}, u32[]{:S(2)}) collective-permute-start(bf16[320,1536]{1,0:T(8,128)(2,1)S(1)} %copy-done.7), channel_id=1, source_target_pairs={{0,1},{1,0},{2,3},{3,2},{4,5},{5,4},{6,7},{7,6},{8,9},{9,8},{10,11... | collective-permute-start | bytes 2949128 | tf_op jit(solution)/shard_map/ppermute | solution.py:134
  43.5 59.8 %collective-permute-start.16 = (bf16[96,1152]{1,0:T(8,128)(2,1)}, bf16[96,1152]{1,0:T(8,128)(2,1)}, u32[]{:S(2)}, u32[]{:S(2)}) collective-permute-start(bf16[96,1152]{1,0:T(8,128)(2,1)} %get-tuple-element.197), channel_id=1, source_target_pairs={{0,2},{2,0},{4,6},{6,4},{8,10},{10,8},{12,14},{14,12},{16,18},{18,... | collective-permute-start | bytes 663560 | tf_op jit(solution)/shard_map/ppermute | solution.py:134
  117.0 281.5 %all-gather.10.cloned.1.call-start = ((), (), s32[]{:S(2)}) async-start(), calls=%async_computation.4 | async-start | bytes 4423680 | tf_op jit(solution)/shard_map/all_gather | solution.py:276
  127.0 172.8 %collective-permute-start.29 = (bf16[1280,1536]{1,0:T(8,128)(2,1)}, bf16[1280,1536]{1,0:T(8,128)(2,1)}, u32[]{:S(2)}, u32[]{:S(2)}) collective-permute-start(bf16[1280,1536]{1,0:T(8,128)(2,1)} %pad_maximum_fusion.1), channel_id=1, source_target_pairs={{0,1},{1,0},{2,3},{3,2},{4,5},{5,4},{6,7},{7,6},{8,9},{9,8},{10,11... | collective-permute-start | bytes 11796488 | tf_op jit(solution)/shard_map/ppermute | solution.py:134
  256.1 731.8 %reduce-scatter.9.cloned.1.call-start = ((), (), s32[]{:S(2)}) async-start(), calls=%async_computation.8 | async-start | bytes 2924544
  486.0 185.8 %collective-permute-start.30 = (bf16[1280,1536]{1,0:T(8,128)(2,1)}, bf16[1280,1536]{1,0:T(8,128)(2,1)S(1)}, u32[]{:S(2)}, u32[]{:S(2)}) collective-permute-start(bf16[1280,1536]{1,0:T(8,128)(2,1)} %slice.295), channel_id=1, source_target_pairs={{0,1},{1,0},{2,3},{3,2},{4,5},{5,4},{6,7},{7,6},{8,9},{9,8},{10,11... | collective-permute-start | bytes 11796488 | tf_op jit(solution)/shard_map/ppermute | solution.py:134
  524.2 46.1 %collective-permute-start.56 = (bf16[384,1152]{1,0:T(8,128)(2,1)}, bf16[384,1152]{1,0:T(8,128)(2,1)S(1)}, u32[]{:S(2)}, u32[]{:S(2)}) collective-permute-start(bf16[384,1152]{1,0:T(8,128)(2,1)} %get-tuple-element.158), channel_id=1, source_target_pairs={{24,16},{26,18},{28,20},{30,22},{25,17},{27,19},{29,21},{31,23}} | collective-permute-start | bytes 2654216 | tf_op jit(solution)/shard_map/ppermute | solution.py:354
  675.8 52.9 %collective-permute-start.33 = (bf16[320,1536]{1,0:T(8,128)(2,1)S(1)}, bf16[320,1536]{1,0:T(8,128)(2,1)S(1)}, u32[]{:S(2)}, u32[]{:S(2)}) collective-permute-start(bf16[320,1536]{1,0:T(8,128)(2,1)S(1)} %get-tuple-element.146), channel_id=1, source_target_pairs={{0,6},{2,4},{4,2},{6,0},{8,14},{10,12},{12,10},{14,8},{16,22},{18,... | collective-permute-start | bytes 2949128 | tf_op jit(solution)/shard_map/ppermute | solution.py:134
  678.2 50.5 %collective-permute-start.32 = (bf16[320,1536]{1,0:T(8,128)(2,1)S(1)}, bf16[320,1536]{1,0:T(8,128)(2,1)S(1)}, u32[]{:S(2)}, u32[]{:S(2)}) collective-permute-start(bf16[320,1536]{1,0:T(8,128)(2,1)S(1)} %get-tuple-element.147), channel_id=1, source_target_pairs={{0,4},{2,6},{4,0},{6,2},{8,12},{10,14},{12,8},{14,10},{16,20},{18,... | collective-permute-start | bytes 2949128 | tf_op jit(solution)/shard_map/ppermute | solution.py:134
  678.8 50.0 %collective-permute-start.31 = (bf16[320,1536]{1,0:T(8,128)(2,1)S(1)}, bf16[320,1536]{1,0:T(8,128)(2,1)S(1)}, u32[]{:S(2)}, u32[]{:S(2)}) collective-permute-start(bf16[320,1536]{1,0:T(8,128)(2,1)S(1)} %get-tuple-element.145), channel_id=1, source_target_pairs={{0,2},{2,0},{4,6},{6,4},{8,10},{10,8},{12,14},{14,12},{16,18},{18,... | collective-permute-start | bytes 2949128 | tf_op jit(solution)/shard_map/ppermute | solution.py:134
  680.3 45.3 %collective-permute-start.52 = (bf16[96,1152]{1,0:T(8,128)(2,1)S(1)}, bf16[96,1152]{1,0:T(8,128)(2,1)S(1)}, u32[]{:S(2)}, u32[]{:S(2)}) collective-permute-start(bf16[96,1152]{1,0:T(8,128)(2,1)S(1)} %copy-done.40), channel_id=1, source_target_pairs={{0,6},{2,4},{4,2},{6,0},{8,14},{10,12},{12,10},{14,8},{16,22},{18,... | collective-permute-start | bytes 663560 | tf_op jit(solution)/shard_map/ppermute | solution.py:134
  683.7 44.3 %collective-permute-start.59 = (bf16[96,1152]{1,0:T(8,128)(2,1)S(1)}, bf16[96,1152]{1,0:T(8,128)(2,1)S(1)}, u32[]{:S(2)}, u32[]{:S(2)}) collective-permute-start(bf16[96,1152]{1,0:T(8,128)(2,1)S(1)} %copy-done.41), channel_id=1, source_target_pairs={{0,2},{2,0},{4,6},{6,4},{8,10},{10,8},{12,14},{14,12},{16,18},{18,... | collective-permute-start | bytes 663560 | tf_op jit(solution)/shard_map/ppermute | solution.py:134
  762.1 365.0 %reduce-scatter.7.cloned.1.call-start = ((), (), s32[]{:S(2)}) async-start(), calls=%async_computation.7 | async-start | bytes 3760128
  769.2 56.7 %collective-permute-start.41 = (bf16[640,256]{1,0:T(8,128)(2,1)}, bf16[640,256]{1,0:T(8,128)(2,1)}, u32[]{:S(2)}, u32[]{:S(2)}) collective-permute-start(bf16[640,256]{1,0:T(8,128)(2,1)} %get-tuple-element.139), channel_id=1, source_target_pairs={{0,14},{2,12},{4,10},{6,8},{8,6},{10,4},{12,2},{14,0},{16,30},{18,... | collective-permute-start | bytes 983048 | tf_op jit(solution)/shard_map/ppermute | solution.py:134
  842.5 51.3 %collective-permute-start.22 = (bf16[1280,1536]{1,0:T(8,128)(2,1)}, bf16[1280,1536]{1,0:T(8,128)(2,1)}, u32[]{:S(2)}, u32[]{:S(2)}) collective-permute-start(bf16[1280,1536]{1,0:T(8,128)(2,1)} %slice.289), channel_id=1, source_target_pairs={{0,1},{1,0},{2,3},{3,2},{4,5},{5,4},{6,7},{7,6},{8,9},{9,8},{10,11... | collective-permute-start | bytes 11796488 | tf_op jit(solution)/shard_map/ppermute | solution.py:134
  901.4 45.6 %collective-permute-start.24 = (bf16[320,1536]{1,0:T(8,128)(2,1)S(1)}, bf16[320,1536]{1,0:T(8,128)(2,1)S(1)}, u32[]{:S(2)}, u32[]{:S(2)}) collective-permute-start(bf16[320,1536]{1,0:T(8,128)(2,1)S(1)} %get-tuple-element.150), channel_id=1, source_target_pairs={{0,4},{2,6},{4,0},{6,2},{8,12},{10,14},{12,8},{14,10},{16,20},{18,... | collective-permute-start | bytes 2949128 | tf_op jit(solution)/shard_map/ppermute | solution.py:134
  902.1 44.9 %collective-permute-start.23 = (bf16[320,1536]{1,0:T(8,128)(2,1)S(1)}, bf16[320,1536]{1,0:T(8,128)(2,1)S(1)}, u32[]{:S(2)}, u32[]{:S(2)}) collective-permute-start(bf16[320,1536]{1,0:T(8,128)(2,1)S(1)} %get-tuple-element.148), channel_id=1, source_target_pairs={{0,2},{2,0},{4,6},{6,4},{8,10},{10,8},{12,14},{14,12},{16,18},{18,... | collective-permute-start | bytes 2949128 | tf_op jit(solution)/shard_map/ppermute | solution.py:134
  (114 other events, 2394.6 us)
Sparse Core Ops, SparseCore 0:
  15.9 95.0 all-gather.5
  113.8 71.2 all-gather.7
  186.7 71.7 all-gather.13
  259.9 68.5 all-gather.11
  329.9 68.5 all-gather.9
  762.2 225.5 reduce-scatter.8
  993.8 133.2 reduce-scatter.6

commit v2 on v1

v2 whole, which is shorter than its diff:
```python
import functools

import jax
import jax.numpy as jnp
from jax import lax
from jax.experimental import pallas as pl
from jax.experimental.pallas import tpu as pltpu
from jax.sharding import PartitionSpec as P

EPS = 1e-06
THETA = 10000.0
TREE_TOK = 5120
TRUNK = 2048
PLANE = 4
NEG = -1e30
QB=128; KC=512; KB=256
LOG2E=1.4426950408889634

MESH = pl.DeviceIdType.MESH


def dot_nt(a,b): return lax.dot_general(a,b,(((1,),(1,)),((),())),preferred_element_type=jnp.float32)
def dot_nn(a,b): return lax.dot_general(a,b,(((1,),(0,)),((),())),preferred_element_type=jnp.float32)

def fwd_kernel(info, q_ref, t_ref, o_ref, l_ref, *, heads, scale):
    blk = pl.program_id(0)
    nfull = info[blk*8]
    rows = heads*QB
    q = jnp.concatenate([q_ref[:, h*128:(h+1)*128] for h in range(heads)], axis=0)
    c2 = scale*LOG2E
    def step(carry, s, v):
        m,l,acc = carry
        mt = s[:, :128]
        for j in range(1, KC//128): mt = jnp.maximum(mt, s[:, j*128:(j+1)*128])
        mn = jnp.maximum(m, jnp.max(mt, axis=1, keepdims=True))
        p = jnp.exp2((s-mn)*c2)
        ps = p[:, :128]
        for j in range(1, KC//128): ps = ps + p[:, j*128:(j+1)*128]
        a = jnp.exp2((m-mn)*c2)
        l = l*a + ps
        acc = acc*a + dot_nn(p.astype(jnp.bfloat16), v)
        return mn,l,acc
    def body(c, carry):
        k = t_ref[pl.ds(pl.multiple_of(c*KC,KC),KC),0:128]
        v = t_ref[pl.ds(pl.multiple_of(c*KC,KC),KC),128:256]
        return step(carry, dot_nt(q,k), v)
    init = (jnp.full((rows,1),NEG,jnp.float32), jnp.zeros((rows,128),jnp.float32), jnp.zeros((rows,128),jnp.float32))
    b0 = pl.multiple_of(info[blk*8+1]*KB,KB); b1 = pl.multiple_of(info[blk*8+2]*KB,KB)
    k = jnp.concatenate([t_ref[pl.ds(b0,KB),0:128], t_ref[pl.ds(b1,KB),0:128]],axis=0)
    v = jnp.concatenate([t_ref[pl.ds(b0,KB),128:256], t_ref[pl.ds(b1,KB),128:256]],axis=0)
    s = dot_nt(q,k)
    col = lax.broadcasted_iota(jnp.int32,(QB,KC),1)
    row = lax.broadcasted_iota(jnp.int32,(QB,KC),0)
    base = jnp.where(col<KB, info[blk*8+3], info[blk*8+4]-KB)
    ok = col+base <= row
    s = jnp.concatenate([jnp.where(ok, s[h*QB:(h+1)*QB], NEG) for h in range(heads)],axis=0)
    carry = step(init, s, v)
    m,l,acc = lax.fori_loop(0,nfull,body,carry)
    lsum = jnp.sum(l,axis=1,keepdims=True)
    out = (acc/lsum).astype(jnp.bfloat16)
    o_ref[...] = jnp.concatenate([out[h*QB:(h+1)*QB] for h in range(heads)],axis=1)
    lse2 = m*c2+jnp.log2(lsum)
    t = jnp.broadcast_to(lse2,(rows,128)).T
    l_ref[...] = t[:8,:].reshape(1,8,rows)

def attn_fwd(info, q, tree, scale):
    T=q.shape[0]; heads=q.shape[1]//128; nb=T//QB; rows=heads*QB
    return pl.pallas_call(functools.partial(fwd_kernel,heads=heads,scale=scale),
        grid_spec=pltpu.PrefetchScalarGridSpec(num_scalar_prefetch=1,grid=(nb,),
            in_specs=[pl.BlockSpec((QB,heads*128),lambda i,s:(i,0)),
                      pl.BlockSpec(tree.shape,lambda i,s:(0,0))],
            out_specs=[pl.BlockSpec((QB,heads*128),lambda i,s:(i,0)),pl.BlockSpec((1,8,rows),lambda i,s:(i,0,0))]),
        out_shape=[jax.ShapeDtypeStruct((T,heads*128),jnp.bfloat16),jax.ShapeDtypeStruct((nb,8,rows),jnp.float32)],
        compiler_params=pltpu.CompilerParams(vmem_limit_bytes=56<<20),
        name="attention_forward",
        cost_estimate=pl.CostEstimate(flops=4*T*heads*128*2304,bytes_accessed=6<<20,transcendentals=T*heads*2304),
    )(info,q,tree)

def bwd_kernel(info, q_ref, do_ref, o_ref, l_ref, t_ref, dq_ref, dt_ref, sum_ref, *, heads, scale):
    blk = pl.program_id(0)
    @pl.when(blk==0)
    def _():
        sum_ref[...] = jnp.zeros_like(sum_ref)
    nfull = info[blk*8]
    rows = heads*QB
    cat = lambda ref: jnp.concatenate([ref[:, h*128:(h+1)*128] for h in range(heads)], axis=0)
    q = cat(q_ref); do = cat(do_ref); o = cat(o_ref)
    c2 = scale*LOG2E
    delta = jnp.sum((do.astype(jnp.float32)*o.astype(jnp.float32)).T, axis=0, keepdims=True)
    lse2 = l_ref[0,0:1,:]
    def tile(k, v, ok):
        s = dot_nt(k,q)
        p = jnp.exp2(s*c2-lse2)
        if ok is not None:
            p = jnp.concatenate([jnp.where(ok, p[:, h*QB:(h+1)*QB], 0.0) for h in range(heads)],axis=1)
        dp = dot_nt(v,do)
        ds = (p*(dp-delta)).astype(jnp.bfloat16)
        dv = dot_nn(p.astype(jnp.bfloat16), do)
        dk = dot_nn(ds, q)
        dq = lax.dot_general(ds,k,(((0,),(0,)),((),())),preferred_element_type=jnp.float32)
        return dq,dk,dv
    def body(c, acc):
        at = pl.ds(pl.multiple_of(c*KC,KC),KC)
        dq,dk,dv = tile(t_ref[at,0:128], t_ref[at,128:256], None)
        sum_ref[at,0:128] += dk
        sum_ref[at,128:256] += dv
        return acc+dq
    b0 = pl.multiple_of(info[blk*8+1]*KB,KB); b1 = pl.multiple_of(info[blk*8+2]*KB,KB)
    k = jnp.concatenate([t_ref[pl.ds(b0,KB),0:128], t_ref[pl.ds(b1,KB),0:128]],axis=0)
    v = jnp.concatenate([t_ref[pl.ds(b0,KB),128:256], t_ref[pl.ds(b1,KB),128:256]],axis=0)
    col = lax.broadcasted_iota(jnp.int32,(KC,QB),0)
    row = lax.broadcasted_iota(jnp.int32,(KC,QB),1)
    base = jnp.where(col<KB, info[blk*8+3], info[blk*8+4]-KB)
    dq,dk,dv = tile(k,v,col+base<=row)
    sum_ref[pl.ds(b0,KB),0:128] += dk[:KB]
    sum_ref[pl.ds(b0,KB),128:256] += dv[:KB]
    sum_ref[pl.ds(b1,KB),0:128] += dk[KB:]
    sum_ref[pl.ds(b1,KB),128:256] += dv[KB:]
    dq = lax.fori_loop(0,nfull,body,dq)
    dq = dq*scale
    dq_ref[...] = jnp.concatenate([dq[h*QB:(h+1)*QB] for h in range(heads)],axis=1)

    @pl.when(blk == pl.num_programs(0) - 1)
    def _():
        dt_ref[...] = sum_ref[...].astype(jnp.bfloat16)


def attn_bwd(info,q,do,o,lse,tree,scale):
    T=q.shape[0]; heads=q.shape[1]//128; nb=T//QB; rows=heads*QB
    qspec=pl.BlockSpec((QB,heads*128),lambda i,s:(i,0))
    full=pl.BlockSpec(tree.shape,lambda i,s:(0,0))
    return pl.pallas_call(functools.partial(bwd_kernel,heads=heads,scale=scale),
        grid_spec=pltpu.PrefetchScalarGridSpec(num_scalar_prefetch=1,grid=(nb,),
            in_specs=[qspec,qspec,qspec,pl.BlockSpec((1,8,rows),lambda i,s:(i,0,0)),full],
            out_specs=[qspec,full],
            scratch_shapes=[pltpu.VMEM(tree.shape,jnp.float32)]),
        out_shape=[jax.ShapeDtypeStruct((T,heads*128),jnp.float32),jax.ShapeDtypeStruct(tree.shape,jnp.bfloat16)],
        compiler_params=pltpu.CompilerParams(vmem_limit_bytes=56<<20),
        name="attention_backward",
        cost_estimate=pl.CostEstimate(flops=10*T*heads*128*2304,bytes_accessed=12<<20,transcendentals=T*heads*2304),
    )(info,q,do,o,lse,tree)


def plane_partner(dp, bits):
    one = dp + 1 - 2 * lax.rem(dp, 2)
    if bits == 1:
        return one
    two = 2 - 4 * lax.rem(dp // 2, 2)
    return (dp if bits == 2 else one) + two


def line_partner(dp):
    return dp + PLANE - 2 * PLANE * lax.rem(dp // PLANE, 2)


def greet(dp, core, lines):
    z_at = dp // PLANE
    barrier = pltpu.get_barrier_semaphore()
    for bits in range(1, PLANE):
        pl.semaphore_signal(barrier, inc=1, device_id={"dp": plane_partner(dp, bits)}, device_id_type=MESH)
    pl.semaphore_signal(barrier, inc=1, device_id={"tensor": 1 - core}, device_id_type=MESH)

    @pl.when(z_at > 0)
    def _():
        pl.semaphore_signal(barrier, inc=1, device_id={"dp": dp - PLANE}, device_id_type=MESH)

    @pl.when(z_at < lines - 1)
    def _():
        pl.semaphore_signal(barrier, inc=1, device_id={"dp": dp + PLANE}, device_id_type=MESH)

    beside = jnp.minimum(z_at, 1) + jnp.minimum(lines - 1 - z_at, 1)
    pl.semaphore_wait(barrier, PLANE + beside)


class Gather:
    def __init__(self, own, whole, sems, dp, lines):
        self.own, self.whole, self.dp, self.lines = own, whole, dp, lines
        self.z_at = dp // PLANE
        self.local_sem, self.line_send, self.line_recv, self.plane_send, self.plane_recv = sems
        self.rows_per = own.shape[0]

    def rows(self, owner):
        return pl.ds(pl.multiple_of(owner * self.rows_per, self.rows_per), self.rows_per)

    def local(self):
        return pltpu.make_async_copy(self.own, self.whole.at[self.rows(self.dp)], self.local_sem)

    def place(self, sign):
        return self.z_at if sign == 1 else self.lines - 1 - self.z_at

    def line_copy(self, sign, step):
        owner = self.dp - sign * step * PLANE
        way = (1 - sign) // 2
        return pltpu.make_async_remote_copy(
            src_ref=self.own if step == 0 else self.whole.at[self.rows(owner)],
            dst_ref=self.whole.at[self.rows(owner)],
            send_sem=self.line_send.at[way, step], recv_sem=self.line_recv.at[way, step],
            device_id={"dp": self.dp + sign * PLANE}, device_id_type=MESH)

    def line_start(self, sign, step):
        place = self.place(sign)

        @pl.when((place >= step) & (place < self.lines - 1))
        def _():
            self.line_copy(sign, step).start()

    def line_wait_send(self, sign, step):
        place = self.place(sign)

        @pl.when((place >= step) & (place < self.lines - 1))
        def _():
            self.line_copy(sign, step).wait_send()

    def plane_copy(self, bits, owner, own=False):
        z = owner // PLANE
        return pltpu.make_async_remote_copy(
            src_ref=self.own if own else self.whole.at[self.rows(owner)],
            dst_ref=self.whole.at[self.rows(owner)],
            send_sem=self.plane_send.at[bits - 1, z], recv_sem=self.plane_recv.at[bits - 1, z],
            device_id={"dp": plane_partner(self.dp, bits)}, device_id_type=MESH)

    def plane_start_own(self):
        for bits in range(1, PLANE):
            self.plane_copy(bits, self.dp, True).start()

    def arrived(self, sign, step):
        place = self.place(sign)

        @pl.when(place >= step + 1)
        def _():
            owner = self.dp - sign * (step + 1) * PLANE
            pltpu.make_async_remote_copy(
                src_ref=self.own, dst_ref=self.whole.at[self.rows(owner)],
                send_sem=self.line_send.at[(1 - sign) // 2, step],
                recv_sem=self.line_recv.at[(1 - sign) // 2, step],
                device_id={"dp": self.dp - sign * PLANE}, device_id_type=MESH).wait_recv()
            if step + 1 < self.lines - 1:

                @pl.when(place < self.lines - 1)
                def _():
                    self.line_copy(sign, step + 1).start()

            for bits in range(1, PLANE):
                self.plane_copy(bits, owner).start()

    def plane_wait_recv(self):
        for bits in range(1, PLANE):
            for z in range(self.lines):
                owner = z * PLANE + lax.rem(plane_partner(self.dp, bits), PLANE)
                self.plane_copy(bits, owner).wait_recv()

    def finish(self):
        for sign in (1, -1):
            for step in range(self.lines - 1):
                self.line_wait_send(sign, step)
        for bits in range(1, PLANE):
            for z in range(self.lines):
                self.plane_copy(bits, z * PLANE + lax.rem(self.dp, PLANE)).wait_send()


def front_kernel(*refs, lines, members, steps):
    (
        ff_in, first_in, out_in, extra_in, x_in, cos_in, sin_in,
        own_out, *slab_outs,
    ) = refs[: 8 + 2 * steps]
    (
        first_out, out_t, q_out, tree_out, normed_out, rows_out,
        first_all, extra_all, x_all, normed, pair,
        first_local, first_ls, first_lr, first_ps, first_pr,
        extra_local, extra_ls, extra_lr, extra_ps, extra_pr,
        out_local, out_ls, out_lr, out_ps, out_pr,
        spread_local, spread_send, spread_recv, hop_send, hop_recv,
        x_local, x_send, x_recv, keep_sem, pair_local, pair_send, pair_recv,
    ) = refs[8 + 2 * steps :]
    bf16, f32 = jnp.bfloat16, jnp.float32
    dp = lax.axis_index("dp")
    core = lax.axis_index("tensor")
    z_at = dp // PLANE
    j_at = lax.rem(dp, PLANE)
    half, width = x_in.shape
    shard = first_in.shape[0]
    local_tok = 2 * half
    slab_rows = PLANE * shard
    ups, downs = slab_outs[:steps], slab_outs[steps:]
    mate = {"tensor": 1 - core}

    first = Gather(first_in, first_all, (first_local, first_ls, first_lr, first_ps, first_pr), dp, lines)
    extra = Gather(extra_in, extra_all, (extra_local, extra_ls, extra_lr, extra_ps, extra_pr), dp, lines)
    outer = Gather(out_in, out_t, (out_local, out_ls, out_lr, out_ps, out_pr), dp, lines)

    token_rows = lambda c: pl.ds(pl.multiple_of(c * half, half), half)
    x_keep = pltpu.make_async_copy(x_in, x_all.at[token_rows(core)], x_local)
    x_copy = pltpu.make_async_remote_copy(
        src_ref=x_in, dst_ref=x_all.at[token_rows(core)], send_sem=x_send, recv_sem=x_recv,
        device_id=mate, device_id_type=MESH)
    shard_rows = lambda j: pl.ds(pl.multiple_of(j * shard, shard), shard)

    def spread(which, bits):
        there = lax.rem(plane_partner(dp, bits), PLANE)
        return pltpu.make_async_remote_copy(
            src_ref=ff_in.at[which, there], dst_ref=own_out.at[which, shard_rows(j_at)],
            send_sem=spread_send.at[which, bits - 1], recv_sem=spread_recv.at[which, bits - 1],
            device_id={"dp": plane_partner(dp, bits)}, device_id_type=MESH)

    def spread_keep(which):
        return pltpu.make_async_copy(ff_in.at[which, j_at], own_out.at[which, shard_rows(j_at)], spread_local.at[which])

    def hop(which, sign, step):
        way = (1 - sign) // 2
        outs = ups if sign == 1 else downs
        return pltpu.make_async_remote_copy(
            src_ref=(own_out if step == 0 else outs[step - 1]).at[which], dst_ref=outs[step].at[which],
            send_sem=hop_send.at[which, way, step], recv_sem=hop_recv.at[which, way, step],
            device_id={"dp": dp + sign * PLANE}, device_id_type=MESH)

    for one in (first, extra, outer):
        one.local().start()
    x_keep.start()
    for which in range(3):
        spread_keep(which).start()
    greet(dp, core, lines)
    x_copy.start()
    for sign in (1, -1):
        first.line_start(sign, 0)
        extra.line_start(sign, 0)
    for bits in range(1, PLANE):
        spread(2, bits).start()
    first.plane_start_own()
    extra.plane_start_own()
    for which in (0, 1):
        for bits in range(1, PLANE):
            spread(which, bits).start()

    x_keep.wait()
    x_copy.wait_recv()
    wide = x_all[...].astype(f32)
    scale = lax.rsqrt(jnp.mean(wide * wide, axis=1, keepdims=True) + EPS)

    def hop_start(which):
        spread_keep(which).wait()
        for bits in range(1, PLANE):
            spread(which, bits).wait_recv()
        for sign in (1, -1):
            place = z_at if sign == 1 else lines - 1 - z_at

            @pl.when(place < lines - 1)
            def _():
                hop(which, sign, 0).start()

    for step in range(lines - 1):
        for sign in (1, -1):
            first.arrived(sign, step)
            extra.arrived(sign, step)
        if step == 0:
            hop_start(2)
    hop_start(0)
    hop_start(1)
    first.local().wait()
    extra.local().wait()
    for sign in (1, -1):
        outer.line_start(sign, 0)
    outer.plane_start_own()
    extra.plane_wait_recv()
    first.plane_wait_recv()
    keep = pltpu.make_async_copy(first_all, first_out, keep_sem)
    keep.start()
    small = extra_all[0:16, :].astype(f32)
    for owner in range(1, lines * PLANE):
        small = small + extra_all[16 * owner : 16 * (owner + 1), :].astype(f32)
    rows_out[...] = small
    normed[...] = (x_all[...].astype(f32) * scale * small[0:1, :]).astype(bf16)
    normed_out[...] = normed[...]
    columns = first_all.shape[1]
    q_width = columns - 256
    cosines, sines = cos_in[...], sin_in[...]

    def project(at, count):
        part = dot_nn(normed[...], first_all[:, at : at + count])
        return part + small[2:3, at : at + count]

    def turned(part):
        return (part * cosines + pltpu.roll(part, 64, 1) * sines).astype(bf16)

    both = project(q_width, 256)
    pair[:, 0:128] = turned(both[:, 0:128])
    pair[:, 128:256] = both[:, 128:256].astype(bf16)
    member = lax.rem(dp, members)
    tree_rows = lambda m: pl.ds(pl.multiple_of(m * local_tok, local_tok), local_tok)
    partner = lax.rem(line_partner(dp), members)
    pair_keep = pltpu.make_async_copy(pair, tree_out.at[tree_rows(member)], pair_local)
    pair_keep.start()

    def pair_copy(bits, forward=False):
        at = tree_rows(partner if forward else member)
        index = PLANE + bits - 1 if forward else bits
        return pltpu.make_async_remote_copy(
            src_ref=tree_out.at[at] if forward else pair, dst_ref=tree_out.at[at],
            send_sem=pair_send.at[index], recv_sem=pair_recv.at[index],
            device_id={"dp": plane_partner(dp, bits) if bits else line_partner(dp)}, device_id_type=MESH)

    for bits in range(PLANE):
        pair_copy(bits).start()
    for at in range(0, q_width, 256):
        part = project(at, 256)
        q_out[:, at : at + 128] = turned(part[:, 0:128])
        q_out[:, at + 128 : at + 256] = turned(part[:, 128:256])
    pltpu.make_async_remote_copy(
        src_ref=pair, dst_ref=tree_out.at[tree_rows(partner)], send_sem=pair_send.at[0],
        recv_sem=pair_recv.at[0], device_id={"dp": line_partner(dp)}, device_id_type=MESH).wait_recv()
    for bits in range(1, PLANE):
        pair_copy(bits, True).start()
    for step in range(lines - 1):
        for sign in (1, -1):
            outer.arrived(sign, step)
    for step in range(steps):
        for which in (2, 0, 1):
            for sign in (1, -1):
                place = z_at if sign == 1 else lines - 1 - z_at

                @pl.when(place >= step + 1)
                def _():
                    hop(which, sign, step).wait_recv()
                    if step + 1 < steps:

                        @pl.when(place < lines - 1)
                        def _():
                            hop(which, sign, step + 1).start()
    for bits in range(1, PLANE):
        pair_copy(bits).wait_recv()
        pair_copy(bits, True).wait_recv()
    outer.plane_wait_recv()

    for one in (first, extra, outer):
        one.finish()
    outer.local().wait()
    x_copy.wait_send()
    keep.wait()
    pair_keep.wait()
    for bits in range(PLANE):
        pair_copy(bits).wait_send()
        if bits:
            pair_copy(bits, True).wait_send()
    for which in range(3):
        for bits in range(1, PLANE):
            spread(which, bits).wait_send()
        for sign in (1, -1):
            for step in range(steps):
                place = z_at if sign == 1 else lines - 1 - z_at

                @pl.when((place >= step) & (place < lines - 1))
                def _():
                    hop(which, sign, step).wait_send()


def front(ff_blocks, first, out_t, extra, x, cosines, sines, lines, members):
    bf16, f32 = jnp.bfloat16, jnp.float32
    half, width = x.shape
    local_tok = 2 * half
    shard, columns = first.shape
    block = ff_blocks.shape[-1]
    q_width = out_t.shape[1]
    count = lines * PLANE
    steps = max(lines - 3, 1)
    anywhere = pl.BlockSpec(memory_space=pl.ANY)
    inside = pl.BlockSpec(memory_space=pltpu.VMEM)
    dma = pltpu.SemaphoreType.DMA
    slab = jax.ShapeDtypeStruct((3, PLANE * shard, block), bf16)
    gather_sems = [dma, dma((2, lines)), dma((2, lines)), dma((PLANE - 1, lines)), dma((PLANE - 1, lines))]
    return pl.pallas_call(
        functools.partial(front_kernel, lines=lines, members=members, steps=steps),
        out_shape=(slab,) * (1 + 2 * steps)
        + (
            jax.ShapeDtypeStruct((width, columns), bf16),
            jax.ShapeDtypeStruct((width, q_width), bf16),
            jax.ShapeDtypeStruct((local_tok, q_width), bf16),
            jax.ShapeDtypeStruct((members * local_tok, 256), bf16),
            jax.ShapeDtypeStruct((local_tok, width), bf16),
            jax.ShapeDtypeStruct((16, width), f32),
        ),
        in_specs=[anywhere] * 5 + [inside] * 2,
        out_specs=(anywhere,) * (1 + 2 * steps) + (anywhere, anywhere, inside, anywhere, inside, inside),
        scratch_shapes=[
            pltpu.VMEM((width, columns), bf16), pltpu.VMEM((16 * count, width), bf16),
            pltpu.VMEM((local_tok, width), bf16), pltpu.VMEM((local_tok, width), bf16),
            pltpu.VMEM((local_tok, 256), bf16),
        ]
        + gather_sems * 3
        + [
            dma((3,)), dma((3, PLANE - 1)), dma((3, PLANE - 1)), dma((3, 2, steps)), dma((3, 2, steps)),
            dma, dma, dma, dma, dma, dma((2 * PLANE - 1,)), dma((2 * PLANE - 1,)),
        ],
        compiler_params=pltpu.CompilerParams(vmem_limit_bytes=56 << 20, collective_id=1, has_side_effects=True),
        name="front",
        cost_estimate=pl.CostEstimate(flops=2 * local_tok * width * columns, bytes_accessed=30 << 20, transcendentals=0),
    )(ff_blocks, first, out_t, extra, x, cosines, sines)


def ff_kernel(
    *refs, tile_h, tile_n, tile_m, lines,
):
    spread = 1 + 2 * (lines - 2)
    x_in, cots, slabs = refs[0], refs[1 : 1 + PLANE], refs[1 + PLANE : 1 + PLANE + spread]
    (
        dx_out, y_out, parts_out, top_out, bottom_out,
        x_all, cot_all, gate_w, up_w, down_w, prod, gate_g, up_g, far, near, back, y_stage,
        x_send, x_recv, fwd_send, fwd_recv, pair_send, pair_recv, dx_send, dx_recv,
        x_load, cot_load, cot_send, cot_recv, weight_sem, hop_send, hop_recv, y_sem, out_sem,
    ) = refs[1 + PLANE + spread :]
    bf16 = jnp.bfloat16
    half = x_in.shape[0]
    width = x_in.shape[1]
    block = gate_w.shape[1]
    chunk = 2 * half
    dp = lax.axis_index("dp")
    core = lax.axis_index("tensor")
    chip = [None] + [{"dp": plane_partner(dp, bits)} for bits in range(1, PLANE)]
    mate = {"tensor": 1 - core}
    rows = lambda k, r, n=1: pl.ds((2 * k + r) * half, n * half)

    z_at = dp // PLANE
    slab_rows = width // lines
    weights = (gate_w, up_w, down_w)
    ways = ((1, 0), (-1, 1))
    place_of = lambda sign: z_at if sign == 1 else lines - 1 - z_at
    place_rows = lambda z: pl.ds(pl.multiple_of(z * slab_rows, slab_rows), slab_rows)

    def weight_loads(which, act):
        for sign, way in ways:
            for step in range(lines - 2):
                piece = 1 + way * (lines - 2) + step

                @pl.when(place_of(sign) >= step + 1)
                def _():
                    act(pltpu.make_async_copy(
                        slabs[piece].at[which], weights[which].at[place_rows(z_at - sign * (step + 1))],
                        weight_sem.at[which, piece]))

        act(pltpu.make_async_copy(slabs[0].at[which], weights[which].at[place_rows(z_at)], weight_sem.at[which, 0]))

    def last_hop(which, sign, way):
        origin = 0 if sign == 1 else lines - 1
        return pltpu.make_async_remote_copy(
            src_ref=slabs[(way + 1) * (lines - 2)].at[which],
            dst_ref=weights[which].at[pl.ds(origin * slab_rows, slab_rows)],
            send_sem=hop_send.at[which, way], recv_sem=hop_recv.at[which, way],
            device_id={"dp": dp + sign * PLANE}, device_id_type=MESH)

    def weight_wait(which):
        weight_loads(which, lambda copy: copy.wait())
        for sign, way in ways:

            @pl.when(place_of(sign) == lines - 1)
            def _():
                last_hop(which, sign, way).wait_recv()

    x_keep = pltpu.make_async_copy(x_in, x_all.at[rows(0, 0)], x_load)
    x_keep.start()

    def cot_keep(k):
        return pltpu.make_async_copy(cots[k], cot_all.at[rows(k, 0)], cot_load.at[k])

    def cot_copy(k):
        return pltpu.make_async_remote_copy(
            src_ref=cots[k], dst_ref=cot_all.at[rows(k, 1)], send_sem=cot_send.at[k], recv_sem=cot_recv.at[k],
            device_id=mate, device_id_type=MESH)

    for k in range(PLANE):
        cot_keep(k).start()
    for which in (2, 0, 1):
        weight_loads(which, lambda copy: copy.start())
    greet(dp, core, lines)
    for which in (2, 0, 1):
        for sign, way in ways:

            @pl.when(place_of(sign) == lines - 2)
            def _():
                last_hop(which, sign, way).start()

    def x_copy(k):
        return pltpu.make_async_remote_copy(
            src_ref=x_in, dst_ref=x_all.at[rows(k, 0) if k else rows(0, 1)],
            send_sem=x_send.at[k], recv_sem=x_recv.at[k],
            device_id=chip[k] if k else mate, device_id_type=MESH)

    def x_forward(k):
        return pltpu.make_async_remote_copy(
            src_ref=x_all.at[rows(k, 0)], dst_ref=x_all.at[rows(k, 1)],
            send_sem=fwd_send.at[k - 1], recv_sem=fwd_recv.at[k - 1],
            device_id=mate, device_id_type=MESH)

    def pair_copy(k):
        return pltpu.make_async_remote_copy(
            src_ref=far.at[k], dst_ref=near.at[k],
            send_sem=pair_send.at[k], recv_sem=pair_recv.at[k],
            device_id=mate, device_id_type=MESH)

    def dx_copy(k):
        return pltpu.make_async_remote_copy(
            src_ref=near.at[k], dst_ref=back.at[k - 1],
            send_sem=dx_send.at[k - 1], recv_sem=dx_recv.at[k - 1],
            device_id=chip[k], device_id_type=MESH)

    x_copy(0).start()
    x_copy(1).start()
    x_copy(2).start()
    for k in range(PLANE):
        cot_copy(k).start()
    for k in range(PLANE):
        cot_keep(k).wait()
        cot_copy(k).wait_recv()
    weight_wait(2)

    @pl.loop(0, PLANE)
    def _(k):
        at = pl.ds(pl.multiple_of(k * chunk, chunk), chunk)

        @pl.loop(0, block // tile_h)
        def _(t):
            cols = pl.ds(pl.multiple_of(t * tile_h, tile_h), tile_h)
            up_g[at, cols] = dot_nn(cot_all[at, :], down_w[:, cols]).astype(bf16)

    def gate_up(k):
        at = rows(k, 0, 2)

        @pl.loop(0, block // tile_h)
        def _(t):
            cols = pl.ds(pl.multiple_of(t * tile_h, tile_h), tile_h)
            gate = dot_nn(x_all[at, :], gate_w[:, cols])
            up = dot_nn(x_all[at, :], up_w[:, cols])
            pg = up_g[at, cols].astype(jnp.float32)
            sig = 0.5 * jnp.tanh(0.5 * gate) + 0.5
            silu = gate * sig
            prod[at, cols] = (silu * up).astype(bf16)
            up_g[at, cols] = (pg * silu).astype(bf16)
            gate_g[at, cols] = (pg * up * (sig + silu * (1.0 - sig))).astype(bf16)

    def dx_half(k, r):
        at = rows(k, r)

        @pl.loop(0, width // tile_n)
        def _(t):
            cols = pl.ds(pl.multiple_of(t * tile_n, tile_n), tile_n)
            part = dot_nt(gate_g[at, :], gate_w[cols, :]) + dot_nt(up_g[at, :], up_w[cols, :])
            if r:
                far[k, :, cols] = part.astype(bf16)
            else:
                near[k, :, cols] = (part + near[k, :, cols].astype(jnp.float32)).astype(bf16)

    def dx_first(k):
        dx_half(k, 1)
        pair_copy(k).start()

    def dx_second(k):
        pair_copy(k).wait_recv()
        dx_half(k, 0)
        if k:
            dx_copy(k).start()

    def y_copies(k, act):
        for r in range(2):
            act(pltpu.make_async_copy(y_stage.at[pl.ds(r * half, half)], y_out.at[r, k], y_sem.at[r]))

    def y_part(k):
        if k:
            y_copies(k - 1, lambda copy: copy.wait())

        @pl.loop(0, width // tile_n)
        def _(t):
            cols = pl.ds(pl.multiple_of(t * tile_n, tile_n), tile_n)
            y_stage[:, cols] = dot_nt(prod[rows(k, 0, 2), :], down_w[cols, :]).astype(bf16)

        y_copies(k, lambda copy: copy.start())

    x_keep.wait()
    weight_wait(0)
    weight_wait(1)
    x_copy(0).wait_recv()
    gate_up(0)
    dx_first(0)
    x_copy(3).start()
    x_copy(1).wait_recv()
    x_forward(1).start()
    x_copy(2).wait_recv()
    x_forward(2).start()
    dx_second(0)
    x_forward(1).wait_recv()
    gate_up(1)
    dx_first(1)
    y_part(0)
    dx_second(1)
    x_forward(2).wait_recv()
    gate_up(2)
    dx_first(2)
    y_part(1)
    x_copy(3).wait_recv()
    x_forward(3).start()
    dx_second(2)
    x_forward(3).wait_recv()
    gate_up(3)
    dx_first(3)
    y_part(2)
    dx_second(3)
    y_part(3)

    def out_copies(which, act):
        for z in range(lines):
            at = pl.ds(z * slab_rows, slab_rows)
            act(pltpu.make_async_copy(weights[which].at[at], parts_out.at[which, z], out_sem.at[which, z]))
        for index, out in ((lines, top_out), (lines + 1, bottom_out)):
            at = pl.ds((lines - 1) * slab_rows if out is top_out else 0, slab_rows)
            act(pltpu.make_async_copy(weights[which].at[at], out.at[which], out_sem.at[which, index]))

    @pl.loop(0, width // tile_m)
    def _(m):
        at = pl.ds(pl.multiple_of(m * tile_m, tile_m), tile_m)
        turned = cot_all[:, at].T
        down_w[at, :] = dot_nn(turned, prod[...]).astype(bf16)

    out_copies(2, lambda copy: copy.start())

    @pl.loop(0, width // tile_m)
    def _(m):
        at = pl.ds(pl.multiple_of(m * tile_m, tile_m), tile_m)
        turned = x_all[:, at].T
        gate_w[at, :] = dot_nn(turned, gate_g[...]).astype(bf16)
        up_w[at, :] = dot_nn(turned, up_g[...]).astype(bf16)

    out_copies(0, lambda copy: copy.start())
    out_copies(1, lambda copy: copy.start())

    for k in range(1, PLANE):
        dx_copy(k).wait_recv()
    total = near[0].astype(jnp.float32)
    for k in range(PLANE - 1):
        total = total + back[k].astype(jnp.float32)
    dx_out[...] = total

    for k in range(PLANE):
        x_copy(k).wait_send()
        pair_copy(k).wait_send()
        if k:
            x_forward(k).wait_send()
            dx_copy(k).wait_send()
    y_copies(PLANE - 1, lambda copy: copy.wait())
    for which in range(3):
        out_copies(which, lambda copy: copy.wait())
        for sign, way in ways:

            @pl.when(place_of(sign) == lines - 2)
            def _():
                last_hop(which, sign, way).wait_send()

    for k in range(PLANE):
        cot_copy(k).wait_send()


def feed_forward(x, cots, slabs, lines, tile_h=384, tile_n=512, tile_m=256):
    half, width = x.shape
    block = slabs[0].shape[-1]
    slab_rows = width // lines
    tokens = 2 * PLANE * half
    bf16 = jnp.bfloat16
    anywhere = pl.BlockSpec(memory_space=pl.ANY)
    dma = pltpu.SemaphoreType.DMA
    slab = jax.ShapeDtypeStruct((3, slab_rows, block), bf16)
    return pl.pallas_call(
        functools.partial(ff_kernel, tile_h=tile_h, tile_n=tile_n, tile_m=tile_m, lines=lines),
        out_shape=(
            jax.ShapeDtypeStruct((half, width), jnp.float32),
            jax.ShapeDtypeStruct((2, PLANE, half, width), bf16),
            jax.ShapeDtypeStruct((3, lines, slab_rows, block), bf16),
            slab,
            slab,
        ),
        in_specs=[anywhere] * (1 + PLANE + len(slabs)),
        out_specs=(pl.BlockSpec(memory_space=pltpu.VMEM),) + (anywhere,) * 4,
        scratch_shapes=[
            pltpu.VMEM((tokens, width), bf16), pltpu.VMEM((tokens, width), bf16),
            pltpu.VMEM((width, block), bf16), pltpu.VMEM((width, block), bf16), pltpu.VMEM((width, block), bf16),
            pltpu.VMEM((tokens, block), bf16), pltpu.VMEM((tokens, block), bf16), pltpu.VMEM((tokens, block), bf16),
            pltpu.VMEM((PLANE, half, width), bf16), pltpu.VMEM((PLANE, half, width), bf16), pltpu.VMEM((PLANE - 1, half, width), bf16),
            pltpu.VMEM((2 * half, width), bf16),
            dma((PLANE,)), dma((PLANE,)), dma((PLANE - 1,)), dma((PLANE - 1,)), dma((PLANE,)), dma((PLANE,)),
            dma((PLANE - 1,)), dma((PLANE - 1,)), dma, dma((PLANE,)), dma((PLANE,)), dma((PLANE,)), dma((3, 2 * lines)), dma((3, 2)), dma((3, 2)), dma((2,)), dma((3, lines + 2)),
        ],
        compiler_params=pltpu.CompilerParams(vmem_limit_bytes=62 << 20, collective_id=0, has_side_effects=True),
        name="feed_forward",
        cost_estimate=pl.CostEstimate(flops=18 * tokens * width * block, bytes_accessed=60 << 20, transcendentals=tokens * block),
    )(x, *cots, *slabs)


def back_kernel(
    dkv_in, dq_in, cos_in, sin_in, normed_in, first_in, out_part, x_in, rows_in, gain_row_in, middle_grad_in,
    ff_in, carried_up, carried_down, y_in,
    input_grad_out, sums_out, small_out, ff_out, y_out,
    kv_own, kv_other, kv_plane, kv_merged, kv_line, grads, part_q, part_kv, own_o,
    recv_q, recv_kv, recv_o, line_q, line_kv, line_o, from_q, from_kv, from_o,
    far, near, small_own, small_mate, small_plane, small_line,
    own_buf, recv_buf, first_buf, total_buf,
    kv_local, kv_send, kv_recv, kv_line_send, kv_line_recv,
    plane_send, plane_recv, line_send, line_recv, own_o_sem,
    mate_send, mate_recv, small_mate_sem, small_plane_send, small_plane_recv, small_line_send, small_line_recv,
    load_sem, own_sem, carry_sem, hop_send, hop_recv, spread_local, spread_send, spread_recv, y_send, y_recv,
    *, lines, members, scale,
):
    bf16, f32 = jnp.bfloat16, jnp.float32
    dp = lax.axis_index("dp")
    core = lax.axis_index("tensor")
    z_at, j_at = dp // PLANE, lax.rem(dp, PLANE)
    half, width = x_in.shape
    local_tok = 2 * half
    slab_rows = width // lines
    shard = slab_rows // PLANE
    q_width = dq_in.shape[1]
    block = total_buf.shape[-1]
    mate = {"tensor": 1 - core}
    chip = [None] + [{"dp": plane_partner(dp, bits)} for bits in range(1, PLANE)]
    there = [j_at] + [lax.rem(plane_partner(dp, bits), PLANE) for bits in range(1, PLANE)]
    side = lax.rem(z_at, 2) * PLANE
    other_side = PLANE - side
    member = lax.rem(dp, members)
    del member
    ways = ((1, 0), (-1, 1))
    place_of = lambda sign: z_at if sign == 1 else lines - 1 - z_at
    tree_rows = lambda m: pl.ds(pl.multiple_of(m * local_tok, local_tok), local_tok)

    kv_loads = [
        pltpu.make_async_copy(dkv_in.at[tree_rows(side + j_at)], kv_own, kv_local.at[0]),
        pltpu.make_async_copy(dkv_in.at[tree_rows(other_side + j_at)], kv_other, kv_local.at[1]),
    ]
    for load in kv_loads:
        load.start()
    o_load = pltpu.make_async_copy(out_part.at[:, j_at], own_o, own_o_sem)
    o_load.start()

    def slab_load(which, sign, way, step):
        target = lines - 1 - step + place_of(sign)
        slab = target if sign == 1 else lines - 1 - target
        return pltpu.make_async_copy(ff_in.at[which, slab], own_buf.at[which, way], load_sem.at[which, way])

    def own_load(which):
        return pltpu.make_async_copy(ff_in.at[which, z_at], total_buf.at[which], own_sem.at[which])

    def carry_load(which, sign, way):
        return pltpu.make_async_copy(
            (carried_up if sign == 1 else carried_down).at[which], first_buf.at[which, way], carry_sem.at[which, way])

    order = (2, 0, 1)
    for which in order:
        for sign, way in ways:
            carry_load(which, sign, way).start()

            @pl.when(place_of(sign) == 1)
            def _():
                slab_load(which, sign, way, 1).start()

        own_load(which).start()

    barrier = pltpu.get_barrier_semaphore()
    for bits in range(1, PLANE):
        pl.semaphore_signal(barrier, inc=1, device_id=chip[bits], device_id_type=MESH)
    pl.semaphore_signal(barrier, inc=1, device_id=mate, device_id_type=MESH)
    for apart in range(1, lines):
        pl.semaphore_signal(
            barrier, inc=1, device_id={"dp": lax.rem(z_at + apart, lines) * PLANE + j_at}, device_id_type=MESH)
    pl.semaphore_wait(barrier, PLANE + lines - 1)

    def kv_copy(bits, part):
        at = tree_rows((side if part == 0 else other_side) + there[bits])
        return pltpu.make_async_remote_copy(
            src_ref=dkv_in.at[at], dst_ref=kv_plane.at[bits - 1, part],
            send_sem=kv_send.at[bits - 1, part], recv_sem=kv_recv.at[bits - 1, part],
            device_id=chip[bits], device_id_type=MESH)

    for part in (1, 0):
        for bits in range(1, PLANE):
            kv_copy(bits, part).start()

    def hop(which, sign, way, step, first_place=False):
        slab = lines - 1 - step if sign == 1 else step
        carried = first_buf.at[which, way] if step == 1 else recv_buf.at[which, way, step - 2]
        return pltpu.make_async_remote_copy(
            src_ref=ff_in.at[which, slab] if first_place else carried, dst_ref=recv_buf.at[which, way, step - 1],
            send_sem=hop_send.at[which, way, step - 1], recv_sem=hop_recv.at[which, way, step - 1],
            device_id={"dp": dp + sign * PLANE}, device_id_type=MESH)

    def hop_step(which, step):
        for sign, way in ways:
            place = place_of(sign)
            if step == 1:
                carry_load(which, sign, way).wait()

            @pl.when(place == 0)
            def _():
                hop(which, sign, way, step, True).start()

            @pl.when((place >= 1) & (place <= step))
            def _():
                if step > 1:
                    hop(which, sign, way, step - 1).wait_recv()
                slab_load(which, sign, way, step).wait()
                mine = own_buf[which, way].astype(f32)
                if step == 1:
                    first_buf[which, way] = (mine + first_buf[which, way].astype(f32)).astype(bf16)
                else:
                    recv_buf[which, way, step - 2] = (mine + recv_buf[which, way, step - 2].astype(f32)).astype(bf16)
                hop(which, sign, way, step).start()

            if step < lines - 2:

                @pl.when((place >= 1) & (place <= step + 1))
                def _():
                    slab_load(which, sign, way, step + 1).start()

    for which in order:
        hop_step(which, 1)

    groups = {
        "o": (0, out_part, own_o, recv_o, line_o, from_o, q_width + 256, q_width),
        "q": (1, part_q, None, recv_q, line_q, from_q, 0, q_width),
        "kv": (2, part_kv, None, recv_kv, line_kv, from_kv, q_width, 256),
    }

    def plane_copy(name, bits):
        index, part, _, recv, *_ = groups[name]
        return pltpu.make_async_remote_copy(
            src_ref=part.at[:, there[bits]], dst_ref=recv.at[bits - 1],
            send_sem=plane_send.at[index, bits - 1], recv_sem=plane_recv.at[index, bits - 1],
            device_id=chip[bits], device_id_type=MESH)

    def line_copy(name, apart):
        index, _, _, _, line, came, *_ = groups[name]
        target = lax.rem(z_at + apart, lines)
        return pltpu.make_async_remote_copy(
            src_ref=line.at[target], dst_ref=came.at[apart - 1],
            send_sem=line_send.at[index, apart - 1], recv_sem=line_recv.at[index, apart - 1],
            device_id={"dp": target * PLANE + j_at}, device_id_type=MESH)

    def plane_start(name):
        for bits in range(1, PLANE):
            plane_copy(name, bits).start()

    def plane_sum(name):
        _, part, own, recv, line, *_ = groups[name]
        for bits in range(1, PLANE):
            plane_copy(name, bits).wait_recv()
        for z in range(lines):
            total = (part[z, j_at] if own is None else own[z]).astype(f32)
            for bits in range(1, PLANE):
                total = total + recv[bits - 1, z].astype(f32)
            line[z] = total.astype(bf16)
        for apart in range(1, lines):
            line_copy(name, apart).start()

    def line_sum(name):
        *_, line, came, at, size = groups[name]
        for apart in range(1, lines):
            line_copy(name, apart).wait_recv()
        total = line[z_at].astype(f32)
        for apart in range(1, lines):
            total = total + came[apart - 1].astype(f32)
        sums_out[:, at : at + size] = total

    plane_start("o")
    cosines, sines = cos_in[...], sin_in[...]

    def turned_back(part):
        return (part * cosines - pltpu.roll(part, 64, 1) * sines).astype(bf16)

    for at in range(0, q_width, 128):
        grads[:, at : at + 128] = turned_back(dq_in[:, at : at + 128])

    def y_copy(bits):
        return pltpu.make_async_remote_copy(
            src_ref=y_in.at[bits], dst_ref=y_out.at[bits - 1], send_sem=y_send.at[bits - 1], recv_sem=y_recv.at[bits - 1],
            device_id=chip[bits], device_id_type=MESH)

    def weight_part(part, at, size):
        for z in range(lines):
            turned = normed_in[:, z * slab_rows : (z + 1) * slab_rows].T
            tile = dot_nn(turned, grads[:, at : at + size]).astype(bf16)
            for j in range(PLANE):
                part[z, j] = tile[j * shard : (j + 1) * shard]

    weight_part(part_q, 0, q_width)
    plane_start("q")

    for load in kv_loads:
        load.wait()
    for bits in range(1, PLANE):
        kv_copy(bits, 1).wait_recv()
    total = kv_other[...].astype(f32)
    for bits in range(1, PLANE):
        total = total + kv_plane[bits - 1, 1].astype(f32)
    kv_merged[...] = total.astype(bf16)
    kv_across = pltpu.make_async_remote_copy(
        src_ref=kv_merged, dst_ref=kv_line, send_sem=kv_line_send, recv_sem=kv_line_recv,
        device_id={"dp": line_partner(dp)}, device_id_type=MESH)
    kv_across.start()
    for step in range(2, lines - 1):
        hop_step(order[0], step)
    for bits in range(1, PLANE):
        kv_copy(bits, 0).wait_recv()
    kv_across.wait_recv()
    total = kv_own[...].astype(f32) + kv_line[...].astype(f32)
    for bits in range(1, PLANE):
        total = total + kv_plane[bits - 1, 0].astype(f32)
    grads[:, q_width : q_width + 128] = turned_back(total[:, 0:128] * scale)
    grads[:, q_width + 128 :] = total[:, 128:256].astype(bf16)
    weight_part(part_kv, q_width, 256)
    plane_start("kv")
    for bits in range(1, PLANE):
        y_copy(bits).start()

    def normed_grad(c):
        at = pl.ds(pl.multiple_of(c * half, half), half)
        return dot_nt(grads[at, :], first_in[...])

    far[...] = normed_grad(1 - core).astype(bf16)
    mate_copy = pltpu.make_async_remote_copy(
        src_ref=far, dst_ref=near, send_sem=mate_send, recv_sem=mate_recv, device_id=mate, device_id_type=MESH)
    mate_copy.start()
    mine = normed_grad(core)
    o_load.wait()
    plane_sum("o")
    mate_copy.wait_recv()
    mine = mine + near[...].astype(f32)
    wide = x_in[...].astype(f32)
    norm = lax.rsqrt(jnp.mean(wide * wide, axis=1, keepdims=True) + EPS)
    z_own = wide * norm
    w = mine * gain_row_in[...]
    back = norm * (w - z_own * jnp.mean(w * z_own, axis=1, keepdims=True))
    input_grad_out[...] = (middle_grad_in[...] + back).astype(bf16)
    bias = jnp.sum(grads[...].astype(f32), axis=0, keepdims=True)
    small_own[...] = jnp.concatenate(
        [
            jnp.sum(mine * z_own, axis=0, keepdims=True),
            rows_in[...],
            jnp.concatenate([bias, jnp.zeros((1, width - q_width - 256), f32)], axis=1),
            jnp.zeros((5, width), f32),
        ],
        axis=0,
    )
    small_copy = pltpu.make_async_remote_copy(
        src_ref=small_own, dst_ref=small_mate, send_sem=small_mate_sem.at[0], recv_sem=small_mate_sem.at[1],
        device_id=mate, device_id_type=MESH)
    small_copy.start()
    for step in range(2, lines - 1):
        hop_step(order[1], step)
    plane_sum("q")
    for step in range(2, lines - 1):
        hop_step(order[2], step)
    plane_sum("kv")

    small_copy.wait_recv()
    gain_rows = lax.broadcasted_iota(jnp.int32, (8, width), 0) < 2
    small_plane[0] = small_own[...] + jnp.where(gain_rows, small_mate[...], 0.0)

    def small_plane_copy(bits):
        return pltpu.make_async_remote_copy(
            src_ref=small_plane.at[0], dst_ref=small_plane.at[bits],
            send_sem=small_plane_send.at[bits - 1], recv_sem=small_plane_recv.at[bits - 1],
            device_id=chip[bits], device_id_type=MESH)

    def small_line_copy(apart):
        return pltpu.make_async_remote_copy(
            src_ref=small_line.at[0], dst_ref=small_line.at[apart],
            send_sem=small_line_send.at[apart - 1], recv_sem=small_line_recv.at[apart - 1],
            device_id={"dp": lax.rem(z_at + apart, lines) * PLANE + j_at}, device_id_type=MESH)

    for bits in range(1, PLANE):
        small_plane_copy(bits).start()
    for bits in range(1, PLANE):
        small_plane_copy(bits).wait_recv()
    total = small_plane[0]
    for bits in range(1, PLANE):
        total = total + small_plane[bits]
    small_line[0] = total
    for apart in range(1, lines):
        small_line_copy(apart).start()
    line_sum("o")
    line_sum("q")
    line_sum("kv")
    for apart in range(1, lines):
        small_line_copy(apart).wait_recv()
    total = small_line[0]
    for apart in range(1, lines):
        total = total + small_line[apart]
    small_out[...] = total

    columns = lambda j: pl.ds(pl.multiple_of(j * block, block), block)

    def spread(which, bits):
        rows = pl.ds(pl.multiple_of(there[bits] * shard, shard), shard)
        return pltpu.make_async_remote_copy(
            src_ref=total_buf.at[which, rows], dst_ref=ff_out.at[which, :, columns(j_at)],
            send_sem=spread_send.at[which, bits - 1], recv_sem=spread_recv.at[which, bits - 1],
            device_id=chip[bits], device_id_type=MESH)

    def spread_keep(which):
        rows = pl.ds(pl.multiple_of(j_at * shard, shard), shard)
        return pltpu.make_async_copy(
            total_buf.at[which, rows], ff_out.at[which, :, columns(j_at)], spread_local.at[which])

    for which in order:
        own_load(which).wait()
        for sign, way in ways:

            @pl.when(place_of(sign) >= 1)
            def _():
                hop(which, sign, way, lines - 2).wait_recv()
                came = recv_buf[which, way, lines - 3].astype(f32)
                total_buf[which] = (total_buf[which].astype(f32) + came).astype(bf16)

        for bits in range(1, PLANE):
            spread(which, bits).start()
        spread_keep(which).start()

    for which in order:
        for bits in range(1, PLANE):
            spread(which, bits).wait_recv()
            spread(which, bits).wait_send()
        spread_keep(which).wait()
        for sign, way in ways:
            for step in range(1, lines - 1):

                @pl.when(place_of(sign) <= step)
                def _():
                    hop(which, sign, way, step).wait_send()

    for bits in range(1, PLANE):
        y_copy(bits).wait_recv()
        y_copy(bits).wait_send()
        small_plane_copy(bits).wait_send()
        for part in range(2):
            kv_copy(bits, part).wait_send()
        for name in groups:
            plane_copy(name, bits).wait_send()
    for apart in range(1, lines):
        small_line_copy(apart).wait_send()
        for name in groups:
            line_copy(name, apart).wait_send()
    kv_across.wait_send()
    mate_copy.wait_send()
    small_copy.wait_send()


def finish(dkv, dq, cosines, sines, normed, first, out_part, x, gain_rows, gain_row, middle_grad, ff_parts, up, down, y_parts, lines, members, scale):
    bf16, f32 = jnp.bfloat16, jnp.float32
    half, width = x.shape
    local_tok = 2 * half
    q_width = dq.shape[1]
    slab_rows = width // lines
    shard = slab_rows // PLANE
    block = ff_parts.shape[-1]
    anywhere = pl.BlockSpec(memory_space=pl.ANY)
    inside = pl.BlockSpec(memory_space=pltpu.VMEM)
    dma = pltpu.SemaphoreType.DMA
    near = PLANE - 1
    vmem = lambda *shape: pltpu.VMEM(shape, bf16)
    wide = lambda *shape: pltpu.VMEM(shape, f32)
    pair = (local_tok, 256)
    return pl.pallas_call(
        functools.partial(back_kernel, lines=lines, members=members, scale=scale),
        out_shape=(
            jax.ShapeDtypeStruct((half, width), bf16),
            jax.ShapeDtypeStruct((shard, 2 * q_width + 256), f32),
            jax.ShapeDtypeStruct((8, width), f32),
            jax.ShapeDtypeStruct((3, shard, PLANE * block), bf16),
            jax.ShapeDtypeStruct((PLANE - 1, half, width), bf16),
        ),
        in_specs=[anywhere] + [inside] * 5 + [anywhere] + [inside] * 4 + [anywhere] * 4,
        out_specs=(inside, inside, inside, anywhere, anywhere),
        scratch_shapes=[
            vmem(*pair), vmem(*pair), vmem(near, 2, *pair), vmem(*pair), vmem(*pair),
            vmem(local_tok, q_width + 256), vmem(lines, PLANE, shard, q_width), vmem(lines, PLANE, shard, 256), vmem(lines, shard, q_width),
            vmem(near, lines, shard, q_width), vmem(near, lines, shard, 256), vmem(near, lines, shard, q_width),
            vmem(lines, shard, q_width), vmem(lines, shard, 256), vmem(lines, shard, q_width),
            vmem(lines - 1, shard, q_width), vmem(lines - 1, shard, 256), vmem(lines - 1, shard, q_width),
            vmem(half, width), vmem(half, width), wide(8, width), wide(8, width), wide(PLANE, 8, width), wide(lines, 8, width),
            vmem(3, 2, slab_rows, block), vmem(3, 2, lines - 2, slab_rows, block), vmem(3, 2, slab_rows, block), vmem(3, slab_rows, block),
            dma((2,)), dma((near, 2)), dma((near, 2)), dma, dma,
            dma((3, near)), dma((3, near)), dma((3, lines - 1)), dma((3, lines - 1)), dma,
            dma, dma, dma((2,)), dma((near,)), dma((near,)), dma((lines - 1,)), dma((lines - 1,)),
            dma((3, 2)), dma((3,)), dma((3, 2)), dma((3, 2, lines - 2)), dma((3, 2, lines - 2)), dma((3,)), dma((3, near)), dma((3, near)), dma((near,)), dma((near,)),
        ],
        compiler_params=pltpu.CompilerParams(vmem_limit_bytes=62 << 20, collective_id=2, has_side_effects=True),
        name="back",
        cost_estimate=pl.CostEstimate(flops=6 * local_tok * width * (q_width + 256), bytes_accessed=40 << 20, transcendentals=0),
    )(dkv, dq, cosines, sines, normed, first, out_part, x, gain_rows, gain_row, middle_grad, ff_parts, up, down, y_parts)


def swap(block, axis, count, bits):
    return lax.ppermute(block, axis, [(i, i ^ bits) for i in range(count)])


def rms_scale(values):
    return lax.rsqrt(jnp.mean(values * values, axis=1, keepdims=True) + EPS)


def norm_back(grad, values, gain):
    scale = rms_scale(values)
    z = values * scale
    w = grad * gain
    gain_grad = jnp.sum(grad * z, axis=0)
    return scale * (w - z * jnp.mean(w * z, axis=1, keepdims=True)), gain_grad


def rope_tables(positions):
    exponents = jnp.arange(64, dtype=jnp.float32) * (2.0 / 128)
    frequency = jnp.power(THETA, -exponents)
    angles = positions.astype(jnp.float32)[:, None] * frequency[None, :]
    cosines, sines = jnp.cos(angles), jnp.sin(angles)
    return (
        jnp.concatenate([cosines, cosines], axis=1),
        jnp.concatenate([-sines, sines], axis=1),
    )


def contract_rows(left, right):
    return lax.dot_general(
        left, right, (((0,), (0,)), ((), ())), preferred_element_type=jnp.float32
    )


def contract_cols(left, right):
    return lax.dot_general(
        left, right, (((1,), (1,)), ((), ())), preferred_element_type=jnp.float32
    )


def matmul(left, right):
    return jnp.dot(left, right, preferred_element_type=jnp.float32)


def attention_plan(segment_ids, parent_ids, dp_index, local_tok):
    members = TREE_TOK // local_tok
    first = dp_index // members * TREE_TOK
    slots = lax.dynamic_slice_in_dim(segment_ids, first, TREE_TOK)[::KB]
    numbers = jnp.arange(parent_ids.shape[0], dtype=jnp.int32)
    parents = jnp.sum(jnp.where(slots[:, None] == numbers[None, :], parent_ids[None, :], 0), axis=1)
    places = jnp.arange(slots.shape[0], dtype=jnp.int32)
    holder = jnp.sum(jnp.where(parents[:, None] == slots[None, :], places[None, :], 0), axis=1)
    starts = dp_index % members * local_tok + QB * jnp.arange(local_tok // QB, dtype=jnp.int32)
    slot = starts // KB
    chosen = slot[:, None] == places[None, :]
    pick = lambda table: jnp.sum(jnp.where(chosen, table[None, :], 0), axis=1)
    in_trunk = starts < TRUNK
    is_leaf = pick(parents) != slots[0]
    chunk = jnp.minimum(starts, TRUNK) // KC
    far = jnp.int32(1 << 20)
    block0 = jnp.where(in_trunk, 2 * chunk, jnp.where(is_leaf, pick(holder), TRUNK // KB))
    block1 = jnp.where(in_trunk, 2 * chunk + 1, slot)
    shift0 = jnp.where(in_trunk, block0 * KB - starts, jnp.where(is_leaf, -far, far))
    shift1 = block1 * KB - starts
    zero = jnp.zeros_like(chunk)
    return jnp.stack([chunk, block0, block1, shift0, shift1, zero, zero, zero], axis=1).reshape(-1)


def on_device(
    dp_size,
    layer_input,
    out_cotangent,
    positions,
    segment_ids,
    parent_ids,
    attention_gain,
    query_weight,
    query_bias,
    key_weight,
    key_bias,
    value_weight,
    value_bias,
    output_weight,
    feedforward_gain,
    gate_weight,
    up_weight,
    down_weight,
):
    bf16, f32 = jnp.bfloat16, jnp.float32
    local_tok = positions.shape[0]
    half_tok, width = layer_input.shape
    shard = attention_gain.shape[0]
    heads, head_dim = query_bias.shape[0], 128
    per_head = query_bias.shape[1]
    q_width = heads * head_dim
    hidden = gate_weight.shape[1]
    block = -(-hidden // (PLANE * 128)) * 128
    lines = dp_size // PLANE
    members = TREE_TOK // local_tok
    dp_index = lax.axis_index("dp")
    core = lax.axis_index("tensor")
    scale = head_dim ** (-0.5)

    def line_route(sign, first, last):
        route = []
        for place in range(first, last + 1):
            z = place if sign == 1 else lines - 1 - place
            route += [(z * PLANE + j, (z + sign) * PLANE + j) for j in range(PLANE)]
        return route

    def by_core(mine):
        other = swap(mine, "tensor", 2, 1)
        first = jnp.where(core == 0, mine, other)
        second = jnp.where(core == 0, other, mine)
        return jnp.concatenate([first, second], axis=0)

    def to_tokens(values):
        halves = values.reshape(2, half_tok, width)
        mine = lax.dynamic_index_in_dim(halves, core, 0, keepdims=False)
        theirs = lax.dynamic_index_in_dim(halves, 1 - core, 0, keepdims=False)
        return mine + swap(theirs.astype(bf16), "tensor", 2, 1).astype(f32)

    blocked = lambda w: jnp.pad(w, ((0, 0), (0, PLANE * block - hidden))).reshape(shard, PLANE, block).transpose(1, 0, 2)
    ff_blocks = jnp.stack([blocked(gate_weight), blocked(up_weight), blocked(down_weight.T)])
    first_own = jnp.concatenate([query_weight, key_weight, value_weight], axis=1)
    biases = jnp.concatenate([query_bias, key_bias, value_bias], axis=0)
    bias_row = lax.dynamic_update_slice(
        jnp.zeros((heads + 2, head_dim), bf16), biases, (0, dp_index * per_head)
    ).reshape(1, -1)
    gains = lax.dynamic_update_slice(
        jnp.zeros((2, width), bf16), jnp.stack([attention_gain, feedforward_gain]), (0, dp_index * shard)
    )
    extra = jnp.concatenate(
        [gains, jnp.pad(bias_row, ((0, 0), (0, width - bias_row.shape[1]))), jnp.zeros((13, width), bf16)], axis=0
    )
    cosines, sines = rope_tables(positions)
    plan = attention_plan(segment_ids, parent_ids, dp_index, local_tok)
    steps = lines - 3
    outs = front(ff_blocks, first_own, output_weight.T, extra, layer_input, cosines, sines, lines, members)
    slab, ups, downs = outs[0], list(outs[1 : 1 + steps]), list(outs[1 + steps : 1 + 2 * steps])
    first_all, out_t, q_rot, tree, normed, rows = outs[1 + 2 * steps :]
    gain_one, gain_two = rows[0:1], rows[1:2]

    ups.append(lax.ppermute(ups[-1], "dp", line_route(1, lines - 3, lines - 2)))
    downs.append(lax.ppermute(downs[-1], "dp", line_route(-1, lines - 3, lines - 2)))
    cot_late = lax.optimization_barrier((out_cotangent, rows))[0]
    cots = [out_cotangent] + [swap(cot_late, "dp", dp_size, bits) for bits in range(1, PLANE)]
    attended, lse = attn_fwd(plan, q_rot, tree, scale)
    input_wide = layer_input.astype(f32)
    middle = input_wide + to_tokens(contract_cols(attended, out_t))
    normed_two = (middle * rms_scale(middle) * gain_two).astype(bf16)

    normed_two_grad, y_parts, ff_parts, top, bottom = feed_forward(
        normed_two, cots, [slab] + ups + downs, lines
    )
    up_first = lax.ppermute(top, "dp", line_route(1, 0, 0))
    down_first = lax.ppermute(bottom, "dp", line_route(-1, 0, 0))
    norm_grad, gain_two_grad = norm_back(normed_two_grad, middle, gain_two)
    middle_grad = out_cotangent.astype(f32) + norm_grad

    branch_grad = by_core(middle_grad.astype(bf16))
    out_part = contract_rows(branch_grad, attended).astype(bf16).reshape(lines, PLANE, shard, q_width)
    attended_grad = matmul(branch_grad, out_t).astype(bf16)
    dq, dtree = attn_bwd(plan, q_rot, attended_grad, attended, lse, tree, scale)
    y_other = lax.optimization_barrier((swap(y_parts[1], "tensor", 2, 1), dq))[0]
    y_sums = y_parts[0].astype(f32) + y_other.astype(f32)
    y_low, dq = lax.optimization_barrier((y_sums.astype(bf16), dq))

    input_grad, sums, small, ff_sums, y_came = finish(
        dtree, dq, cosines, sines, normed, first_all, out_part, layer_input, gain_two_grad[None], gain_one,
        middle_grad, ff_parts, up_first, down_first, y_low, lines, members, scale,
    )
    layer_output = (middle + y_sums[0] + jnp.sum(y_came.astype(f32), axis=0)).astype(bf16)
    ff_sums = ff_sums[:, :, :hidden].astype(f32)
    gains_out = lax.dynamic_slice(small[0:2], (0, dp_index * shard), (2, shard))
    bias_out = lax.dynamic_slice(
        small[2, : (heads + 2) * head_dim].reshape(heads + 2, head_dim), (0, dp_index * per_head), (heads + 2, per_head)
    )
    return (
        layer_output,
        input_grad,
        gains_out[0],
        sums[:, :q_width],
        bias_out[:heads],
        sums[:, q_width : q_width + 128],
        bias_out[heads : heads + 1],
        sums[:, q_width + 128 : q_width + 256],
        bias_out[heads + 1 :],
        sums[:, q_width + 256 :].T,
        gains_out[1],
        ff_sums[0],
        ff_sums[1],
        ff_sums[2].T,
    )


def solution(mesh):
    placed = (
        P(("dp", "tensor"), None),
        P(("dp", "tensor"), None),
        P("dp"),
        P(),
        P(),
        P("dp"),
        P("dp", "tensor"),
        P("tensor", "dp"),
        P("dp", "tensor"),
        P("tensor", "dp"),
        P("dp", "tensor"),
        P("tensor", "dp"),
        P("tensor", "dp"),
        P("dp"),
        P("dp", "tensor"),
        P("dp", "tensor"),
        P("tensor", "dp"),
    )
    return jax.shard_map(
        functools.partial(on_device, mesh.shape["dp"]),
        mesh=mesh,
        in_specs=placed,
        out_specs=(
            P(("dp", "tensor"), None),
            P(("dp", "tensor"), None),
            P("dp"),
            P("dp", "tensor"),
            P("tensor", "dp"),
            P("dp", "tensor"),
            P("tensor", "dp"),
            P("dp", "tensor"),
            P("tensor", "dp"),
            P("tensor", "dp"),
            P("dp"),
            P("dp", "tensor"),
            P("dp", "tensor"),
            P("tensor", "dp"),
        ),
        check_vma=False,
    )
```

time: 1150 us -> 692 us (0.60)
  Pallas kernels: 23.5 us -> 528 us
  waiting for transfers between devices: 562 us -> 61.4 us
  matrix products: 164 us -> 9.04 us
  starting transfers between devices: 164 us -> 27.1 us
  local copies, waits for them, and re-layouts: 137 us -> 23.8 us
  other arithmetic: 73.3 us -> 35.7 us
  between operations: 15.8 us -> 1.21 us
    pallas_call x0 -> x3, Pallas kernels: none -> 505 us  [the longest x1 191 us: finish(): pl.pallas_call(functools.partial(back_kernel, lines=lines, members=member...]
    ppermute x53 -> x6, waiting for transfers between devices: 244 us -> 37.1 us  [swap(): return lax.ppermute(block, axis, [(i, i ^ bits) for i in range(count)])]
    unnamed x9 -> x0, waiting for transfers between devices: 175 us -> none
    ppermute x53 -> x6, starting transfers between devices: 114 us -> 18.5 us  [swap(): return lax.ppermute(block, axis, [(i, i ^ bits) for i in range(count)])]
    ppermute x18 -> x4, waiting for transfers between devices: 90.6 us -> 24.2 us  [the longest x1 24.2 us: on_device(): up_first = lax.ppermute(top, 'dp', line_route(1, 0, 0))]
    dot_general x5 -> x1, matrix products: 66.3 us -> 2.63 us  [matmul(): return jnp.dot(left, right, preferred_element_type=jnp.float32)]
    all_gather x5 -> x0, waiting for transfers between devices: 52.8 us -> none  [the longest x3 52.8 us: spread(): lax.all_gather(result, 'dp', axis=0, tiled=True, axis_index_groups=line_g...]
    dot_general x5 -> x1, matrix products: 50.1 us -> 2.92 us  [contract_cols(): lax.dot_general(left, right, (((1,), (1,)), ((), ())), preferred_element_...]
  transfers between devices with their start and end apart: 78 -> 10, of which waited for: 33 -> 3; matrix products, arithmetic and copies ran while one was open for 22% -> 4% of each run, Pallas kernels for 1% -> 3%
where the time goes in v2:
time: 692 us; the launch traced here: 686 us
  Pallas kernels  528 us (76%)
  waiting for transfers between devices  61.4 us (9%)
  other arithmetic  35.7 us (5%)
  starting transfers between devices  27.1 us (4%)
  local copies, waits for them, and re-layouts  23.8 us (3%)
  matrix products  9.04 us (1%)
    pallas_call x1, Pallas kernels, finish(): pl.pallas_call(functools.partial(back_kernel, lines=lines, members=member...  191 us
    pallas_call x1, Pallas kernels, feed_forward(): pl.pallas_call(functools.partial(ff_kernel, tile_h=tile_h, tile_n=tile_n,...  171 us
    pallas_call x1, Pallas kernels, front(): pl.pallas_call(functools.partial(front_kernel, lines=lines, members=membe...  143 us
    ppermute x6, waiting for transfers between devices, swap(): return lax.ppermute(block, axis, [(i, i ^ bits) for i in range(count)])  37.1 us
    ppermute x1, waiting for transfers between devices, on_device(): up_first = lax.ppermute(top, 'dp', line_route(1, 0, 0))  24.2 us
    ppermute x6, starting transfers between devices, swap(): return lax.ppermute(block, axis, [(i, i ^ bits) for i in range(count)])  18.5 us
  transfers between devices with their start and end apart: 10, of which 3 were waited for; matrix products, arithmetic and copies ran while one was open for 4% of the time, Pallas kernels for 3%

profile of v2, /device:TPU:0, one launch (start us, length us, event | category | flops | bytes accessed | tf_op | source)
XLA Modules:
  0.0 685.8 jit_solution(4080932639368400587)
XLA Ops:
  9.9 3.0 pad_maximum_fusion.refs_0_
  14.0 142.5 %front.1 = (bf16[3,384,1152]{2,1,0:T(8,128)(2,1)}, bf16[3,384,1152]{2,1,0:T(8,128)(2,1)}, bf16[3,384,1152]{2,1,0:T(8,128)(2,1)}, bf16[1536,1024]{1,0:T(8,128)(2,...) custom-call(bf16[3,4,96,1152]{3,2,1,0:T(8,128)(2,1)} %pad_maximum_fu, ...), custom_call_target="tpu_custom_call" | custom-call | flops 2013265920 | bytes 31457280 | tf_op jit(solution)/shard_map/front/pallas_call | solution.py:469
  156.6 2.2 collective-permute-start.4
  162.1 9.6 %attention_forward.1 = (bf16[640,768]{1,0:T(8,128)(2,1)}, f32[5,8,768]{2,1,0:T(8,128)}) custom-call(s32[40]{0:T(128)} %reshape.248.info, bf16[640,768]{1,0:T(8,128)(2,1)} %get-tuple-element.41.q_ref, bf16[5120,256]{1,0:T(8,128)(2,1)} %get-tuple-element.42.t_ref), custom_call_target="tpu_custom_call" | custom-call | flops 4529848320 | bytes 6291456 | tf_op jit(solution)/shard_map/attention_forward/pallas_call | solution.py:68
  171.7 2.9 fusion.23
  176.7 16.7 %collective-permute-start.3 = (bf16[320,1536]{1,0:T(8,128)(2,1)}, bf16[320,1536]{1,0:T(8,128)(2,1)}, u32[]{:S(2)}, u32[]{:S(2)}) collective-permute-start(bf16[320,1536]{1,0:T(8,128)(2,1)} %refs_1_.1), channel_id=1, source_target_pairs={{0,6},{2,4},{4,2},{6,0},{8,14},{10,12},{12,10},{14,8},{16,22},{18,... | collective-permute-start | bytes 2949128 | tf_op jit(solution)/shard_map/ppermute | solution.py:1194
  196.5 2.3 multiply_reduce_fusion.2
  200.0 16.4 %collective-permute-done.3.refs_4_ = bf16[320,1536]{1,0:T(8,128)(2,1)} collective-permute-done((bf16[320,1536]{1,0:T(8,128)(2,1)}, bf16[320,1536]{1,0:T(8,128)(2,1)}, u32[]{:S(2)}, u32[]{:S(2)}) %collective-permute-start.3) | collective-permute-done | bytes 983072 | tf_op jit(solution)/shard_map/ppermute | solution.py:1194
  216.4 20.8 %collective-permute-done.2.refs_3_ = bf16[320,1536]{1,0:T(8,128)(2,1)} collective-permute-done((bf16[320,1536]{1,0:T(8,128)(2,1)}, bf16[320,1536]{1,0:T(8,128)(2,1)}, u32[]{:S(2)}, u32[]{:S(2)}) %collective-permute-start.2) | collective-permute-done | bytes 983072 | tf_op jit(solution)/shard_map/ppermute | solution.py:1194
  237.1 170.7 %feed_forward.1 = (f32[320,1536]{1,0:T(8,128)}, bf16[2,4,320,1536]{3,2,1,0:T(8,128)(2,1)}, bf16[3,4,384,1152]{3,2,1,0:T(8,128)(2,1)}, bf16[3,384,1152]{2,1,0:T(8,128)(2,1)}, bf16[3,384,1152]{2,1,0:T(8,128)(2,1)}) custom-call(bf16[320,1536]{1,0:T(8,128)(2,1)} %multiply_convert_fusion.refs_0_, bf16[320,1536]{1,0:T(8,128)(2,1)} %refs_1_.1, ...), custom_call_target="tpu_custom_call" | custom-call | flops 81537269760 | bytes 62914560 | tf_op jit(solution)/shard_map/feed_forward/pallas_call | solution.py:766
  407.8 2.1 multiply_reduce_fusion
  409.9 4.4 slice_bitcast_fusion
  415.5 3.1 fusion.18
  419.2 2.7 collective-permute-start.8
  421.9 2.2 collective-permute-start.9
  425.5 3.5 convolution_convert_fusion
  429.0 2.6 convolution_convert_fusion.1.do_ref
  431.6 13.5 %attention_backward.1 = (f32[640,768]{1,0:T(8,128)}, bf16[5120,256]{1,0:T(8,128)(2,1)}) custom-call(s32[40]{0:T(128)} %reshape.248.info, bf16[640,768]{1,0:T(8,128)(2,1)} %get-tuple-element.41.q_ref, bf16[640,768]{1,0:T(8,128)(2,1)} %convolution_convert_fusion.1.do_ref, bf16[640,768]{1,0:T(8,128)(2,1)} %get-tuple-element.43.o_ref, ...), custom_call_target="tpu_custom_call" | custom-call | flops 11324620800 | bytes 12582912 | tf_op jit(solution)/shard_map/attention_backward/pallas_call | solution.py:132
  445.1 9.2 %convert_add_fusion = (f32[4,320,1536]{2,1,0:T(8,128)}, bf16[4,320,1536]{2,1,0:T(8,128)(2,1)}) fusion(bf16[4,320,1536]{2,1,0:T(8,128)(2,1)} %collective-permute-done.6, bf16[2,4,320,1536]{3,2,1,0:T(8,128)(2,1)} %get-tuple-element.50), kind=kLoop, calls=%fused_computation | loop fusion | flops 7864320 | bytes 19660800 | tf_op jit(solution)/shard_map/add | solution.py:1357
  454.3 24.2 %collective-permute-done.8.carried_up = bf16[3,384,1152]{2,1,0:T(8,128)(2,1)} collective-permute-done((bf16[3,384,1152]{2,1,0:T(8,128)(2,1)}, bf16[3,384,1152]{2,1,0:T(8,128)(2,1)}, u32[]{:S(2)}, u32[]{:S(2)}) %collective-permute-start.8) | collective-permute-done | bytes 2654240 | tf_op jit(solution)/shard_map/ppermute | solution.py:1347
  478.6 191.3 %back.1 = (bf16[320,1536]{1,0:T(8,128)(2,1)}, f32[96,1792]{1,0:T(8,128)}, f32[8,1536]{1,0:T(8,128)}, bf16[3,96,4608]{2,1,0:T(8,128)(2,1)}, bf16[3,320,1536]{2,1,0:T(8,128)(2,1)}) custom-call(bf16[5120,256]{1,0:T(8,128)(2,1)} %get-tuple-element.55.dkv_in, f32[640,768]{1,0:T(8,128)} %get-tuple-element.56.dq_in, f32[640,128]{1,0:T(8,128)} %get-tuple-element.103.refs_5_.cos_in, ...), custom_call_target="tpu_custom_call" | custom-call | flops 6039797760 | bytes 41943040 | tf_op jit(solution)/shard_map/back/pallas_call | solution.py:1163
  674.8 2.7 convert_reduce_fusion
  679.1 2.4 slice_bitcast_fusion.2
  681.5 3.1 fusion.2
  (99 shorter events, 30.3 us)
Async XLA Ops:
  0.6 4.0 copy-start.6
  2.3 2.4 copy-start.7
  3.6 1.2 copy-start.10
  14.0 146.4 %copy-start.8 = (s32[10240]{0:T(1024)S(1)}, s32[10240]{0:T(1024)}, u32[]{:S(2)}) copy-start(s32[10240]{0:T(1024)} %param.20) | copy-start | bytes 122884
  14.0 146.5 %copy-start.12 = (s32[26]{0:T(128)S(1)}, s32[26]{0:T(128)}, u32[]{:S(2)}) copy-start(s32[26]{0:T(128)} %param.21) | copy-start | bytes 316
  156.6 80.6 %collective-permute-start.4 = (bf16[3,384,1152]{2,1,0:T(8,128)(2,1)}, bf16[3,384,1152]{2,1,0:T(8,128)(2,1)}, u32[]{:S(2)}, u32[]{:S(2)}) collective-permute-start(bf16[3,384,1152]{2,1,0:T(8,128)(2,1)} %get-tuple-element.48.refs_6_), channel_id=1, source_target_pairs={{8,16},{10,18},{12,20},{14,22},{16,24},{18,26},{20,28},{22,30},{9,... | collective-permute-start | bytes 7962632 | tf_op jit(solution)/shard_map/ppermute | solution.py:1335
  158.7 78.4 %collective-permute-start.5 = (bf16[3,384,1152]{2,1,0:T(8,128)(2,1)}, bf16[3,384,1152]{2,1,0:T(8,128)(2,1)}, u32[]{:S(2)}, u32[]{:S(2)}) collective-permute-start(bf16[3,384,1152]{2,1,0:T(8,128)(2,1)} %get-tuple-element.49.refs_8_), channel_id=1, source_target_pairs={{16,8},{18,10},{20,12},{22,14},{8,0},{10,2},{12,4},{14,6},{17,9},{... | collective-permute-start | bytes 7962632 | tf_op jit(solution)/shard_map/ppermute | solution.py:1336
  162.1 9.6 %copy-start.13 = (bf16[1536,768]{1,0:T(8,128)(2,1)S(1)}, bf16[1536,768]{1,0:T(8,128)(2,1)}, u32[]{:S(2)}) copy-start(bf16[1536,768]{1,0:T(8,128)(2,1)} %get-tuple-element.44) | copy-start | bytes 7077892
  174.6 1.9 copy-start.3
  174.7 21.8 %copy-start.1 = (bf16[320,1536]{1,0:T(8,128)(2,1)S(1)}, bf16[320,1536]{1,0:T(8,128)(2,1)}, u32[]{:S(2)}) copy-start(bf16[320,1536]{1,0:T(8,128)(2,1)} %x_in.1) | copy-start | bytes 2949124
  176.6 18.3 %collective-permute-start = (bf16[320,1536]{1,0:T(8,128)(2,1)S(1)}, bf16[320,1536]{1,0:T(8,128)(2,1)S(1)}, u32[]{:S(2)}, u32[]{:S(2)}) collective-permute-start(bf16[320,1536]{1,0:T(8,128)(2,1)S(1)} %fusion.4), channel_id=1, source_target_pairs={{0,1},{1,0},{2,3},{3,2},{4,5},{5,4},{6,7},{7,6},{8,9},{9,8},{10,11... | collective-permute-start | bytes 2949128 | tf_op jit(solution)/shard_map/ppermute | solution.py:1194
  176.7 39.7 %collective-permute-start.3 = (bf16[320,1536]{1,0:T(8,128)(2,1)}, bf16[320,1536]{1,0:T(8,128)(2,1)}, u32[]{:S(2)}, u32[]{:S(2)}) collective-permute-start(bf16[320,1536]{1,0:T(8,128)(2,1)} %refs_1_.1), channel_id=1, source_target_pairs={{0,6},{2,4},{4,2},{6,0},{8,14},{10,12},{12,10},{14,8},{16,22},{18,... | collective-permute-start | bytes 2949128 | tf_op jit(solution)/shard_map/ppermute | solution.py:1194
  193.4 43.7 %collective-permute-start.2 = (bf16[320,1536]{1,0:T(8,128)(2,1)}, bf16[320,1536]{1,0:T(8,128)(2,1)}, u32[]{:S(2)}, u32[]{:S(2)}) collective-permute-start(bf16[320,1536]{1,0:T(8,128)(2,1)} %refs_1_.1), channel_id=1, source_target_pairs={{0,4},{2,6},{4,0},{6,2},{8,12},{10,14},{12,8},{14,10},{16,20},{18,... | collective-permute-start | bytes 2949128 | tf_op jit(solution)/shard_map/ppermute | solution.py:1194
  195.8 41.3 %collective-permute-start.1 = (bf16[320,1536]{1,0:T(8,128)(2,1)}, bf16[320,1536]{1,0:T(8,128)(2,1)}, u32[]{:S(2)}, u32[]{:S(2)}) collective-permute-start(bf16[320,1536]{1,0:T(8,128)(2,1)} %refs_1_.1), channel_id=1, source_target_pairs={{0,2},{2,0},{4,6},{6,4},{8,10},{10,8},{12,14},{14,12},{16,18},{18,... | collective-permute-start | bytes 2949128 | tf_op jit(solution)/shard_map/ppermute | solution.py:1194
  409.9 5.5 copy-start
  414.4 30.7 %collective-permute-start.6 = (bf16[4,320,1536]{2,1,0:T(8,128)(2,1)}, bf16[4,320,1536]{2,1,0:T(8,128)(2,1)}, u32[]{:S(2)}, u32[]{:S(2)}) collective-permute-start(bf16[4,320,1536]{2,1,0:T(8,128)(2,1)} %slice_bitcast_fusion), channel_id=1, source_target_pairs={{0,1},{1,0},{2,3},{3,2},{4,5},{5,4},{6,7},{7,6},{8,9},{9,8},{10,11... | collective-permute-start | bytes 11796488 | tf_op jit(solution)/shard_map/ppermute | solution.py:1194
  418.6 5.6 collective-permute-start.7
  418.6 6.9 %copy-start.15 = (bf16[640,768]{1,0:T(8,128)(2,1)S(1)}, bf16[640,768]{1,0:T(8,128)(2,1)}, u32[]{:S(2)}) copy-start(bf16[640,768]{1,0:T(8,128)(2,1)} %get-tuple-element.43.o_ref) | copy-start | bytes 2949124
  419.2 59.4 %collective-permute-start.8 = (bf16[3,384,1152]{2,1,0:T(8,128)(2,1)}, bf16[3,384,1152]{2,1,0:T(8,128)(2,1)}, u32[]{:S(2)}, u32[]{:S(2)}) collective-permute-start(bf16[3,384,1152]{2,1,0:T(8,128)(2,1)} %get-tuple-element.60), channel_id=1, source_target_pairs={{0,8},{2,10},{4,12},{6,14},{1,9},{3,11},{5,13},{7,15}} | collective-permute-start | bytes 7962632 | tf_op jit(solution)/shard_map/ppermute | solution.py:1347
  421.9 56.6 %collective-permute-start.9 = (bf16[3,384,1152]{2,1,0:T(8,128)(2,1)}, bf16[3,384,1152]{2,1,0:T(8,128)(2,1)}, u32[]{:S(2)}, u32[]{:S(2)}) collective-permute-start(bf16[3,384,1152]{2,1,0:T(8,128)(2,1)} %get-tuple-element.61), channel_id=1, source_target_pairs={{24,16},{26,18},{28,20},{30,22},{25,17},{27,19},{29,21},{31,23}} | collective-permute-start | bytes 7962632 | tf_op jit(solution)/shard_map/ppermute | solution.py:1348
  425.5 3.5 copy-start.14
  674.8 3.9 copy-start.2
  677.7 1.4 copy-start.9
  681.5 3.1 copy-start.4
  (2 other events, 2.1 us)

commit v3 on v2

--- a/solution.py
+++ b/solution.py
@@ -13,6 +13,7 @@
 TRUNK = 2048
 PLANE = 4
 NEG = -1e30
+LATE = (2, 0)
 QB=128; KC=512; KB=256
 LOG2E=1.4426950408889634
 
@@ -21,125 +22,6 @@
 
 def dot_nt(a,b): return lax.dot_general(a,b,(((1,),(1,)),((),())),preferred_element_type=jnp.float32)
 def dot_nn(a,b): return lax.dot_general(a,b,(((1,),(0,)),((),())),preferred_element_type=jnp.float32)
-
-def fwd_kernel(info, q_ref, t_ref, o_ref, l_ref, *, heads, scale):
-    blk = pl.program_id(0)
-    nfull = info[blk*8]
-    rows = heads*QB
-    q = jnp.concatenate([q_ref[:, h*128:(h+1)*128] for h in range(heads)], axis=0)
-    c2 = scale*LOG2E
-    def step(carry, s, v):
-        m,l,acc = carry
-        mt = s[:, :128]
-        for j in range(1, KC//128): mt = jnp.maximum(mt, s[:, j*128:(j+1)*128])
-        mn = jnp.maximum(m, jnp.max(mt, axis=1, keepdims=True))
-        p = jnp.exp2((s-mn)*c2)
-        ps = p[:, :128]
-        for j in range(1, KC//128): ps = ps + p[:, j*128:(j+1)*128]
-        a = jnp.exp2((m-mn)*c2)
-        l = l*a + ps
-        acc = acc*a + dot_nn(p.astype(jnp.bfloat16), v)
-        return mn,l,acc
-    def body(c, carry):
-        k = t_ref[pl.ds(pl.multiple_of(c*KC,KC),KC),0:128]
-        v = t_ref[pl.ds(pl.multiple_of(c*KC,KC),KC),128:256]
-        return step(carry, dot_nt(q,k), v)
-    init = (jnp.full((rows,1),NEG,jnp.float32), jnp.zeros((rows,128),jnp.float32), jnp.zeros((rows,128),jnp.float32))
-    b0 = pl.multiple_of(info[blk*8+1]*KB,KB); b1 = pl.multiple_of(info[blk*8+2]*KB,KB)
-    k = jnp.concatenate([t_ref[pl.ds(b0,KB),0:128], t_ref[pl.ds(b1,KB),0:128]],axis=0)
-    v = jnp.concatenate([t_ref[pl.ds(b0,KB),128:256], t_ref[pl.ds(b1,KB),128:256]],axis=0)
-    s = dot_nt(q,k)
-    col = lax.broadcasted_iota(jnp.int32,(QB,KC),1)
-    row = lax.broadcasted_iota(jnp.int32,(QB,KC),0)
-    base = jnp.where(col<KB, info[blk*8+3], info[blk*8+4]-KB)
-    ok = col+base <= row
-    s = jnp.concatenate([jnp.where(ok, s[h*QB:(h+1)*QB], NEG) for h in range(heads)],axis=0)
-    carry = step(init, s, v)
-    m,l,acc = lax.fori_loop(0,nfull,body,carry)
-    lsum = jnp.sum(l,axis=1,keepdims=True)
-    out = (acc/lsum).astype(jnp.bfloat16)
-    o_ref[...] = jnp.concatenate([out[h*QB:(h+1)*QB] for h in range(heads)],axis=1)
-    lse2 = m*c2+jnp.log2(lsum)
-    t = jnp.broadcast_to(lse2,(rows,128)).T
-    l_ref[...] = t[:8,:].reshape(1,8,rows)
-
-def attn_fwd(info, q, tree, scale):
-    T=q.shape[0]; heads=q.shape[1]//128; nb=T//QB; rows=heads*QB
-    return pl.pallas_call(functools.partial(fwd_kernel,heads=heads,scale=scale),
-        grid_spec=pltpu.PrefetchScalarGridSpec(num_scalar_prefetch=1,grid=(nb,),
-            in_specs=[pl.BlockSpec((QB,heads*128),lambda i,s:(i,0)),
-                      pl.BlockSpec(tree.shape,lambda i,s:(0,0))],
-            out_specs=[pl.BlockSpec((QB,heads*128),lambda i,s:(i,0)),pl.BlockSpec((1,8,rows),lambda i,s:(i,0,0))]),
-        out_shape=[jax.ShapeDtypeStruct((T,heads*128),jnp.bfloat16),jax.ShapeDtypeStruct((nb,8,rows),jnp.float32)],
-        compiler_params=pltpu.CompilerParams(vmem_limit_bytes=56<<20),
-        name="attention_forward",
-        cost_estimate=pl.CostEstimate(flops=4*T*heads*128*2304,bytes_accessed=6<<20,transcendentals=T*heads*2304),
-    )(info,q,tree)
-
-def bwd_kernel(info, q_ref, do_ref, o_ref, l_ref, t_ref, dq_ref, dt_ref, sum_ref, *, heads, scale):
-    blk = pl.program_id(0)
-    @pl.when(blk==0)
-    def _():
-        sum_ref[...] = jnp.zeros_like(sum_ref)
-    nfull = info[blk*8]
-    rows = heads*QB
-    cat = lambda ref: jnp.concatenate([ref[:, h*128:(h+1)*128] for h in range(heads)], axis=0)
-    q = cat(q_ref); do = cat(do_ref); o = cat(o_ref)
-    c2 = scale*LOG2E
-    delta = jnp.sum((do.astype(jnp.float32)*o.astype(jnp.float32)).T, axis=0, keepdims=True)
-    lse2 = l_ref[0,0:1,:]
-    def tile(k, v, ok):
-        s = dot_nt(k,q)
-        p = jnp.exp2(s*c2-lse2)
-        if ok is not None:
-            p = jnp.concatenate([jnp.where(ok, p[:, h*QB:(h+1)*QB], 0.0) for h in range(heads)],axis=1)
-        dp = dot_nt(v,do)
-        ds = (p*(dp-delta)).astype(jnp.bfloat16)
-        dv = dot_nn(p.astype(jnp.bfloat16), do)
-        dk = dot_nn(ds, q)
-        dq = lax.dot_general(ds,k,(((0,),(0,)),((),())),preferred_element_type=jnp.float32)
-        return dq,dk,dv
-    def body(c, acc):
-        at = pl.ds(pl.multiple_of(c*KC,KC),KC)
-        dq,dk,dv = tile(t_ref[at,0:128], t_ref[at,128:256], None)
-        sum_ref[at,0:128] += dk
-        sum_ref[at,128:256] += dv
-        return acc+dq
-    b0 = pl.multiple_of(info[blk*8+1]*KB,KB); b1 = pl.multiple_of(info[blk*8+2]*KB,KB)
-    k = jnp.concatenate([t_ref[pl.ds(b0,KB),0:128], t_ref[pl.ds(b1,KB),0:128]],axis=0)
-    v = jnp.concatenate([t_ref[pl.ds(b0,KB),128:256], t_ref[pl.ds(b1,KB),128:256]],axis=0)
-    col = lax.broadcasted_iota(jnp.int32,(KC,QB),0)
-    row = lax.broadcasted_iota(jnp.int32,(KC,QB),1)
-    base = jnp.where(col<KB, info[blk*8+3], info[blk*8+4]-KB)
-    dq,dk,dv = tile(k,v,col+base<=row)
-    sum_ref[pl.ds(b0,KB),0:128] += dk[:KB]
-    sum_ref[pl.ds(b0,KB),128:256] += dv[:KB]
-    sum_ref[pl.ds(b1,KB),0:128] += dk[KB:]
-    sum_ref[pl.ds(b1,KB),128:256] += dv[KB:]
-    dq = lax.fori_loop(0,nfull,body,dq)
-    dq = dq*scale
-    dq_ref[...] = jnp.concatenate([dq[h*QB:(h+1)*QB] for h in range(heads)],axis=1)
-
-    @pl.when(blk == pl.num_programs(0) - 1)
-    def _():
-        dt_ref[...] = sum_ref[...].astype(jnp.bfloat16)
-
-
-def attn_bwd(info,q,do,o,lse,tree,scale):
-    T=q.shape[0]; heads=q.shape[1]//128; nb=T//QB; rows=heads*QB
-    qspec=pl.BlockSpec((QB,heads*128),lambda i,s:(i,0))
-    full=pl.BlockSpec(tree.shape,lambda i,s:(0,0))
-    return pl.pallas_call(functools.partial(bwd_kernel,heads=heads,scale=scale),
-        grid_spec=pltpu.PrefetchScalarGridSpec(num_scalar_prefetch=1,grid=(nb,),
-            in_specs=[qspec,qspec,qspec,pl.BlockSpec((1,8,rows),lambda i,s:(i,0,0)),full],
-            out_specs=[qspec,full],
-            scratch_shapes=[pltpu.VMEM(tree.shape,jnp.float32)]),
-        out_shape=[jax.ShapeDtypeStruct((T,heads*128),jnp.float32),jax.ShapeDtypeStruct(tree.shape,jnp.bfloat16)],
-        compiler_params=pltpu.CompilerParams(vmem_limit_bytes=56<<20),
-        name="attention_backward",
-        cost_estimate=pl.CostEstimate(flops=10*T*heads*128*2304,bytes_accessed=12<<20,transcendentals=T*heads*2304),
-    )(info,q,do,o,lse,tree)
-
 
 def plane_partner(dp, bits):
     one = dp + 1 - 2 * lax.rem(dp, 2)
@@ -170,6 +52,424 @@
 
     beside = jnp.minimum(z_at, 1) + jnp.minimum(lines - 1 - z_at, 1)
     pl.semaphore_wait(barrier, PLANE + beside)
+
+
+def second_block(start):
+    return jnp.where(start < TRUNK, start // KC * (KC // KB) + 1, start // KB)
+
+
+def masked_chunk(tree_ref, other_ref, blk, start):
+    at = pl.ds(pl.multiple_of(second_block(start) * KB, KB), KB)
+    k = jnp.concatenate([other_ref[blk, :, 0:128], tree_ref[at, 0:128]], axis=0)
+    v = jnp.concatenate([other_ref[blk, :, 128:256], tree_ref[at, 128:256]], axis=0)
+    return k, v
+
+
+def attend_kernel(
+    info, hot, q_ref, tree_ref, out_t, x_in, rows_in, cot_in, up_in, down_in, late_up, late_down,
+    att_out, lse_out, middle_out, normed_out, other_ref, cot_out, mid_up, mid_down, last_up, last_down,
+    far, near, pair_send, pair_recv, cot_send, cot_recv, half_send, half_recv, mid_send, mid_recv, last_send, last_recv,
+    *, lines, members, scale,
+):
+    bf16, f32 = jnp.bfloat16, jnp.float32
+    dp = lax.axis_index("dp")
+    core = lax.axis_index("tensor")
+    z_at = dp // PLANE
+    half, width = x_in.shape
+    local_tok, q_width = q_ref.shape
+    heads = q_width // 128
+    rows = heads * QB
+    c2 = scale * LOG2E
+    mate = {"tensor": 1 - core}
+    chip = [None] + [{"dp": plane_partner(dp, bits)} for bits in range(1, PLANE)]
+    ways = ((1, 0), (-1, 1))
+    place_of = lambda sign: z_at if sign == 1 else lines - 1 - z_at
+
+    def mid_hop(sign, way):
+        return pltpu.make_async_remote_copy(
+            src_ref=(up_in, down_in)[way].at[1], dst_ref=(mid_up, mid_down)[way],
+            send_sem=mid_send.at[way], recv_sem=mid_recv.at[way],
+            device_id={"dp": dp + sign * PLANE}, device_id_type=MESH)
+
+    def last_hop(sign, way):
+        return pltpu.make_async_remote_copy(
+            src_ref=(late_up, late_down)[way].at[0], dst_ref=(last_up, last_down)[way],
+            send_sem=last_send.at[way], recv_sem=last_recv.at[way],
+            device_id={"dp": dp + sign * PLANE}, device_id_type=MESH)
+
+    def cot_copy(bits):
+        return pltpu.make_async_remote_copy(
+            src_ref=cot_in, dst_ref=cot_out.at[bits - 1], send_sem=cot_send.at[bits - 1], recv_sem=cot_recv.at[bits - 1],
+            device_id=chip[bits], device_id_type=MESH)
+
+    def cot_half(bits):
+        at = pl.ds((bits - 1) * (half // 2), half // 2)
+        return pltpu.make_async_remote_copy(
+            src_ref=cot_out.at[2 - bits, at], dst_ref=cot_out.at[2, at],
+            send_sem=half_send.at[bits - 1], recv_sem=half_recv.at[bits - 1],
+            device_id=chip[bits], device_id_type=MESH)
+
+    greet(dp, core, lines)
+    for sign, way in ways:
+        place = place_of(sign)
+
+        @pl.when((place >= lines - 3) & (place < lines - 1))
+        def _():
+            mid_hop(sign, way).start()
+
+        @pl.when(place == lines - 2)
+        def _():
+            last_hop(sign, way).start()
+
+    for bits in (1, 2):
+        cot_copy(bits).start()
+
+    def step(carry, s, v):
+        m, l, acc = carry
+        mt = s[:, :128]
+        for j in range(1, KC // 128):
+            mt = jnp.maximum(mt, s[:, j * 128 : (j + 1) * 128])
+        mn = jnp.maximum(m, jnp.max(mt, axis=1, keepdims=True))
+        p = jnp.exp2((s - mn) * c2)
+        ps = p[:, :128]
+        for j in range(1, KC // 128):
+            ps = ps + p[:, j * 128 : (j + 1) * 128]
+        a = jnp.exp2((m - mn) * c2)
+        return mn, l * a + ps, acc * a + dot_nn(p.astype(bf16), v)
+
+    @pl.loop(0, local_tok // QB)
+    def _(blk):
+        start = lax.rem(dp, members) * local_tok + blk * QB
+        nfull = jnp.minimum(start, TRUNK) // KC
+        mine = pl.ds(pl.multiple_of(blk * QB, QB), QB)
+        slots = members * local_tok // KB
+        at = pl.ds(pl.multiple_of(jnp.minimum(start, TRUNK - KC) // KC * KC, KC), KB)
+        first = tree_ref[at, :].astype(f32) * jnp.where(start < TRUNK, 1.0, 0.0)
+        for slot in range(TRUNK // KB, slots):
+            first = first + hot[blk * slots + slot] * tree_ref[slot * KB : (slot + 1) * KB, :].astype(f32)
+        other_ref[blk] = first.astype(bf16)
+        q = jnp.concatenate([q_ref[mine, h * 128 : (h + 1) * 128] for h in range(heads)], axis=0)
+
+        def body(c, carry):
+            at = pl.ds(pl.multiple_of(c * KC, KC), KC)
+            return step(carry, dot_nt(q, tree_ref[at, 0:128]), tree_ref[at, 128:256])
+
+        init = (jnp.full((rows, 1), NEG, f32), jnp.zeros((rows, 128), f32), jnp.zeros((rows, 128), f32))
+        k, v = masked_chunk(tree_ref, other_ref, blk, start)
+        s = dot_nt(q, k)
+        col = lax.broadcasted_iota(jnp.int32, (QB, KC), 1)
+        row = lax.broadcasted_iota(jnp.int32, (QB, KC), 0)
+        ok = col + jnp.where(col < KB, info[2 * blk], info[2 * blk + 1] - KB) <= row
+        s = jnp.concatenate([jnp.where(ok, s[h * QB : (h + 1) * QB], NEG) for h in range(heads)], axis=0)
+        m, l, acc = lax.fori_loop(0, nfull, body, step(init, s, v))
+        lsum = jnp.sum(l, axis=1, keepdims=True)
+        out = (acc / lsum).astype(bf16)
+        for h in range(heads):
+            att_out[mine, h * 128 : (h + 1) * 128] = out[h * QB : (h + 1) * QB]
+        lse = jnp.broadcast_to(m * c2 + jnp.log2(lsum), (rows, 128)).T
+        lse_out[blk] = lse[0:8, :]
+
+    for bits in (1, 2):
+        cot_copy(bits).wait_recv()
+    for bits in (1, 2):
+        cot_half(bits).start()
+
+    def projected(c):
+        at = pl.ds(pl.multiple_of(c * half, half), half)
+        return dot_nt(att_out[at, :], out_t[...])
+
+    far[...] = projected(1 - core).astype(bf16)
+    pair = pltpu.make_async_remote_copy(
+        src_ref=far, dst_ref=near, send_sem=pair_send, recv_sem=pair_recv, device_id=mate, device_id_type=MESH)
+    pair.start()
+    own = projected(core) + x_in[...].astype(f32)
+    pair.wait_recv()
+    middle = own + near[...].astype(f32)
+    middle_out[...] = middle
+    norm = lax.rsqrt(jnp.mean(middle * middle, axis=1, keepdims=True) + EPS)
+    normed_out[...] = (middle * norm * rows_in[1:2, :]).astype(bf16)
+
+    pair.wait_send()
+    for bits in (1, 2):
+        cot_half(bits).wait_recv()
+        cot_copy(bits).wait_send()
+        cot_half(bits).wait_send()
+    for sign, way in ways:
+        place = place_of(sign)
+
+        @pl.when(place >= lines - 2)
+        def _():
+            mid_hop(sign, way).wait_recv()
+
+        @pl.when((place >= lines - 3) & (place < lines - 1))
+        def _():
+            mid_hop(sign, way).wait_send()
+
+        @pl.when(place == lines - 1)
+        def _():
+            last_hop(sign, way).wait_recv()
+
+        @pl.when(place == lines - 2)
+        def _():
+            last_hop(sign, way).wait_send()
+
+
+def attend(info, hot, q, tree, out_t, x, rows, cot, up, down, late_up, late_down, lines, members, scale):
+    bf16, f32 = jnp.bfloat16, jnp.float32
+    local_tok, q_width = q.shape
+    half, width = x.shape
+    anywhere = pl.BlockSpec(memory_space=pl.ANY)
+    inside = pl.BlockSpec(memory_space=pltpu.VMEM)
+    dma = pltpu.SemaphoreType.DMA
+    slab = jax.ShapeDtypeStruct(up.shape[1:], bf16)
+    return pl.pallas_call(
+        functools.partial(attend_kernel, lines=lines, members=members, scale=scale),
+        out_shape=(
+            jax.ShapeDtypeStruct((local_tok, q_width), bf16),
+            jax.ShapeDtypeStruct((local_tok // QB, 8, q_width // 128 * QB), f32),
+            jax.ShapeDtypeStruct((half, width), f32),
+            jax.ShapeDtypeStruct((half, width), bf16),
+            jax.ShapeDtypeStruct((local_tok // QB, KB, 256), bf16),
+            jax.ShapeDtypeStruct((PLANE - 1, half, width), bf16),
+            slab, slab, slab, slab,
+        ),
+        in_specs=[pl.BlockSpec(memory_space=pltpu.SMEM)] * 2 + [inside] * 5 + [anywhere] * 5,
+        out_specs=(inside,) * 5 + (anywhere,) * 5,
+        scratch_shapes=[
+            pltpu.VMEM((half, width), bf16), pltpu.VMEM((half, width), bf16),
+            dma, dma, dma((2,)), dma((2,)), dma((2,)), dma((2,)), dma((2,)), dma((2,)), dma((2,)), dma((2,)),
+        ],
+        compiler_params=pltpu.CompilerParams(vmem_limit_bytes=56 << 20, collective_id=3, has_side_effects=True),
+        name="attend",
+        cost_estimate=pl.CostEstimate(
+            flops=4 * local_tok * q_width * 2304, bytes_accessed=12 << 20, transcendentals=local_tok * q_width * 18
+        ),
+    )(info, hot, q, tree, out_t, x, rows, cot, up, down, late_up, late_down)
+
+
+def attend_back_kernel(
+    info, hot, q_ref, att_ref, lse_ref, tree_ref, other_ref, out_t, dx_in, middle_in, cot_in, gain_in, cos_in, sin_in,
+    y_own, y_other, ff_in, carried_up, carried_down,
+    dq_out, dtree_out, middle_grad_out, gain_out, part_out, layer_out, next_up, next_down,
+    sum_ref, parent_ref, branch, att_grad, y_sum, y_tmp, y_came, own_buf, sum_buf,
+    branch_send, branch_recv, y_load, y_send, y_recv, load_sem, hop_send, hop_recv,
+    *, lines, members, scale,
+):
+    bf16, f32 = jnp.bfloat16, jnp.float32
+    dp = lax.axis_index("dp")
+    core = lax.axis_index("tensor")
+    z_at = dp // PLANE
+    half, width = cot_in.shape
+    local_tok, q_width = q_ref.shape
+    heads = q_width // 128
+    slab_rows = width // lines
+    shard = slab_rows // PLANE
+    rows = heads * QB
+    c2 = scale * LOG2E
+    mate = {"tensor": 1 - core}
+    chip = [None] + [{"dp": plane_partner(dp, bits)} for bits in range(1, PLANE)]
+    ways = ((1, 0), (-1, 1))
+    place_of = lambda sign: z_at if sign == 1 else lines - 1 - z_at
+
+    def own_slab(which, sign):
+        return ff_in.at[which, lines - 1 if sign == 1 else 0]
+
+    def own_load(which, sign):
+        return pltpu.make_async_copy(own_slab(which, sign), own_buf.at[which], load_sem.at[which, 0])
+
+    def carry_load(which, way):
+        return pltpu.make_async_copy((carried_up, carried_down)[way].at[which], sum_buf.at[which], load_sem.at[which, 1])
+
+    def hop(which, sign, way, first_place):
+        slab = lines - 2 if sign == 1 else 1
+        return pltpu.make_async_remote_copy(
+            src_ref=ff_in.at[which, slab] if first_place else sum_buf.at[which],
+            dst_ref=(next_up, next_down)[way].at[which],
+            send_sem=hop_send.at[which, way], recv_sem=hop_recv.at[which, way],
+            device_id={"dp": dp + sign * PLANE}, device_id_type=MESH)
+
+    for sign, way in ways:
+
+        @pl.when(place_of(sign) == 1)
+        def _():
+            for which in (2, 0, 1):
+                own_load(which, sign).start()
+                carry_load(which, way).start()
+
+    def y_loads(k, act):
+        act(pltpu.make_async_copy(y_own.at[k], y_sum.at[k], y_load.at[k, 0]))
+        act(pltpu.make_async_copy(y_other.at[k], y_tmp.at[k], y_load.at[k, 1]))
+
+    for k in range(PLANE):
+        y_loads(k, lambda copy: copy.start())
+    greet(dp, core, lines)
+    for sign, way in ways:
+
+        @pl.when(place_of(sign) == 0)
+        def _():
+            for which in (2, 0, 1):
+                hop(which, sign, way, True).start()
+
+        @pl.when(place_of(sign) == 1)
+        def _():
+            for which in (2, 0, 1):
+                own_load(which, sign).wait()
+                carry_load(which, way).wait()
+                sum_buf[which] = (own_buf[which].astype(f32) + sum_buf[which].astype(f32)).astype(bf16)
+                hop(which, sign, way, False).start()
+
+    middle = middle_in[...]
+    norm = lax.rsqrt(jnp.mean(middle * middle, axis=1, keepdims=True) + EPS)
+    z_own = middle * norm
+    gain_out[...] = jnp.sum(dx_in[...] * z_own, axis=0, keepdims=True)
+    w = dx_in[...] * gain_in[1:2, :]
+    middle_grad = cot_in[...].astype(f32) + norm * (w - z_own * jnp.mean(w * z_own, axis=1, keepdims=True))
+    middle_grad_out[...] = middle_grad
+    token_rows = pl.ds(pl.multiple_of(core * half, half), half)
+    branch[token_rows, :] = middle_grad.astype(bf16)
+    branch_copy = pltpu.make_async_remote_copy(
+        src_ref=branch.at[token_rows], dst_ref=branch.at[token_rows], send_sem=branch_send, recv_sem=branch_recv,
+        device_id=mate, device_id_type=MESH)
+    branch_copy.start()
+
+    def y_copy(bits):
+        return pltpu.make_async_remote_copy(
+            src_ref=y_sum.at[bits], dst_ref=y_came.at[bits - 1], send_sem=y_send.at[bits - 1], recv_sem=y_recv.at[bits - 1],
+            device_id=chip[bits], device_id_type=MESH)
+
+    for k in (1, 2, 3, 0):
+        y_loads(k, lambda copy: copy.wait())
+        y_sum[k] = (y_sum[k].astype(f32) + y_tmp[k].astype(f32)).astype(bf16)
+        if k:
+            y_copy(k).start()
+    branch_copy.wait_recv()
+    att_grad[...] = dot_nn(branch[...], out_t[...]).astype(bf16)
+    for z in range(lines):
+        tile = dot_nn(branch[:, z * slab_rows : (z + 1) * slab_rows].T, att_ref[...]).astype(bf16)
+        for j in range(PLANE):
+            part_out[z, j] = tile[j * shard : (j + 1) * shard]
+
+    sum_ref[...] = jnp.zeros_like(sum_ref)
+    cosines, sines = cos_in[...], sin_in[...]
+
+    @pl.loop(0, local_tok // QB)
+    def _(blk):
+        start = lax.rem(dp, members) * local_tok + blk * QB
+        nfull = jnp.minimum(start, TRUNK) // KC
+        mine = pl.ds(pl.multiple_of(blk * QB, QB), QB)
+        stacked = lambda ref: jnp.concatenate([ref[mine, h * 128 : (h + 1) * 128] for h in range(heads)], axis=0)
+        q, do, o = stacked(q_ref), stacked(att_grad), stacked(att_ref)
+        delta = jnp.sum((do.astype(f32) * o.astype(f32)).T, axis=0, keepdims=True)
+        lse = lse_ref[blk][0:1, :]
+
+        def tile(k, v, ok):
+            p = jnp.exp2(dot_nt(k, q) * c2 - lse)
+            if ok is not None:
+                p = jnp.concatenate([jnp.where(ok, p[:, h * QB : (h + 1) * QB], 0.0) for h in range(heads)], axis=1)
+            ds = (p * (dot_nt(v, do) - delta)).astype(bf16)
+            dq = lax.dot_general(ds, k, (((0,), (0,)), ((), ())), preferred_element_type=f32)
+            return dq, dot_nn(ds, q), dot_nn(p.astype(bf16), do)
+
+        def body(c, acc):
+            at = pl.ds(pl.multiple_of(c * KC, KC), KC)
+            dq, dk, dv = tile(tree_ref[at, 0:128], tree_ref[at, 128:256], None)
+            sum_ref[at, 0:128] += dk
+            sum_ref[at, 128:256] += dv
+            return acc + dq
+
+        k, v = masked_chunk(tree_ref, other_ref, blk, start)
+        col = lax.broadcasted_iota(jnp.int32, (KC, QB), 0)
+        row = lax.broadcasted_iota(jnp.int32, (KC, QB), 1)
+        ok = col + jnp.where(col < KB, info[2 * blk], info[2 * blk + 1] - KB) <= row
+        dq, dk, dv = tile(k, v, ok)
+        at = pl.ds(pl.multiple_of(second_block(start) * KB, KB), KB)
+        sum_ref[at, 0:128] += dk[KB:]
+        sum_ref[at, 128:256] += dv[KB:]
+        parent_ref[blk, :, 0:128] = dk[:KB]
+        parent_ref[blk, :, 128:256] = dv[:KB]
+
+        @pl.when(start < TRUNK)
+        def _():
+            at = pl.ds(pl.multiple_of(start // KC * KC, KC), KB)
+            sum_ref[at, 0:128] += dk[:KB]
+            sum_ref[at, 128:256] += dv[:KB]
+
+        dq = lax.fori_loop(0, nfull, body, dq) * scale
+        place = pl.ds(pl.multiple_of(blk * QB, QB), QB)
+        for h in range(heads):
+            part = dq[h * QB : (h + 1) * QB]
+            turned = part * cos_in[place, :] - pltpu.roll(part, 64, 1) * sin_in[place, :]
+            dq_out[mine, h * 128 : (h + 1) * 128] = turned.astype(bf16)
+
+    dtree_out[0:TRUNK, :] = sum_ref[0:TRUNK, :].astype(bf16)
+
+    @pl.loop(TRUNK // KB, members * local_tok // KB)
+    def _(slot):
+        at = pl.ds(pl.multiple_of(slot * KB, KB), KB)
+        total = sum_ref[at, :]
+        for blk in range(local_tok // QB):
+            total = total + hot[blk * (members * local_tok // KB) + slot] * parent_ref[blk]
+        dtree_out[at, :] = total.astype(bf16)
+
+    for bits in range(1, PLANE):
+        y_copy(bits).wait_recv()
+    total = middle_in[...] + y_sum[0].astype(f32)
+    for bits in range(1, PLANE):
+        total = total + y_came[bits - 1].astype(f32)
+    layer_out[...] = total.astype(bf16)
+    branch_copy.wait_send()
+    for bits in range(1, PLANE):
+        y_copy(bits).wait_send()
+    for sign, way in ways:
+
+        @pl.when(place_of(sign) <= 1)
+        def _():
+            for which in range(3):
+                hop(which, sign, way, False).wait_send()
+
+        @pl.when((place_of(sign) >= 1) & (place_of(sign) <= 2))
+        def _():
+            for which in range(3):
+                hop(which, sign, way, False).wait_recv()
+
+
+def attend_back(info, hot, q, attended, lse, tree, other, out_t, dx, middle, cot, rows, cosines, sines, y_own, y_other, ff_parts, up, down, lines, members, scale):
+    bf16, f32 = jnp.bfloat16, jnp.float32
+    local_tok, q_width = q.shape
+    half, width = cot.shape
+    slab_rows = width // lines
+    shard = slab_rows // PLANE
+    block = up.shape[-1]
+    anywhere = pl.BlockSpec(memory_space=pl.ANY)
+    inside = pl.BlockSpec(memory_space=pltpu.VMEM)
+    dma = pltpu.SemaphoreType.DMA
+    slab = jax.ShapeDtypeStruct((3, slab_rows, block), bf16)
+    return pl.pallas_call(
+        functools.partial(attend_back_kernel, lines=lines, members=members, scale=scale),
+        out_shape=(
+            jax.ShapeDtypeStruct((local_tok, q_width), bf16),
+            jax.ShapeDtypeStruct(tree.shape, bf16),
+            jax.ShapeDtypeStruct((half, width), f32),
+            jax.ShapeDtypeStruct((1, width), f32),
+            jax.ShapeDtypeStruct((lines, PLANE, shard, q_width), bf16),
+            jax.ShapeDtypeStruct((half, width), bf16),
+            slab, slab,
+        ),
+        in_specs=[pl.BlockSpec(memory_space=pltpu.SMEM)] * 2 + [inside] * 12 + [anywhere] * 5,
+        out_specs=(inside,) * 6 + (anywhere,) * 2,
+        scratch_shapes=[
+            pltpu.VMEM(tree.shape, f32), pltpu.VMEM((local_tok // QB, KB, 256), f32),
+            pltpu.VMEM((local_tok, width), bf16), pltpu.VMEM((local_tok, q_width), bf16),
+            pltpu.VMEM((PLANE, half, width), bf16), pltpu.VMEM((PLANE, half, width), bf16), pltpu.VMEM((PLANE - 1, half, width), bf16),
+            pltpu.VMEM((3, slab_rows, block), bf16), pltpu.VMEM((3, slab_rows, block), bf16),
+            dma, dma, dma((PLANE, 2)), dma((PLANE - 1,)), dma((PLANE - 1,)), dma((3, 2)), dma((3, 2)), dma((3, 2)),
+        ],
+        compiler_params=pltpu.CompilerParams(vmem_limit_bytes=62 << 20, collective_id=4, has_side_effects=True),
+        name="attend_back",
+        cost_estimate=pl.CostEstimate(
+            flops=10 * local_tok * q_width * 2304, bytes_accessed=30 << 20, transcendentals=local_tok * q_width * 18
+        ),
+    )(info, hot, q, attended, lse, tree, other, out_t, dx, middle, cot, rows, cosines, sines, y_own, y_other, ff_parts, up, down)
 
 
 class Gather:
@@ -264,13 +564,13 @@
         own_out, *slab_outs,
     ) = refs[: 8 + 2 * steps]
     (
-        first_out, out_t, q_out, tree_out, normed_out, rows_out,
+        late_up, late_down, first_out, out_t, q_out, tree_out, normed_out, rows_out,
         first_all, extra_all, x_all, normed, pair,
         first_local, first_ls, first_lr, first_ps, first_pr,
         extra_local, extra_ls, extra_lr, extra_ps, extra_pr,
         out_local, out_ls, out_lr, out_ps, out_pr,
         spread_local, spread_send, spread_recv, hop_send, hop_recv,
-        x_local, x_send, x_recv, keep_sem, pair_local, pair_send, pair_recv,
+        x_local, x_send, x_recv, keep_sem, pair_local, pair_send, pair_recv, late_send, late_recv,
     ) = refs[8 + 2 * steps :]
     bf16, f32 = jnp.bfloat16, jnp.float32
     dp = lax.axis_index("dp")
@@ -311,6 +611,14 @@
         return pltpu.make_async_remote_copy(
             src_ref=(own_out if step == 0 else outs[step - 1]).at[which], dst_ref=outs[step].at[which],
             send_sem=hop_send.at[which, way, step], recv_sem=hop_recv.at[which, way, step],
+            device_id={"dp": dp + sign * PLANE}, device_id_type=MESH)
+
+    def late_hop(index, sign):
+        way = (1 - sign) // 2
+        return pltpu.make_async_remote_copy(
+            src_ref=(ups if sign == 1 else downs)[steps - 1].at[LATE[index]],
+            dst_ref=(late_up if sign == 1 else late_down).at[index],
+            send_sem=late_send.at[index, way], recv_sem=late_recv.at[index, way],
             device_id={"dp": dp + sign * PLANE}, device_id_type=MESH)
 
     for one in (first, extra, outer):
@@ -425,10 +733,28 @@
                         @pl.when(place < lines - 1)
                         def _():
                             hop(which, sign, step + 1).start()
+
+                    elif which in LATE:
+
+                        @pl.when(place < lines - 1)
+                        def _():
+                            late_hop(LATE.index(which), sign).start()
+
     for bits in range(1, PLANE):
         pair_copy(bits).wait_recv()
         pair_copy(bits, True).wait_recv()
     outer.plane_wait_recv()
+    for index in range(len(LATE)):
+        for sign in (1, -1):
+            place = z_at if sign == 1 else lines - 1 - z_at
+
+            @pl.when(place >= lines - 2)
+            def _():
+                late_hop(index, sign).wait_recv()
+
+            @pl.when((place >= lines - 3) & (place < lines - 1))
+            def _():
+                late_hop(index, sign).wait_send()
 
     for one in (first, extra, outer):
         one.finish()
@@ -469,6 +795,7 @@
     return pl.pallas_call(
         functools.partial(front_kernel, lines=lines, members=members, steps=steps),
         out_shape=(slab,) * (1 + 2 * steps)
+        + (jax.ShapeDtypeStruct((len(LATE), PLANE * shard, block), bf16),) * 2
         + (
             jax.ShapeDtypeStruct((width, columns), bf16),
             jax.ShapeDtypeStruct((width, q_width), bf16),
@@ -478,7 +805,7 @@
             jax.ShapeDtypeStruct((16, width), f32),
         ),
         in_specs=[anywhere] * 5 + [inside] * 2,
-        out_specs=(anywhere,) * (1 + 2 * steps) + (anywhere, anywhere, inside, anywhere, inside, inside),
+        out_specs=(anywhere,) * (3 + 2 * steps) + (anywhere, anywhere, inside, anywhere, inside, inside),
         scratch_shapes=[
             pltpu.VMEM((width, columns), bf16), pltpu.VMEM((16 * count, width), bf16),
             pltpu.VMEM((local_tok, width), bf16), pltpu.VMEM((local_tok, width), bf16),
@@ -488,6 +815,7 @@
         + [
             dma((3,)), dma((3, PLANE - 1)), dma((3, PLANE - 1)), dma((3, 2, steps)), dma((3, 2, steps)),
             dma, dma, dma, dma, dma, dma((2 * PLANE - 1,)), dma((2 * PLANE - 1,)),
+            dma((len(LATE), 2)), dma((len(LATE), 2)),
         ],
         compiler_params=pltpu.CompilerParams(vmem_limit_bytes=56 << 20, collective_id=1, has_side_effects=True),
         name="front",
@@ -498,14 +826,18 @@
 def ff_kernel(
     *refs, tile_h, tile_n, tile_m, lines,
 ):
-    spread = 1 + 2 * (lines - 2)
-    x_in, cots, slabs = refs[0], refs[1 : 1 + PLANE], refs[1 + PLANE : 1 + PLANE + spread]
+    early = lines - 3
+    x_in, cot_in, cot_came, slab = refs[:4]
+    ups, downs = refs[4 : 4 + early], refs[4 + early : 4 + 2 * early]
+    late_up, late_down, mid_up, mid_down, last_up, last_down = refs[4 + 2 * early : 10 + 2 * early]
+    cots = [cot_in] + [cot_came.at[k] for k in range(PLANE - 1)]
     (
-        dx_out, y_out, parts_out, top_out, bottom_out,
+        dx_out, y_own, y_other, parts_out, carried_up, carried_down,
         x_all, cot_all, gate_w, up_w, down_w, prod, gate_g, up_g, far, near, back, y_stage,
-        x_send, x_recv, fwd_send, fwd_recv, pair_send, pair_recv, dx_send, dx_recv,
-        x_load, cot_load, cot_send, cot_recv, weight_sem, hop_send, hop_recv, y_sem, out_sem,
-    ) = refs[1 + PLANE + spread :]
+        x_send, x_recv, half_send, half_recv, fwd_send, fwd_recv, pair_send, pair_recv, dx_send, dx_recv,
+        x_load, cot_load, cot_send, cot_recv, weight_sem, hop_send, hop_recv, y_keep, y_send, y_recv,
+        out_sem, first_send, first_recv,
+    ) = refs[10 + 2 * early :]
     bf16 = jnp.bfloat16
     half = x_in.shape[0]
     width = x_in.shape[1]
@@ -520,34 +852,43 @@
     z_at = dp // PLANE
     slab_rows = width // lines
     weights = (gate_w, up_w, down_w)
+    grads_of = weights
+    down_y = down_w
     ways = ((1, 0), (-1, 1))
     place_of = lambda sign: z_at if sign == 1 else lines - 1 - z_at
     place_rows = lambda z: pl.ds(pl.multiple_of(z * slab_rows, slab_rows), slab_rows)
 
+    def second_to_last(which, way):
+        if which == 1:
+            return (mid_up, mid_down)[way]
+        return (late_up, late_down)[way].at[LATE.index(which)]
+
     def weight_loads(which, act):
         for sign, way in ways:
-            for step in range(lines - 2):
-                piece = 1 + way * (lines - 2) + step
+            pieces = [piece.at[which] for piece in (ups, downs)[way]] + [second_to_last(which, way)]
+            if which == 2:
+                pieces.append((last_up, last_down)[way])
+            for step, piece in enumerate(pieces):
 
                 @pl.when(place_of(sign) >= step + 1)
                 def _():
                     act(pltpu.make_async_copy(
-                        slabs[piece].at[which], weights[which].at[place_rows(z_at - sign * (step + 1))],
-                        weight_sem.at[which, piece]))
-
-        act(pltpu.make_async_copy(slabs[0].at[which], weights[which].at[place_rows(z_at)], weight_sem.at[which, 0]))
+                        piece, weights[which].at[place_rows(z_at - sign * (step + 1))],
+                        weight_sem.at[which, 1 + way * (lines - 1) + step]))
+
+        act(pltpu.make_async_copy(slab.at[which], weights[which].at[place_rows(z_at)], weight_sem.at[which, 0]))
 
     def last_hop(which, sign, way):
         origin = 0 if sign == 1 else lines - 1
         return pltpu.make_async_remote_copy(
-            src_ref=slabs[(way + 1) * (lines - 2)].at[which],
+            src_ref=second_to_last(which, way),
             dst_ref=weights[which].at[pl.ds(origin * slab_rows, slab_rows)],
             send_sem=hop_send.at[which, way], recv_sem=hop_recv.at[which, way],
             device_id={"dp": dp + sign * PLANE}, device_id_type=MESH)
 
     def weight_wait(which):
         weight_loads(which, lambda copy: copy.wait())
-        for sign, way in ways:
+        for sign, way in ways if which < 2 else ():
 
             @pl.when(place_of(sign) == lines - 1)
             def _():
@@ -569,7 +910,7 @@
     for which in (2, 0, 1):
         weight_loads(which, lambda copy: copy.start())
     greet(dp, core, lines)
-    for which in (2, 0, 1):
+    for which in (0, 1):
         for sign, way in ways:
 
             @pl.when(place_of(sign) == lines - 2)
@@ -581,6 +922,13 @@
             src_ref=x_in, dst_ref=x_all.at[rows(k, 0) if k else rows(0, 1)],
             send_sem=x_send.at[k], recv_sem=x_recv.at[k],
             device_id=chip[k] if k else mate, device_id_type=MESH)
+
+    def x_half(k):
+        at = lambda j: pl.ds(2 * j * half + (k - 1) * (half // 2), half // 2)
+        return pltpu.make_async_remote_copy(
+            src_ref=x_all.at[at(PLANE - 1 - k)], dst_ref=x_all.at[at(PLANE - 1)],
+            send_sem=half_send.at[k - 1], recv_sem=half_recv.at[k - 1],
+            device_id=chip[k], device_id_type=MESH)
 
     def x_forward(k):
         return pltpu.make_async_remote_copy(
@@ -619,14 +967,22 @@
             cols = pl.ds(pl.multiple_of(t * tile_h, tile_h), tile_h)
             up_g[at, cols] = dot_nn(cot_all[at, :], down_w[:, cols]).astype(bf16)
 
-    def gate_up(k):
+    def gate_part(k):
         at = rows(k, 0, 2)
 
         @pl.loop(0, block // tile_h)
         def _(t):
             cols = pl.ds(pl.multiple_of(t * tile_h, tile_h), tile_h)
-            gate = dot_nn(x_all[at, :], gate_w[:, cols])
+            gate_g[at, cols] = dot_nn(x_all[at, :], gate_w[:, cols]).astype(bf16)
+
+    def up_part(k):
+        at = rows(k, 0, 2)
+
+        @pl.loop(0, block // tile_h)
+        def _(t):
+            cols = pl.ds(pl.multiple_of(t * tile_h, tile_h), tile_h)
             up = dot_nn(x_all[at, :], up_w[:, cols])
+            gate = gate_g[at, cols].astype(jnp.float32)
             pg = up_g[at, cols].astype(jnp.float32)
             sig = 0.5 * jnp.tanh(0.5 * gate) + 0.5
             silu = gate * sig
@@ -656,77 +1012,90 @@
         if k:
             dx_copy(k).start()
 
-    def y_copies(k, act):
-        for r in range(2):
-            act(pltpu.make_async_copy(y_stage.at[pl.ds(r * half, half)], y_out.at[r, k], y_sem.at[r]))
+    def y_local(k):
+        return pltpu.make_async_copy(y_stage.at[pl.ds(0, half)], y_own.at[k], y_keep)
+
+    def y_copy(k):
+        return pltpu.make_async_remote_copy(
+            src_ref=y_stage.at[pl.ds(half, half)], dst_ref=y_other.at[k],
+            send_sem=y_send.at[k], recv_sem=y_recv.at[k], device_id=mate, device_id_type=MESH)
 
     def y_part(k):
         if k:
-            y_copies(k - 1, lambda copy: copy.wait())
+            y_local(k - 1).wait()
+            y_copy(k - 1).wait_send()
 
         @pl.loop(0, width // tile_n)
         def _(t):
             cols = pl.ds(pl.multiple_of(t * tile_n, tile_n), tile_n)
-            y_stage[:, cols] = dot_nt(prod[rows(k, 0, 2), :], down_w[cols, :]).astype(bf16)
-
-        y_copies(k, lambda copy: copy.start())
+            y_stage[:, cols] = dot_nt(prod[rows(k, 0, 2), :], down_y[cols, :]).astype(bf16)
+
+        y_local(k).start()
+        y_copy(k).start()
 
     x_keep.wait()
+    x_copy(0).wait_recv()
     weight_wait(0)
+    gate_part(0)
+    for k in (1, 2):
+        x_copy(k).wait_recv()
+        x_forward(k).start()
+    for k in (1, 2):
+        x_half(k).start()
+    x_forward(1).wait_recv()
+    gate_part(1)
+    x_forward(2).wait_recv()
+    gate_part(2)
+    for k in (1, 2):
+        x_half(k).wait_recv()
+    x_forward(3).start()
     weight_wait(1)
-    x_copy(0).wait_recv()
-    gate_up(0)
-    dx_first(0)
-    x_copy(3).start()
-    x_copy(1).wait_recv()
-    x_forward(1).start()
-    x_copy(2).wait_recv()
-    x_forward(2).start()
-    dx_second(0)
-    x_forward(1).wait_recv()
-    gate_up(1)
-    dx_first(1)
-    y_part(0)
-    dx_second(1)
-    x_forward(2).wait_recv()
-    gate_up(2)
-    dx_first(2)
-    y_part(1)
-    x_copy(3).wait_recv()
-    x_forward(3).start()
-    dx_second(2)
+    up_part(0)
+    up_part(1)
     x_forward(3).wait_recv()
-    gate_up(3)
-    dx_first(3)
-    y_part(2)
-    dx_second(3)
-    y_part(3)
+    gate_part(3)
+    up_part(2)
+    up_part(3)
+
+    def first_hop(which, sign, way):
+        at = pl.ds((lines - 1) * slab_rows if sign == 1 else 0, slab_rows)
+        return pltpu.make_async_remote_copy(
+            src_ref=grads_of[which].at[at], dst_ref=(carried_up, carried_down)[way].at[which],
+            send_sem=first_send.at[which, way], recv_sem=first_recv.at[which, way],
+            device_id={"dp": dp + sign * PLANE}, device_id_type=MESH)
 
     def out_copies(which, act):
         for z in range(lines):
             at = pl.ds(z * slab_rows, slab_rows)
-            act(pltpu.make_async_copy(weights[which].at[at], parts_out.at[which, z], out_sem.at[which, z]))
-        for index, out in ((lines, top_out), (lines + 1, bottom_out)):
-            at = pl.ds((lines - 1) * slab_rows if out is top_out else 0, slab_rows)
-            act(pltpu.make_async_copy(weights[which].at[at], out.at[which], out_sem.at[which, index]))
-
-    @pl.loop(0, width // tile_m)
-    def _(m):
-        at = pl.ds(pl.multiple_of(m * tile_m, tile_m), tile_m)
-        turned = cot_all[:, at].T
-        down_w[at, :] = dot_nn(turned, prod[...]).astype(bf16)
-
-    out_copies(2, lambda copy: copy.start())
-
-    @pl.loop(0, width // tile_m)
-    def _(m):
-        at = pl.ds(pl.multiple_of(m * tile_m, tile_m), tile_m)
-        turned = x_all[:, at].T
-        gate_w[at, :] = dot_nn(turned, gate_g[...]).astype(bf16)
-        up_w[at, :] = dot_nn(turned, up_g[...]).astype(bf16)
-
-    out_copies(0, lambda copy: copy.start())
-    out_copies(1, lambda copy: copy.start())
+            act(pltpu.make_async_copy(grads_of[which].at[at], parts_out.at[which, z], out_sem.at[which, z]))
+
+    def weight_grad(which, tokens, grad):
+        @pl.loop(0, width // tile_m)
+        def _(m):
+            at = pl.ds(pl.multiple_of(m * tile_m, tile_m), tile_m)
+            grads_of[which][at, :] = dot_nn(tokens[:, at].T, grad[...]).astype(bf16)
+
+        for sign, way in ways:
+
+            @pl.when(place_of(sign) == 0)
+            def _():
+                first_hop(which, sign, way).start()
+
+        out_copies(which, lambda copy: copy.start())
+
+    for k in range(PLANE):
+        y_part(k)
+    weight_grad(2, cot_all, prod)
+    dx_first(1)
+    dx_first(2)
+    dx_second(1)
+    dx_first(3)
+    dx_second(2)
+    dx_first(0)
+    dx_second(3)
+    dx_second(0)
+    weight_grad(0, x_all, gate_g)
+    weight_grad(1, x_all, up_g)
 
     for k in range(1, PLANE):
         dx_copy(k).wait_recv()
@@ -736,25 +1105,40 @@
     dx_out[...] = total
 
     for k in range(PLANE):
-        x_copy(k).wait_send()
+        if k < PLANE - 1:
+            x_copy(k).wait_send()
+        if k in (1, 2):
+            x_half(k).wait_send()
         pair_copy(k).wait_send()
         if k:
             x_forward(k).wait_send()
             dx_copy(k).wait_send()
-    y_copies(PLANE - 1, lambda copy: copy.wait())
+    y_local(PLANE - 1).wait()
+    y_copy(PLANE - 1).wait_send()
+    for k in range(PLANE):
+        y_copy(k).wait_recv()
     for which in range(3):
         out_copies(which, lambda copy: copy.wait())
         for sign, way in ways:
-
-            @pl.when(place_of(sign) == lines - 2)
+            if which < 2:
+
+                @pl.when(place_of(sign) == lines - 2)
+                def _():
+                    last_hop(which, sign, way).wait_send()
+
+            @pl.when(place_of(sign) == 0)
             def _():
-                last_hop(which, sign, way).wait_send()
+                first_hop(which, sign, way).wait_send()
+
+            @pl.when(place_of(sign) == 1)
+            def _():
+                first_hop(which, sign, way).wait_recv()
 
     for k in range(PLANE):
         cot_copy(k).wait_send()
 
 
-def feed_forward(x, cots, slabs, lines, tile_h=384, tile_n=512, tile_m=256):
+def feed_forward(x, cot, cot_came, slabs, lines, tile_h=384, tile_n=512, tile_m=256):
     half, width = x.shape
     block = slabs[0].shape[-1]
     slab_rows = width // lines
@@ -767,32 +1151,34 @@
         functools.partial(ff_kernel, tile_h=tile_h, tile_n=tile_n, tile_m=tile_m, lines=lines),
         out_shape=(
             jax.ShapeDtypeStruct((half, width), jnp.float32),
-            jax.ShapeDtypeStruct((2, PLANE, half, width), bf16),
+            jax.ShapeDtypeStruct((PLANE, half, width), bf16),
+            jax.ShapeDtypeStruct((PLANE, half, width), bf16),
             jax.ShapeDtypeStruct((3, lines, slab_rows, block), bf16),
             slab,
             slab,
         ),
-        in_specs=[anywhere] * (1 + PLANE + len(slabs)),
-        out_specs=(pl.BlockSpec(memory_space=pltpu.VMEM),) + (anywhere,) * 4,
+        in_specs=[anywhere] * (3 + len(slabs)),
+        out_specs=(pl.BlockSpec(memory_space=pltpu.VMEM),) + (anywhere,) * 5,
         scratch_shapes=[
             pltpu.VMEM((tokens, width), bf16), pltpu.VMEM((tokens, width), bf16),
             pltpu.VMEM((width, block), bf16), pltpu.VMEM((width, block), bf16), pltpu.VMEM((width, block), bf16),
             pltpu.VMEM((tokens, block), bf16), pltpu.VMEM((tokens, block), bf16), pltpu.VMEM((tokens, block), bf16),
             pltpu.VMEM((PLANE, half, width), bf16), pltpu.VMEM((PLANE, half, width), bf16), pltpu.VMEM((PLANE - 1, half, width), bf16),
             pltpu.VMEM((2 * half, width), bf16),
-            dma((PLANE,)), dma((PLANE,)), dma((PLANE - 1,)), dma((PLANE - 1,)), dma((PLANE,)), dma((PLANE,)),
-            dma((PLANE - 1,)), dma((PLANE - 1,)), dma, dma((PLANE,)), dma((PLANE,)), dma((PLANE,)), dma((3, 2 * lines)), dma((3, 2)), dma((3, 2)), dma((2,)), dma((3, lines + 2)),
+            dma((PLANE - 1,)), dma((PLANE - 1,)), dma((2,)), dma((2,)), dma((PLANE - 1,)), dma((PLANE - 1,)), dma((PLANE,)), dma((PLANE,)),
+            dma((PLANE - 1,)), dma((PLANE - 1,)), dma, dma((PLANE,)), dma((PLANE,)), dma((PLANE,)), dma((3, 2 * lines)), dma((3, 2)), dma((3, 2)), dma, dma((PLANE,)), dma((PLANE,)),
+            dma((3, lines)), dma((3, 2)), dma((3, 2)),
         ],
         compiler_params=pltpu.CompilerParams(vmem_limit_bytes=62 << 20, collective_id=0, has_side_effects=True),
         name="feed_forward",
         cost_estimate=pl.CostEstimate(flops=18 * tokens * width * block, bytes_accessed=60 << 20, transcendentals=tokens * block),
-    )(x, *cots, *slabs)
+    )(x, cot, cot_came, *slabs)
 
 
 def back_kernel(
     dkv_in, dq_in, cos_in, sin_in, normed_in, first_in, out_part, x_in, rows_in, gain_row_in, middle_grad_in,
-    ff_in, carried_up, carried_down, y_in,
-    input_grad_out, sums_out, small_out, ff_out, y_out,
+    ff_in, carried_up, carried_down,
+    input_grad_out, sums_out, small_out, ff_out,
     kv_own, kv_other, kv_plane, kv_merged, kv_line, grads, part_q, part_kv, own_o,
     recv_q, recv_kv, recv_o, line_q, line_kv, line_o, from_q, from_kv, from_o,
     far, near, small_own, small_mate, small_plane, small_line,
@@ -800,7 +1186,7 @@
     kv_local, kv_send, kv_recv, kv_line_send, kv_line_recv,
     plane_send, plane_recv, line_send, line_recv, own_o_sem,
     mate_send, mate_recv, small_mate_sem, small_plane_send, small_plane_recv, small_line_send, small_line_recv,
-    load_sem, own_sem, carry_sem, hop_send, hop_recv, spread_local, spread_send, spread_recv, y_send, y_recv,
+    load_sem, own_sem, carry_sem, hop_send, hop_recv, spread_local, spread_send, spread_recv,
     *, lines, members, scale,
 ):
     bf16, f32 = jnp.bfloat16, jnp.float32
@@ -850,9 +1236,9 @@
         for sign, way in ways:
             carry_load(which, sign, way).start()
 
-            @pl.when(place_of(sign) == 1)
+            @pl.when((place_of(sign) >= 1) & (place_of(sign) <= 2))
             def _():
-                slab_load(which, sign, way, 1).start()
+                slab_load(which, sign, way, 2).start()
 
         own_load(which).start()
 
@@ -878,16 +1264,16 @@
 
     def hop(which, sign, way, step, first_place=False):
         slab = lines - 1 - step if sign == 1 else step
-        carried = first_buf.at[which, way] if step == 1 else recv_buf.at[which, way, step - 2]
-        return pltpu.make_async_remote_copy(
-            src_ref=ff_in.at[which, slab] if first_place else carried, dst_ref=recv_buf.at[which, way, step - 1],
-            send_sem=hop_send.at[which, way, step - 1], recv_sem=hop_recv.at[which, way, step - 1],
+        carried = first_buf.at[which, way] if step == 2 else recv_buf.at[which, way, step - 3]
+        return pltpu.make_async_remote_copy(
+            src_ref=ff_in.at[which, slab] if first_place else carried, dst_ref=recv_buf.at[which, way, step - 2],
+            send_sem=hop_send.at[which, way, step - 2], recv_sem=hop_recv.at[which, way, step - 2],
             device_id={"dp": dp + sign * PLANE}, device_id_type=MESH)
 
     def hop_step(which, step):
         for sign, way in ways:
             place = place_of(sign)
-            if step == 1:
+            if step == 2:
                 carry_load(which, sign, way).wait()
 
             @pl.when(place == 0)
@@ -896,14 +1282,14 @@
 
             @pl.when((place >= 1) & (place <= step))
             def _():
-                if step > 1:
+                if step > 2:
                     hop(which, sign, way, step - 1).wait_recv()
                 slab_load(which, sign, way, step).wait()
                 mine = own_buf[which, way].astype(f32)
-                if step == 1:
+                if step == 2:
                     first_buf[which, way] = (mine + first_buf[which, way].astype(f32)).astype(bf16)
                 else:
-                    recv_buf[which, way, step - 2] = (mine + recv_buf[which, way, step - 2].astype(f32)).astype(bf16)
+                    recv_buf[which, way, step - 3] = (mine + recv_buf[which, way, step - 3].astype(f32)).astype(bf16)
                 hop(which, sign, way, step).start()
 
             if step < lines - 2:
@@ -913,7 +1299,7 @@
                     slab_load(which, sign, way, step + 1).start()
 
     for which in order:
-        hop_step(which, 1)
+        hop_step(which, 2)
 
     groups = {
         "o": (0, out_part, own_o, recv_o, line_o, from_o, q_width + 256, q_width),
@@ -967,13 +1353,7 @@
     def turned_back(part):
         return (part * cosines - pltpu.roll(part, 64, 1) * sines).astype(bf16)
 
-    for at in range(0, q_width, 128):
-        grads[:, at : at + 128] = turned_back(dq_in[:, at : at + 128])
-
-    def y_copy(bits):
-        return pltpu.make_async_remote_copy(
-            src_ref=y_in.at[bits], dst_ref=y_out.at[bits - 1], send_sem=y_send.at[bits - 1], recv_sem=y_recv.at[bits - 1],
-            device_id=chip[bits], device_id_type=MESH)
+    grads[:, 0:q_width] = dq_in[...]
 
     def weight_part(part, at, size):
         for z in range(lines):
@@ -997,7 +1377,7 @@
         src_ref=kv_merged, dst_ref=kv_line, send_sem=kv_line_send, recv_sem=kv_line_recv,
         device_id={"dp": line_partner(dp)}, device_id_type=MESH)
     kv_across.start()
-    for step in range(2, lines - 1):
+    for step in range(3, lines - 1):
         hop_step(order[0], step)
     for bits in range(1, PLANE):
         kv_copy(bits, 0).wait_recv()
@@ -1009,8 +1389,6 @@
     grads[:, q_width + 128 :] = total[:, 128:256].astype(bf16)
     weight_part(part_kv, q_width, 256)
     plane_start("kv")
-    for bits in range(1, PLANE):
-        y_copy(bits).start()
 
     def normed_grad(c):
         at = pl.ds(pl.multiple_of(c * half, half), half)
@@ -1045,10 +1423,10 @@
         src_ref=small_own, dst_ref=small_mate, send_sem=small_mate_sem.at[0], recv_sem=small_mate_sem.at[1],
         device_id=mate, device_id_type=MESH)
     small_copy.start()
-    for step in range(2, lines - 1):
+    for step in range(3, lines - 1):
         hop_step(order[1], step)
     plane_sum("q")
-    for step in range(2, lines - 1):
+    for step in range(3, lines - 1):
         hop_step(order[2], step)
     plane_sum("kv")
 
@@ -1109,7 +1487,7 @@
             @pl.when(place_of(sign) >= 1)
             def _():
                 hop(which, sign, way, lines - 2).wait_recv()
-                came = recv_buf[which, way, lines - 3].astype(f32)
+                came = recv_buf[which, way, lines - 4].astype(f32)
                 total_buf[which] = (total_buf[which].astype(f32) + came).astype(bf16)
 
         for bits in range(1, PLANE):
@@ -1122,15 +1500,13 @@
             spread(which, bits).wait_send()
         spread_keep(which).wait()
         for sign, way in ways:
-            for step in range(1, lines - 1):
+            for step in range(2, lines - 1):
 
                 @pl.when(place_of(sign) <= step)
                 def _():
                     hop(which, sign, way, step).wait_send()
 
     for bits in range(1, PLANE):
-        y_copy(bits).wait_recv()
-        y_copy(bits).wait_send()
         small_plane_copy(bits).wait_send()
         for part in range(2):
             kv_copy(bits, part).wait_send()
@@ -1145,7 +1521,7 @@
     small_copy.wait_send()
 
 
-def finish(dkv, dq, cosines, sines, normed, first, out_part, x, gain_rows, gain_row, middle_grad, ff_parts, up, down, y_parts, lines, members, scale):
+def finish(dkv, dq, cosines, sines, normed, first, out_part, x, gain_rows, gain_row, middle_grad, ff_parts, up, down, lines, members, scale):
     bf16, f32 = jnp.bfloat16, jnp.float32
     half, width = x.shape
     local_tok = 2 * half
@@ -1167,10 +1543,9 @@
             jax.ShapeDtypeStruct((shard, 2 * q_width + 256), f32),
             jax.ShapeDtypeStruct((8, width), f32),
             jax.ShapeDtypeStruct((3, shard, PLANE * block), bf16),
-            jax.ShapeDtypeStruct((PLANE - 1, half, width), bf16),
         ),
-        in_specs=[anywhere] + [inside] * 5 + [anywhere] + [inside] * 4 + [anywhere] * 4,
-        out_specs=(inside, inside, inside, anywhere, anywhere),
+        in_specs=[anywhere] + [inside] * 5 + [anywhere] + [inside] * 4 + [anywhere] * 3,
+        out_specs=(inside, inside, inside, anywhere),
         scratch_shapes=[
             vmem(*pair), vmem(*pair), vmem(near, 2, *pair), vmem(*pair), vmem(*pair),
             vmem(local_tok, q_width + 256), vmem(lines, PLANE, shard, q_width), vmem(lines, PLANE, shard, 256), vmem(lines, shard, q_width),
@@ -1178,16 +1553,16 @@
             vmem(lines, shard, q_width), vmem(lines, shard, 256), vmem(lines, shard, q_width),
             vmem(lines - 1, shard, q_width), vmem(lines - 1, shard, 256), vmem(lines - 1, shard, q_width),
             vmem(half, width), vmem(half, width), wide(8, width), wide(8, width), wide(PLANE, 8, width), wide(lines, 8, width),
-            vmem(3, 2, slab_rows, block), vmem(3, 2, lines - 2, slab_rows, block), vmem(3, 2, slab_rows, block), vmem(3, slab_rows, block),
+            vmem(3, 2, slab_rows, block), vmem(3, 2, lines - 3, slab_rows, block), vmem(3, 2, slab_rows, block), vmem(3, slab_rows, block),
             dma((2,)), dma((near, 2)), dma((near, 2)), dma, dma,
             dma((3, near)), dma((3, near)), dma((3, lines - 1)), dma((3, lines - 1)), dma,
             dma, dma, dma((2,)), dma((near,)), dma((near,)), dma((lines - 1,)), dma((lines - 1,)),
-            dma((3, 2)), dma((3,)), dma((3, 2)), dma((3, 2, lines - 2)), dma((3, 2, lines - 2)), dma((3,)), dma((3, near)), dma((3, near)), dma((near,)), dma((near,)),
+            dma((3, 2)), dma((3,)), dma((3, 2)), dma((3, 2, lines - 3)), dma((3, 2, lines - 3)), dma((3,)), dma((3, near)), dma((3, near)),
         ],
         compiler_params=pltpu.CompilerParams(vmem_limit_bytes=62 << 20, collective_id=2, has_side_effects=True),
         name="back",
         cost_estimate=pl.CostEstimate(flops=6 * local_tok * width * (q_width + 256), bytes_accessed=40 << 20, transcendentals=0),
-    )(dkv, dq, cosines, sines, normed, first, out_part, x, gain_rows, gain_row, middle_grad, ff_parts, up, down, y_parts)
+    )(dkv, dq, cosines, sines, normed, first, out_part, x, gain_rows, gain_row, middle_grad, ff_parts, up, down)
 
 
 def swap(block, axis, count, bits):
@@ -1253,8 +1628,8 @@
     block1 = jnp.where(in_trunk, 2 * chunk + 1, slot)
     shift0 = jnp.where(in_trunk, block0 * KB - starts, jnp.where(is_leaf, -far, far))
     shift1 = block1 * KB - starts
-    zero = jnp.zeros_like(chunk)
-    return jnp.stack([chunk, block0, block1, shift0, shift1, zero, zero, zero], axis=1).reshape(-1)
+    hot = jnp.where(~in_trunk[:, None] & (block0[:, None] == places[None, :]), 1.0, 0.0)
+    return jnp.stack([shift0, shift1], axis=1).reshape(-1), hot.reshape(-1)
 
 
 def on_device(
@@ -1305,12 +1680,6 @@
         second = jnp.where(core == 0, other, mine)
         return jnp.concatenate([first, second], axis=0)
 
-    def to_tokens(values):
-        halves = values.reshape(2, half_tok, width)
-        mine = lax.dynamic_index_in_dim(halves, core, 0, keepdims=False)
-        theirs = lax.dynamic_index_in_dim(halves, 1 - core, 0, keepdims=False)
-        return mine + swap(theirs.astype(bf16), "tensor", 2, 1).astype(f32)
-
     blocked = lambda w: jnp.pad(w, ((0, 0), (0, PLANE * block - hidden))).reshape(shard, PLANE, block).transpose(1, 0, 2)
     ff_blocks = jnp.stack([blocked(gate_weight), blocked(up_weight), blocked(down_weight.T)])
     first_own = jnp.concatenate([query_weight, key_weight, value_weight], axis=1)
@@ -1325,43 +1694,30 @@
         [gains, jnp.pad(bias_row, ((0, 0), (0, width - bias_row.shape[1]))), jnp.zeros((13, width), bf16)], axis=0
     )
     cosines, sines = rope_tables(positions)
-    plan = attention_plan(segment_ids, parent_ids, dp_index, local_tok)
+    plan, hot = attention_plan(segment_ids, parent_ids, dp_index, local_tok)
     steps = lines - 3
     outs = front(ff_blocks, first_own, output_weight.T, extra, layer_input, cosines, sines, lines, members)
     slab, ups, downs = outs[0], list(outs[1 : 1 + steps]), list(outs[1 + steps : 1 + 2 * steps])
-    first_all, out_t, q_rot, tree, normed, rows = outs[1 + 2 * steps :]
+    late_up, late_down, first_all, out_t, q_rot, tree, normed, rows = outs[1 + 2 * steps :]
     gain_one, gain_two = rows[0:1], rows[1:2]
 
-    ups.append(lax.ppermute(ups[-1], "dp", line_route(1, lines - 3, lines - 2)))
-    downs.append(lax.ppermute(downs[-1], "dp", line_route(-1, lines - 3, lines - 2)))
-    cot_late = lax.optimization_barrier((out_cotangent, rows))[0]
-    cots = [out_cotangent] + [swap(cot_late, "dp", dp_size, bits) for bits in range(1, PLANE)]
-    attended, lse = attn_fwd(plan, q_rot, tree, scale)
-    input_wide = layer_input.astype(f32)
-    middle = input_wide + to_tokens(contract_cols(attended, out_t))
-    normed_two = (middle * rms_scale(middle) * gain_two).astype(bf16)
-
-    normed_two_grad, y_parts, ff_parts, top, bottom = feed_forward(
-        normed_two, cots, [slab] + ups + downs, lines
+    attended, lse, middle, normed_two, other, cot_came, *more = attend(
+        plan, hot, q_rot, tree, out_t, layer_input, rows, out_cotangent, ups[-1], downs[-1], late_up, late_down,
+        lines, members, scale,
     )
-    up_first = lax.ppermute(top, "dp", line_route(1, 0, 0))
-    down_first = lax.ppermute(bottom, "dp", line_route(-1, 0, 0))
-    norm_grad, gain_two_grad = norm_back(normed_two_grad, middle, gain_two)
-    middle_grad = out_cotangent.astype(f32) + norm_grad
-
-    branch_grad = by_core(middle_grad.astype(bf16))
-    out_part = contract_rows(branch_grad, attended).astype(bf16).reshape(lines, PLANE, shard, q_width)
-    attended_grad = matmul(branch_grad, out_t).astype(bf16)
-    dq, dtree = attn_bwd(plan, q_rot, attended_grad, attended, lse, tree, scale)
-    y_other = lax.optimization_barrier((swap(y_parts[1], "tensor", 2, 1), dq))[0]
-    y_sums = y_parts[0].astype(f32) + y_other.astype(f32)
-    y_low, dq = lax.optimization_barrier((y_sums.astype(bf16), dq))
-
-    input_grad, sums, small, ff_sums, y_came = finish(
-        dtree, dq, cosines, sines, normed, first_all, out_part, layer_input, gain_two_grad[None], gain_one,
-        middle_grad, ff_parts, up_first, down_first, y_low, lines, members, scale,
+
+    normed_two_grad, y_own, y_other, ff_parts, up_first, down_first = feed_forward(
+        normed_two, out_cotangent, cot_came, [slab] + ups + downs + [late_up, late_down] + more, lines
     )
-    layer_output = (middle + y_sums[0] + jnp.sum(y_came.astype(f32), axis=0)).astype(bf16)
+
+    dq, dtree, middle_grad, gain_two_grad, out_part, layer_output, up_next, down_next = attend_back(
+        plan, hot, q_rot, attended, lse, tree, other, out_t, normed_two_grad, middle, out_cotangent, rows, cosines, sines,
+        y_own, y_other, ff_parts, up_first, down_first, lines, members, scale,
+    )
+    input_grad, sums, small, ff_sums = finish(
+        dtree, dq, cosines, sines, normed, first_all, out_part, layer_input, gain_two_grad, gain_one,
+        middle_grad, ff_parts, up_next, down_next, lines, members, scale,
+    )
     ff_sums = ff_sums[:, :, :hidden].astype(f32)
     gains_out = lax.dynamic_slice(small[0:2], (0, dp_index * shard), (2, shard))
     bias_out = lax.dynamic_slice(

time: 692 us -> 614 us (0.89)
  waiting for transfers between devices: 61.4 us -> 0 us
  Pallas kernels: 528 us -> 578 us
  starting transfers between devices: 27.1 us -> 0 us
  other arithmetic: 35.7 us -> 11.2 us
  local copies, waits for them, and re-layouts: 23.8 us -> 14 us
  matrix products: 9.04 us -> 0 us
    pallas_call x2, Pallas kernels: 23.1 us -> 113 us  [the longest x1 68.3 us: attend_back(): pl.pallas_call(functools.partial(attend_back_kernel, lines=lines, members...]
    ppermute x10 -> x0, waiting for transfers between devices: 61.4 us -> none  [the longest x6 37.1 us: swap(): return lax.ppermute(block, axis, [(i, i ^ bits) for i in range(count)])]
    pallas_call x1, Pallas kernels: 191 us -> 142 us  [finish(): pl.pallas_call(functools.partial(back_kernel, lines=lines, members=member...]
    ppermute x10 -> x0, starting transfers between devices: 27.1 us -> none  [the longest x6 18.5 us: swap(): return lax.ppermute(block, axis, [(i, i ^ bits) for i in range(count)])]
    pallas_call x1, Pallas kernels: 143 us -> 153 us  [front(): pl.pallas_call(functools.partial(front_kernel, lines=lines, members=membe...]
    add x1 -> x0, other arithmetic: 9.22 us -> none  [on_device(): y_sums = y_parts[0].astype(f32) + y_other.astype(f32)]
    dot_general x3 -> x0, matrix products: 9.04 us -> none  [the longest x1 3.49 us: contract_rows(): lax.dot_general(left, right, (((0,), (0,)), ((), ())), preferred_element_...]
    convert_element_type x3 -> x0, other arithmetic: 7.38 us -> none  [the longest x1 3.14 us: on_device(): branch_grad = by_core(middle_grad.astype(bf16))]
  transfers between devices with their start and end apart: 10 -> 0, of which waited for: 3 -> 0; matrix products, arithmetic and copies ran while one was open for 4% -> 0% of each run, Pallas kernels for 3% -> 0%
where the time goes in v3:
time: 614 us; the launch traced here: 605 us
  Pallas kernels  578 us (94%)
  local copies, waits for them, and re-layouts  14 us (2%)
  other arithmetic  11.2 us (2%)
    pallas_call x1, Pallas kernels, feed_forward(): pl.pallas_call(functools.partial(ff_kernel, tile_h=tile_h, tile_n=tile_n,...  170 us
    pallas_call x1, Pallas kernels, front(): pl.pallas_call(functools.partial(front_kernel, lines=lines, members=membe...  153 us
    pallas_call x1, Pallas kernels, finish(): pl.pallas_call(functools.partial(back_kernel, lines=lines, members=member...  142 us
    pallas_call x1, Pallas kernels, attend_back(): pl.pallas_call(functools.partial(attend_back_kernel, lines=lines, members...  68.3 us
    pallas_call x1, Pallas kernels, attend(): pl.pallas_call(functools.partial(attend_kernel, lines=lines, members=memb...  44.6 us

profile of v3, /device:TPU:0, one launch (start us, length us, event | category | flops | bytes accessed | tf_op | source)
XLA Modules:
  0.0 604.9 jit_solution(14384943724552629854)
XLA Ops:
  0.7 0.9 dynamic_slice.9
  1.6 0.8 select_reduce_fusion.1
  4.4 0.7 pad_maximum_fusion.5
  5.2 0.7 pad_maximum_fusion.4
  6.2 0.7 fusion.4.refs_3_
  6.9 0.7 convert_element_type.12
  7.6 1.2 fusion
  8.8 1.1 pad_maximum_fusion.1
  10.2 0.9 copy-done.4
  11.3 1.9 pad_maximum_fusion.refs_0_
  13.2 0.7 pad_maximum_fusion.3.refs_1_
  13.9 153.5 %front.1 = (bf16[3,384,1152]{2,1,0:T(8,128)(2,1)}, bf16[3,384,1152]{2,1,0:T(8,128)(2,1)}, bf16[3,384,1152]{2,1,0:T(8,128)(2,1)}, bf16[2,384,1152]{2,1,0:T(8,128)...) custom-call(bf16[3,4,96,1152]{3,2,1,0:T(8,128)(2,1)} %pad_maximum_fu, ...), custom_call_target="tpu_custom_call" | custom-call | flops 2013265920 | bytes 31457280 | tf_op jit(solution)/shard_map/front/pallas_call | solution.py:795
  167.4 44.6 %attend.1 = (bf16[640,768]{1,0:T(8,128)(2,1)}, f32[5,8,768]{2,1,0:T(8,128)}, f32[320,1536]{1,0:T(8,128)}, bf16[320,1536]{1,0:T(8,128)(2,1)}, bf16[5,256,256]{2,1...) custom-call(s32[10]{0:T(128)} %reshape.235.info, ...), custom_call_target="tpu_custom_call" | custom-call | flops 4529848320 | bytes 12582912 | tf_op jit(solution)/shard_map/attend/pallas_call | solution.py:225
  212.0 169.7 %feed_forward.1 = (f32[320,1536]{1,0:T(8,128)}, bf16[4,320,1536]{2,1,0:T(8,128)(2,1)}, bf16[4,320,1536]{2,1,0:T(8,128)(2,1)}, bf16[3,4,384,1152]{3,2,1,0:T(8,128...) custom-call(bf16[320,1536]{1,0:T(8,128)(2,1)} %get-tuple-element.64.refs_0_, ...), custom_call_target="tpu_custom_call" | custom-call | flops 81537269760 | bytes 62914560 | tf_op jit(solution)/shard_map/feed_forward/pallas_call | solution.py:1150
  381.8 68.3 %attend_back.1 = (bf16[640,768]{1,0:T(8,128)(2,1)}, bf16[5120,256]{1,0:T(8,128)(2,1)}, f32[320,1536]{1,0:T(8,128)}, f32[1,1536]{1,0:T(1,128)}, bf16[4,4,96,768]{...) custom-call(s32[10]{0:T(128)} %reshape.235.info, ...), custom_call_target="tpu_custom_call" | custom-call | flops 11324620800 | bytes 31457280 | tf_op jit(solution)/shard_map/attend_back/pallas_call | solution.py:447
  450.1 1.4 slice.56.gain_row_in
  451.5 142.2 %back.1 = (bf16[320,1536]{1,0:T(8,128)(2,1)}, f32[96,1792]{1,0:T(8,128)}, f32[8,1536]{1,0:T(8,128)}, bf16[3,96,4608]{2,1,0:T(8,128)(2,1)}) custom-call(bf16[5120,256]{1,0:T(8,128)(2,1)} %get-tuple-element.79.dkv_in, bf16[640,768]{1,0:T(8,128)(2,1)} %get-tuple-element.80.dq_in, f32[640,128]{1,0:T(8,128)} %get-tuple-element.112.refs_5_.cos_in, ...), custom_call_target="tpu_custom_call" | custom-call | flops 6039797760 | bytes 41943040 | tf_op jit(solution)/shard_map/back/pallas_call | solution.py:1539
  593.8 2.1 slice_convert_fusion
  595.9 2.4 slice_bitcast_fusion
  598.3 0.8 slice_bitcast_fusion.3
  599.8 0.8 slice.57
  601.2 0.8 slice.60
  602.6 0.9 copy.54
  603.5 0.9 copy.55
  (49 shorter events, 4.6 us)
Async XLA Ops:
  0.6 9.3 %copy-start.2 = (bf16[96,4480]{1,0:T(8,128)(2,1)S(1)}, bf16[96,4480]{1,0:T(8,128)(2,1)}, u32[]{:S(2)}) copy-start(bf16[96,4480]{1,0:T(8,128)(2,1)} %param.32) | copy-start | bytes 2580484
  0.7 9.3 %copy-start.3 = (bf16[4480,96]{0,1:T(8,128)(2,1)S(1)}, bf16[4480,96]{0,1:T(8,128)(2,1)}, u32[]{:S(2)}) copy-start(bf16[4480,96]{0,1:T(8,128)(2,1)} %param.33) | copy-start | bytes 2580484
  10.0 1.2 copy-start.4
  11.3 1.9 copy-start.6
  11.3 1.9 copy-start.7
  11.3 1.9 copy-start.8
  595.9 2.5 copy-start.5
  595.9 6.7 %copy-start = (bf16[320,1536]{1,0:T(8,128)(2,1)S(1)}, bf16[320,1536]{1,0:T(8,128)(2,1)}, u32[]{:S(2)}) copy-start(bf16[320,1536]{1,0:T(8,128)(2,1)} %get-tuple-element.128) | copy-start | bytes 2949124
  598.3 5.2 copy-start.1
  602.0 2.4 copy-start.9

commit v4 on v3

--- a/solution.py
+++ b/solution.py
@@ -250,9 +250,9 @@
 def attend_back_kernel(
     info, hot, q_ref, att_ref, lse_ref, tree_ref, other_ref, out_t, dx_in, middle_in, cot_in, gain_in, cos_in, sin_in,
     y_own, y_other, ff_in, carried_up, carried_down,
-    dq_out, dtree_out, middle_grad_out, gain_out, part_out, layer_out, next_up, next_down,
-    sum_ref, parent_ref, branch, att_grad, y_sum, y_tmp, y_came, own_buf, sum_buf,
-    branch_send, branch_recv, y_load, y_send, y_recv, load_sem, hop_send, hop_recv,
+    dq_out, dtree_out, middle_grad_out, gain_out, line_out, layer_out, next_up, next_down,
+    part_out, part_came, sum_ref, parent_ref, branch, att_grad, y_sum, y_tmp, y_came, own_buf, sum_buf,
+    branch_send, branch_recv, y_load, y_send, y_recv, part_send, part_recv, load_sem, hop_send, hop_recv,
     *, lines, members, scale,
 ):
     bf16, f32 = jnp.bfloat16, jnp.float32
@@ -332,22 +332,48 @@
         device_id=mate, device_id_type=MESH)
     branch_copy.start()
 
-    def y_copy(bits):
-        return pltpu.make_async_remote_copy(
-            src_ref=y_sum.at[bits], dst_ref=y_came.at[bits - 1], send_sem=y_send.at[bits - 1], recv_sem=y_recv.at[bits - 1],
-            device_id=chip[bits], device_id_type=MESH)
-
-    for k in (1, 2, 3, 0):
+    quarter = lambda part: pl.ds(part * (half // 2), half // 2)
+
+    def across_copy(bits):
+        part = bits - 1
+        return pltpu.make_async_remote_copy(
+            src_ref=y_sum.at[3, quarter(part)], dst_ref=y_came.at[2, quarter(part)],
+            send_sem=y_send.at[0, part], recv_sem=y_recv.at[0, part], device_id=chip[bits], device_id_type=MESH)
+
+    def y_copy(bits, part):
+        return pltpu.make_async_remote_copy(
+            src_ref=y_sum.at[bits, quarter(part)], dst_ref=y_came.at[bits - 1, quarter(part)],
+            send_sem=y_send.at[bits, part], recv_sem=y_recv.at[bits, part], device_id=chip[bits], device_id_type=MESH)
+
+    for k in (3, 1, 2, 0):
         y_loads(k, lambda copy: copy.wait())
         y_sum[k] = (y_sum[k].astype(f32) + y_tmp[k].astype(f32)).astype(bf16)
-        if k:
-            y_copy(k).start()
+        if k == 3:
+            across_copy(1).start()
+            across_copy(2).start()
+        elif k:
+            y_copy(k, k - 1).start()
     branch_copy.wait_recv()
     att_grad[...] = dot_nn(branch[...], out_t[...]).astype(bf16)
     for z in range(lines):
         tile = dot_nn(branch[:, z * slab_rows : (z + 1) * slab_rows].T, att_ref[...]).astype(bf16)
         for j in range(PLANE):
             part_out[z, j] = tile[j * shard : (j + 1) * shard]
+
+    def part_copy(bits):
+        there = lax.rem(plane_partner(dp, bits), PLANE)
+        return pltpu.make_async_remote_copy(
+            src_ref=part_out.at[:, there], dst_ref=part_came.at[bits - 1],
+            send_sem=part_send.at[bits - 1], recv_sem=part_recv.at[bits - 1],
+            device_id=chip[bits], device_id_type=MESH)
+
+    for bits in (1, 2):
+        across_copy(bits).wait_recv()
+        at = quarter(bits - 1)
+        y_sum[PLANE - 1 - bits, at] = (y_sum[PLANE - 1 - bits, at].astype(f32) + y_came[2, at].astype(f32)).astype(bf16)
+        y_copy(PLANE - 1 - bits, bits - 1).start()
+    for bits in range(1, PLANE):
+        part_copy(bits).start()
 
     sum_ref[...] = jnp.zeros_like(sum_ref)
     cosines, sines = cos_in[...], sin_in[...]
@@ -412,14 +438,24 @@
         dtree_out[at, :] = total.astype(bf16)
 
     for bits in range(1, PLANE):
-        y_copy(bits).wait_recv()
-    total = middle_in[...] + y_sum[0].astype(f32)
-    for bits in range(1, PLANE):
-        total = total + y_came[bits - 1].astype(f32)
+        part_copy(bits).wait_recv()
+    for z in range(lines):
+        total = part_out[z, lax.rem(dp, PLANE)].astype(f32)
+        for bits in range(1, PLANE):
+            total = total + part_came[bits - 1, z].astype(f32)
+        line_out[z] = total.astype(bf16)
+    for bits in (1, 2):
+        for part in range(2):
+            y_copy(bits, part).wait_recv()
+    total = middle_in[...] + y_sum[0].astype(f32) + y_came[0].astype(f32) + y_came[1].astype(f32)
     layer_out[...] = total.astype(bf16)
     branch_copy.wait_send()
     for bits in range(1, PLANE):
-        y_copy(bits).wait_send()
+        part_copy(bits).wait_send()
+    for bits in (1, 2):
+        across_copy(bits).wait_send()
+        for part in range(2):
+            y_copy(bits, part).wait_send()
     for sign, way in ways:
 
         @pl.when(place_of(sign) <= 1)
@@ -451,18 +487,19 @@
             jax.ShapeDtypeStruct(tree.shape, bf16),
             jax.ShapeDtypeStruct((half, width), f32),
             jax.ShapeDtypeStruct((1, width), f32),
-            jax.ShapeDtypeStruct((lines, PLANE, shard, q_width), bf16),
+            jax.ShapeDtypeStruct((lines, shard, q_width), bf16),
             jax.ShapeDtypeStruct((half, width), bf16),
             slab, slab,
         ),
         in_specs=[pl.BlockSpec(memory_space=pltpu.SMEM)] * 2 + [inside] * 12 + [anywhere] * 5,
         out_specs=(inside,) * 6 + (anywhere,) * 2,
         scratch_shapes=[
+            pltpu.VMEM((lines, PLANE, shard, q_width), bf16), pltpu.VMEM((PLANE - 1, lines, shard, q_width), bf16),
             pltpu.VMEM(tree.shape, f32), pltpu.VMEM((local_tok // QB, KB, 256), f32),
             pltpu.VMEM((local_tok, width), bf16), pltpu.VMEM((local_tok, q_width), bf16),
             pltpu.VMEM((PLANE, half, width), bf16), pltpu.VMEM((PLANE, half, width), bf16), pltpu.VMEM((PLANE - 1, half, width), bf16),
             pltpu.VMEM((3, slab_rows, block), bf16), pltpu.VMEM((3, slab_rows, block), bf16),
-            dma, dma, dma((PLANE, 2)), dma((PLANE - 1,)), dma((PLANE - 1,)), dma((3, 2)), dma((3, 2)), dma((3, 2)),
+            dma, dma, dma((PLANE, 2)), dma((3, 2)), dma((3, 2)), dma((PLANE - 1,)), dma((PLANE - 1,)), dma((3, 2)), dma((3, 2)), dma((3, 2)),
         ],
         compiler_params=pltpu.CompilerParams(vmem_limit_bytes=62 << 20, collective_id=4, has_side_effects=True),
         name="attend_back",
@@ -833,10 +870,10 @@
     cots = [cot_in] + [cot_came.at[k] for k in range(PLANE - 1)]
     (
         dx_out, y_own, y_other, parts_out, carried_up, carried_down,
-        x_all, cot_all, gate_w, up_w, down_w, prod, gate_g, up_g, far, near, back, y_stage,
+        x_all, cot_all, gate_w, up_w, down_w, prod, gate_g, up_g, far, near, back, y_stage, stage,
         x_send, x_recv, half_send, half_recv, fwd_send, fwd_recv, pair_send, pair_recv, dx_send, dx_recv,
         x_load, cot_load, cot_send, cot_recv, weight_sem, hop_send, hop_recv, y_keep, y_send, y_recv,
-        out_sem, first_send, first_recv,
+        stage_sem, first_send, first_recv,
     ) = refs[10 + 2 * early :]
     bf16 = jnp.bfloat16
     half = x_in.shape[0]
@@ -852,8 +889,6 @@
     z_at = dp // PLANE
     slab_rows = width // lines
     weights = (gate_w, up_w, down_w)
-    grads_of = weights
-    down_y = down_w
     ways = ((1, 0), (-1, 1))
     place_of = lambda sign: z_at if sign == 1 else lines - 1 - z_at
     place_rows = lambda z: pl.ds(pl.multiple_of(z * slab_rows, slab_rows), slab_rows)
@@ -1028,7 +1063,7 @@
         @pl.loop(0, width // tile_n)
         def _(t):
             cols = pl.ds(pl.multiple_of(t * tile_n, tile_n), tile_n)
-            y_stage[:, cols] = dot_nt(prod[rows(k, 0, 2), :], down_y[cols, :]).astype(bf16)
+            y_stage[:, cols] = dot_nt(prod[rows(k, 0, 2), :], down_w[cols, :]).astype(bf16)
 
         y_local(k).start()
         y_copy(k).start()
@@ -1060,31 +1095,38 @@
     def first_hop(which, sign, way):
         at = pl.ds((lines - 1) * slab_rows if sign == 1 else 0, slab_rows)
         return pltpu.make_async_remote_copy(
-            src_ref=grads_of[which].at[at], dst_ref=(carried_up, carried_down)[way].at[which],
+            src_ref=parts_out.at[which, at], dst_ref=(carried_up, carried_down)[way].at[which],
             send_sem=first_send.at[which, way], recv_sem=first_recv.at[which, way],
             device_id={"dp": dp + sign * PLANE}, device_id_type=MESH)
 
-    def out_copies(which, act):
-        for z in range(lines):
-            at = pl.ds(z * slab_rows, slab_rows)
-            act(pltpu.make_async_copy(grads_of[which].at[at], parts_out.at[which, z], out_sem.at[which, z]))
+    tiles = width // tile_m
+
+    def stage_copy(which, m, slot):
+        at = pl.ds(pl.multiple_of(m * tile_m, tile_m), tile_m)
+        return pltpu.make_async_copy(stage.at[slot], parts_out.at[which, at], stage_sem.at[slot])
 
     def weight_grad(which, tokens, grad):
-        @pl.loop(0, width // tile_m)
+        @pl.loop(0, tiles)
         def _(m):
             at = pl.ds(pl.multiple_of(m * tile_m, tile_m), tile_m)
-            grads_of[which][at, :] = dot_nn(tokens[:, at].T, grad[...]).astype(bf16)
-
+            tile = dot_nn(tokens[:, at].T, grad[...]).astype(bf16)
+            slot = lax.rem(m, 2)
+
+            @pl.when(m >= 2)
+            def _():
+                stage_copy(which, m - 2, slot).wait()
+
+            stage[slot] = tile
+            stage_copy(which, m, slot).start()
+
+        for m in (tiles - 2, tiles - 1):
+            stage_copy(which, m, m % 2).wait()
         for sign, way in ways:
 
             @pl.when(place_of(sign) == 0)
             def _():
                 first_hop(which, sign, way).start()
 
-        out_copies(which, lambda copy: copy.start())
-
-    for k in range(PLANE):
-        y_part(k)
     weight_grad(2, cot_all, prod)
     dx_first(1)
     dx_first(2)
@@ -1096,6 +1138,8 @@
     dx_second(0)
     weight_grad(0, x_all, gate_g)
     weight_grad(1, x_all, up_g)
+    for k in range(PLANE):
+        y_part(k)
 
     for k in range(1, PLANE):
         dx_copy(k).wait_recv()
@@ -1118,7 +1162,6 @@
     for k in range(PLANE):
         y_copy(k).wait_recv()
     for which in range(3):
-        out_copies(which, lambda copy: copy.wait())
         for sign, way in ways:
             if which < 2:
 
@@ -1153,7 +1196,7 @@
             jax.ShapeDtypeStruct((half, width), jnp.float32),
             jax.ShapeDtypeStruct((PLANE, half, width), bf16),
             jax.ShapeDtypeStruct((PLANE, half, width), bf16),
-            jax.ShapeDtypeStruct((3, lines, slab_rows, block), bf16),
+            jax.ShapeDtypeStruct((3, width, block), bf16),
             slab,
             slab,
         ),
@@ -1164,10 +1207,10 @@
             pltpu.VMEM((width, block), bf16), pltpu.VMEM((width, block), bf16), pltpu.VMEM((width, block), bf16),
             pltpu.VMEM((tokens, block), bf16), pltpu.VMEM((tokens, block), bf16), pltpu.VMEM((tokens, block), bf16),
             pltpu.VMEM((PLANE, half, width), bf16), pltpu.VMEM((PLANE, half, width), bf16), pltpu.VMEM((PLANE - 1, half, width), bf16),
-            pltpu.VMEM((2 * half, width), bf16),
+            pltpu.VMEM((2 * half, width), bf16), pltpu.VMEM((2, tile_m, block), bf16),
             dma((PLANE - 1,)), dma((PLANE - 1,)), dma((2,)), dma((2,)), dma((PLANE - 1,)), dma((PLANE - 1,)), dma((PLANE,)), dma((PLANE,)),
             dma((PLANE - 1,)), dma((PLANE - 1,)), dma, dma((PLANE,)), dma((PLANE,)), dma((PLANE,)), dma((3, 2 * lines)), dma((3, 2)), dma((3, 2)), dma, dma((PLANE,)), dma((PLANE,)),
-            dma((3, lines)), dma((3, 2)), dma((3, 2)),
+            dma((2,)), dma((3, 2)), dma((3, 2)),
         ],
         compiler_params=pltpu.CompilerParams(vmem_limit_bytes=62 << 20, collective_id=0, has_side_effects=True),
         name="feed_forward",
@@ -1176,15 +1219,15 @@
 
 
 def back_kernel(
-    dkv_in, dq_in, cos_in, sin_in, normed_in, first_in, out_part, x_in, rows_in, gain_row_in, middle_grad_in,
+    dkv_in, dq_in, cos_in, sin_in, normed_in, first_in, line_o, x_in, rows_in, gain_row_in, middle_grad_in,
     ff_in, carried_up, carried_down,
     input_grad_out, sums_out, small_out, ff_out,
-    kv_own, kv_other, kv_plane, kv_merged, kv_line, grads, part_q, part_kv, own_o,
-    recv_q, recv_kv, recv_o, line_q, line_kv, line_o, from_q, from_kv, from_o,
+    kv_own, kv_other, kv_plane, kv_merged, kv_line, grads, part_q, part_kv,
+    recv_q, recv_kv, line_q, line_kv, from_q, from_kv, from_o,
     far, near, small_own, small_mate, small_plane, small_line,
     own_buf, recv_buf, first_buf, total_buf,
     kv_local, kv_send, kv_recv, kv_line_send, kv_line_recv,
-    plane_send, plane_recv, line_send, line_recv, own_o_sem,
+    plane_send, plane_recv, line_send, line_recv,
     mate_send, mate_recv, small_mate_sem, small_plane_send, small_plane_recv, small_line_send, small_line_recv,
     load_sem, own_sem, carry_sem, hop_send, hop_recv, spread_local, spread_send, spread_recv,
     *, lines, members, scale,
@@ -1216,8 +1259,6 @@
     ]
     for load in kv_loads:
         load.start()
-    o_load = pltpu.make_async_copy(out_part.at[:, j_at], own_o, own_o_sem)
-    o_load.start()
 
     def slab_load(which, sign, way, step):
         target = lines - 1 - step + place_of(sign)
@@ -1302,20 +1343,20 @@
         hop_step(which, 2)
 
     groups = {
-        "o": (0, out_part, own_o, recv_o, line_o, from_o, q_width + 256, q_width),
-        "q": (1, part_q, None, recv_q, line_q, from_q, 0, q_width),
-        "kv": (2, part_kv, None, recv_kv, line_kv, from_kv, q_width, 256),
+        "o": (0, None, None, line_o, from_o, q_width + 256, q_width),
+        "q": (1, part_q, recv_q, line_q, from_q, 0, q_width),
+        "kv": (2, part_kv, recv_kv, line_kv, from_kv, q_width, 256),
     }
 
     def plane_copy(name, bits):
-        index, part, _, recv, *_ = groups[name]
+        index, part, recv, *_ = groups[name]
         return pltpu.make_async_remote_copy(
             src_ref=part.at[:, there[bits]], dst_ref=recv.at[bits - 1],
             send_sem=plane_send.at[index, bits - 1], recv_sem=plane_recv.at[index, bits - 1],
             device_id=chip[bits], device_id_type=MESH)
 
     def line_copy(name, apart):
-        index, _, _, _, line, came, *_ = groups[name]
+        index, _, _, line, came, *_ = groups[name]
         target = lax.rem(z_at + apart, lines)
         return pltpu.make_async_remote_copy(
             src_ref=line.at[target], dst_ref=came.at[apart - 1],
@@ -1327,14 +1368,17 @@
             plane_copy(name, bits).start()
 
     def plane_sum(name):
-        _, part, own, recv, line, *_ = groups[name]
+        _, part, recv, line, *_ = groups[name]
         for bits in range(1, PLANE):
             plane_copy(name, bits).wait_recv()
         for z in range(lines):
-            total = (part[z, j_at] if own is None else own[z]).astype(f32)
+            total = part[z, j_at].astype(f32)
             for bits in range(1, PLANE):
                 total = total + recv[bits - 1, z].astype(f32)
             line[z] = total.astype(bf16)
+        line_start(name)
+
+    def line_start(name):
         for apart in range(1, lines):
             line_copy(name, apart).start()
 
@@ -1347,7 +1391,7 @@
             total = total + came[apart - 1].astype(f32)
         sums_out[:, at : at + size] = total
 
-    plane_start("o")
+    line_start("o")
     cosines, sines = cos_in[...], sin_in[...]
 
     def turned_back(part):
@@ -1363,7 +1407,36 @@
                 part[z, j] = tile[j * shard : (j + 1) * shard]
 
     weight_part(part_q, 0, q_width)
-    plane_start("q")
+
+    columns = lambda j: pl.ds(pl.multiple_of(j * block, block), block)
+
+    def spread(which, bits):
+        rows = pl.ds(pl.multiple_of(there[bits] * shard, shard), shard)
+        return pltpu.make_async_remote_copy(
+            src_ref=total_buf.at[which, rows], dst_ref=ff_out.at[which, :, columns(j_at)],
+            send_sem=spread_send.at[which, bits - 1], recv_sem=spread_recv.at[which, bits - 1],
+            device_id=chip[bits], device_id_type=MESH)
+
+    def spread_keep(which):
+        rows = pl.ds(pl.multiple_of(j_at * shard, shard), shard)
+        return pltpu.make_async_copy(
+            total_buf.at[which, rows], ff_out.at[which, :, columns(j_at)], spread_local.at[which])
+
+    def line_done(which):
+        for step in range(3, lines - 1):
+            hop_step(which, step)
+        own_load(which).wait()
+        for sign, way in ways:
+
+            @pl.when(place_of(sign) >= 1)
+            def _():
+                hop(which, sign, way, lines - 2).wait_recv()
+                came = recv_buf[which, way, lines - 4].astype(f32)
+                total_buf[which] = (total_buf[which].astype(f32) + came).astype(bf16)
+
+        for bits in range(1, PLANE):
+            spread(which, bits).start()
+        spread_keep(which).start()
 
     for load in kv_loads:
         load.wait()
@@ -1377,8 +1450,8 @@
         src_ref=kv_merged, dst_ref=kv_line, send_sem=kv_line_send, recv_sem=kv_line_recv,
         device_id={"dp": line_partner(dp)}, device_id_type=MESH)
     kv_across.start()
-    for step in range(3, lines - 1):
-        hop_step(order[0], step)
+    plane_start("q")
+    line_done(2)
     for bits in range(1, PLANE):
         kv_copy(bits, 0).wait_recv()
     kv_across.wait_recv()
@@ -1399,8 +1472,7 @@
         src_ref=far, dst_ref=near, send_sem=mate_send, recv_sem=mate_recv, device_id=mate, device_id_type=MESH)
     mate_copy.start()
     mine = normed_grad(core)
-    o_load.wait()
-    plane_sum("o")
+    line_done(0)
     mate_copy.wait_recv()
     mine = mine + near[...].astype(f32)
     wide = x_in[...].astype(f32)
@@ -1423,12 +1495,9 @@
         src_ref=small_own, dst_ref=small_mate, send_sem=small_mate_sem.at[0], recv_sem=small_mate_sem.at[1],
         device_id=mate, device_id_type=MESH)
     small_copy.start()
-    for step in range(3, lines - 1):
-        hop_step(order[1], step)
     plane_sum("q")
-    for step in range(3, lines - 1):
-        hop_step(order[2], step)
     plane_sum("kv")
+    line_done(1)
 
     small_copy.wait_recv()
     gain_rows = lax.broadcasted_iota(jnp.int32, (8, width), 0) < 2
@@ -1466,34 +1535,6 @@
         total = total + small_line[apart]
     small_out[...] = total
 
-    columns = lambda j: pl.ds(pl.multiple_of(j * block, block), block)
-
-    def spread(which, bits):
-        rows = pl.ds(pl.multiple_of(there[bits] * shard, shard), shard)
-        return pltpu.make_async_remote_copy(
-            src_ref=total_buf.at[which, rows], dst_ref=ff_out.at[which, :, columns(j_at)],
-            send_sem=spread_send.at[which, bits - 1], recv_sem=spread_recv.at[which, bits - 1],
-            device_id=chip[bits], device_id_type=MESH)
-
-    def spread_keep(which):
-        rows = pl.ds(pl.multiple_of(j_at * shard, shard), shard)
-        return pltpu.make_async_copy(
-            total_buf.at[which, rows], ff_out.at[which, :, columns(j_at)], spread_local.at[which])
-
-    for which in order:
-        own_load(which).wait()
-        for sign, way in ways:
-
-            @pl.when(place_of(sign) >= 1)
-            def _():
-                hop(which, sign, way, lines - 2).wait_recv()
-                came = recv_buf[which, way, lines - 4].astype(f32)
-                total_buf[which] = (total_buf[which].astype(f32) + came).astype(bf16)
-
-        for bits in range(1, PLANE):
-            spread(which, bits).start()
-        spread_keep(which).start()
-
     for which in order:
         for bits in range(1, PLANE):
             spread(which, bits).wait_recv()
@@ -1510,7 +1551,7 @@
         small_plane_copy(bits).wait_send()
         for part in range(2):
             kv_copy(bits, part).wait_send()
-        for name in groups:
+        for name in ("q", "kv"):
             plane_copy(name, bits).wait_send()
     for apart in range(1, lines):
         small_line_copy(apart).wait_send()
@@ -1521,7 +1562,7 @@
     small_copy.wait_send()
 
 
-def finish(dkv, dq, cosines, sines, normed, first, out_part, x, gain_rows, gain_row, middle_grad, ff_parts, up, down, lines, members, scale):
+def finish(dkv, dq, cosines, sines, normed, first, line_o, x, gain_rows, gain_row, middle_grad, ff_parts, up, down, lines, members, scale):
     bf16, f32 = jnp.bfloat16, jnp.float32
     half, width = x.shape
     local_tok = 2 * half
@@ -1544,25 +1585,25 @@
             jax.ShapeDtypeStruct((8, width), f32),
             jax.ShapeDtypeStruct((3, shard, PLANE * block), bf16),
         ),
-        in_specs=[anywhere] + [inside] * 5 + [anywhere] + [inside] * 4 + [anywhere] * 3,
+        in_specs=[anywhere] + [inside] * 10 + [anywhere] * 3,
         out_specs=(inside, inside, inside, anywhere),
         scratch_shapes=[
             vmem(*pair), vmem(*pair), vmem(near, 2, *pair), vmem(*pair), vmem(*pair),
-            vmem(local_tok, q_width + 256), vmem(lines, PLANE, shard, q_width), vmem(lines, PLANE, shard, 256), vmem(lines, shard, q_width),
-            vmem(near, lines, shard, q_width), vmem(near, lines, shard, 256), vmem(near, lines, shard, q_width),
-            vmem(lines, shard, q_width), vmem(lines, shard, 256), vmem(lines, shard, q_width),
+            vmem(local_tok, q_width + 256), vmem(lines, PLANE, shard, q_width), vmem(lines, PLANE, shard, 256),
+            vmem(near, lines, shard, q_width), vmem(near, lines, shard, 256),
+            vmem(lines, shard, q_width), vmem(lines, shard, 256),
             vmem(lines - 1, shard, q_width), vmem(lines - 1, shard, 256), vmem(lines - 1, shard, q_width),
             vmem(half, width), vmem(half, width), wide(8, width), wide(8, width), wide(PLANE, 8, width), wide(lines, 8, width),
             vmem(3, 2, slab_rows, block), vmem(3, 2, lines - 3, slab_rows, block), vmem(3, 2, slab_rows, block), vmem(3, slab_rows, block),
             dma((2,)), dma((near, 2)), dma((near, 2)), dma, dma,
-            dma((3, near)), dma((3, near)), dma((3, lines - 1)), dma((3, lines - 1)), dma,
+            dma((3, near)), dma((3, near)), dma((3, lines - 1)), dma((3, lines - 1)),
             dma, dma, dma((2,)), dma((near,)), dma((near,)), dma((lines - 1,)), dma((lines - 1,)),
             dma((3, 2)), dma((3,)), dma((3, 2)), dma((3, 2, lines - 3)), dma((3, 2, lines - 3)), dma((3,)), dma((3, near)), dma((3, near)),
         ],
         compiler_params=pltpu.CompilerParams(vmem_limit_bytes=62 << 20, collective_id=2, has_side_effects=True),
         name="back",
         cost_estimate=pl.CostEstimate(flops=6 * local_tok * width * (q_width + 256), bytes_accessed=40 << 20, transcendentals=0),
-    )(dkv, dq, cosines, sines, normed, first, out_part, x, gain_rows, gain_row, middle_grad, ff_parts, up, down)
+    )(dkv, dq, cosines, sines, normed, first, line_o, x, gain_rows, gain_row, middle_grad, ff_parts, up, down)
 
 
 def swap(block, axis, count, bits):
@@ -1710,12 +1751,14 @@
         normed_two, out_cotangent, cot_came, [slab] + ups + downs + [late_up, late_down] + more, lines
     )
 
-    dq, dtree, middle_grad, gain_two_grad, out_part, layer_output, up_next, down_next = attend_back(
+    ff_parts = ff_parts.reshape(3, lines, width // lines, block)
+
+    dq, dtree, middle_grad, gain_two_grad, line_o, layer_output, up_next, down_next = attend_back(
         plan, hot, q_rot, attended, lse, tree, other, out_t, normed_two_grad, middle, out_cotangent, rows, cosines, sines,
         y_own, y_other, ff_parts, up_first, down_first, lines, members, scale,
     )
     input_grad, sums, small, ff_sums = finish(
-        dtree, dq, cosines, sines, normed, first_all, out_part, layer_input, gain_two_grad, gain_one,
+        dtree, dq, cosines, sines, normed, first_all, line_o, layer_input, gain_two_grad, gain_one,
         middle_grad, ff_parts, up_next, down_next, lines, members, scale,
     )
     ff_sums = ff_sums[:, :, :hidden].astype(f32)

time: 614 us -> 580 us (0.945)
  Pallas kernels: 578 us -> 545 us
    pallas_call x1, Pallas kernels: 142 us -> 123 us  [finish(): pl.pallas_call(functools.partial(back_kernel, lines=lines, members=member...]
    pallas_call x1, Pallas kernels: 170 us -> 153 us  [feed_forward(): pl.pallas_call(functools.partial(ff_kernel, tile_h=tile_h, tile_n=tile_n,...]
where the time goes in v4:
time: 580 us; the launch traced here: 572 us
  Pallas kernels  545 us (94%)
  local copies, waits for them, and re-layouts  14 us (2%)
  other arithmetic  11.2 us (2%)
    pallas_call x1, Pallas kernels, front(): pl.pallas_call(functools.partial(front_kernel, lines=lines, members=membe...  153 us
    pallas_call x1, Pallas kernels, feed_forward(): pl.pallas_call(functools.partial(ff_kernel, tile_h=tile_h, tile_n=tile_n,...  153 us
    pallas_call x1, Pallas kernels, finish(): pl.pallas_call(functools.partial(back_kernel, lines=lines, members=member...  123 us
    pallas_call x1, Pallas kernels, attend_back(): pl.pallas_call(functools.partial(attend_back_kernel, lines=lines, members...  71.6 us
    pallas_call x1, Pallas kernels, attend(): pl.pallas_call(functools.partial(attend_kernel, lines=lines, members=memb...  44.6 us

profile of v4, /device:TPU:0, one launch (start us, length us, event | category | flops | bytes accessed | tf_op | source)
XLA Modules:
  0.0 571.7 jit_solution(15801453275085500236)
XLA Ops:
  0.7 0.9 dynamic_slice.9
  1.6 0.8 select_reduce_fusion.1
  4.4 0.7 pad_maximum_fusion.5
  5.2 0.7 pad_maximum_fusion.4
  6.2 0.7 fusion.4.refs_3_
  6.9 0.7 convert_element_type.12
  7.6 1.2 fusion
  8.8 1.1 pad_maximum_fusion.1
  10.2 0.9 copy-done.4
  11.3 1.9 pad_maximum_fusion.refs_0_
  13.2 0.7 pad_maximum_fusion.3.refs_1_
  13.9 153.5 %front.1 = (bf16[3,384,1152]{2,1,0:T(8,128)(2,1)}, bf16[3,384,1152]{2,1,0:T(8,128)(2,1)}, bf16[3,384,1152]{2,1,0:T(8,128)(2,1)}, bf16[2,384,1152]{2,1,0:T(8,128)...) custom-call(bf16[3,4,96,1152]{3,2,1,0:T(8,128)(2,1)} %pad_maximum_fu, ...), custom_call_target="tpu_custom_call" | custom-call | flops 2013265920 | bytes 31457280 | tf_op jit(solution)/shard_map/front/pallas_call | solution.py:832
  167.4 44.6 %attend.1 = (bf16[640,768]{1,0:T(8,128)(2,1)}, f32[5,8,768]{2,1,0:T(8,128)}, f32[320,1536]{1,0:T(8,128)}, bf16[320,1536]{1,0:T(8,128)(2,1)}, bf16[5,256,256]{2,1...) custom-call(s32[10]{0:T(128)} %reshape.238.info, ...), custom_call_target="tpu_custom_call" | custom-call | flops 4529848320 | bytes 12582912 | tf_op jit(solution)/shard_map/attend/pallas_call | solution.py:225
  212.0 152.8 %feed_forward.1 = (f32[320,1536]{1,0:T(8,128)}, bf16[4,320,1536]{2,1,0:T(8,128)(2,1)}, bf16[4,320,1536]{2,1,0:T(8,128)(2,1)}, bf16[3,1536,1152]{2,1,0:T(8,128)(2...) custom-call(bf16[320,1536]{1,0:T(8,128)(2,1)} %get-tuple-element.64.refs_0_, bf16[320,1536]{1,0:T(8,128)(2,1)} %cot_in.3, ...), custom_call_target="tpu_custom_call" | custom-call | flops 81537269760 | bytes 62914560 | tf_op jit(solution)/shard_map/feed_forward/pallas_call | solution.py:1193
  364.8 71.6 %attend_back.1 = (bf16[640,768]{1,0:T(8,128)(2,1)}, bf16[5120,256]{1,0:T(8,128)(2,1)}, f32[320,1536]{1,0:T(8,128)}, f32[1,1536]{1,0:T(1,128)}, bf16[4,96,768]{2,...) custom-call(s32[10]{0:T(128)} %reshape.238.info, ...), custom_call_target="tpu_custom_call" | custom-call | flops 11324620800 | bytes 31457280 | tf_op jit(solution)/shard_map/attend_back/pallas_call | solution.py:483
  436.4 1.4 slice.56.gain_row_in
  437.8 122.8 %back.1 = (bf16[320,1536]{1,0:T(8,128)(2,1)}, f32[96,1792]{1,0:T(8,128)}, f32[8,1536]{1,0:T(8,128)}, bf16[3,96,4608]{2,1,0:T(8,128)(2,1)}) custom-call(bf16[5120,256]{1,0:T(8,128)(2,1)} %get-tuple-element.79.dkv_in, bf16[640,768]{1,0:T(8,128)(2,1)} %get-tuple-element.80.dq_in, f32[640,128]{1,0:T(8,128)} %get-tuple-element.112.refs_5_.cos_in, ...), custom_call_target="tpu_custom_call" | custom-call | flops 6039797760 | bytes 41943040 | tf_op jit(solution)/shard_map/back/pallas_call | solution.py:1580
  560.5 2.1 slice_convert_fusion
  562.6 2.4 slice_bitcast_fusion
  565.1 0.8 slice_bitcast_fusion.3
  566.6 0.8 slice.57
  568.0 0.8 slice.60
  569.3 0.9 copy.54
  570.3 0.9 copy.55
  (49 shorter events, 4.6 us)
Async XLA Ops:
  0.6 9.3 %copy-start.2 = (bf16[96,4480]{1,0:T(8,128)(2,1)S(1)}, bf16[96,4480]{1,0:T(8,128)(2,1)}, u32[]{:S(2)}) copy-start(bf16[96,4480]{1,0:T(8,128)(2,1)} %param.32) | copy-start | bytes 2580484
  0.7 9.3 %copy-start.3 = (bf16[4480,96]{0,1:T(8,128)(2,1)S(1)}, bf16[4480,96]{0,1:T(8,128)(2,1)}, u32[]{:S(2)}) copy-start(bf16[4480,96]{0,1:T(8,128)(2,1)} %param.33) | copy-start | bytes 2580484
  10.0 1.2 copy-start.4
  11.3 1.9 copy-start.6
  11.3 1.9 copy-start.7
  11.3 1.9 copy-start.8
  562.6 2.5 copy-start.5
  562.6 6.7 %copy-start = (bf16[320,1536]{1,0:T(8,128)(2,1)S(1)}, bf16[320,1536]{1,0:T(8,128)(2,1)}, u32[]{:S(2)}) copy-start(bf16[320,1536]{1,0:T(8,128)(2,1)} %get-tuple-element.128) | copy-start | bytes 2949124
  565.1 5.2 copy-start.1
  568.8 2.4 copy-start.9

commit v5 on v4

--- a/solution.py
+++ b/solution.py
@@ -597,9 +597,9 @@
 
 def front_kernel(*refs, lines, members, steps):
     (
-        ff_in, first_in, out_in, extra_in, x_in, cos_in, sin_in,
+        gate_in, up_in, down_in, first_in, out_in, extra_in, x_in, cos_in, sin_in,
         own_out, *slab_outs,
-    ) = refs[: 8 + 2 * steps]
+    ) = refs[: 10 + 2 * steps]
     (
         late_up, late_down, first_out, out_t, q_out, tree_out, normed_out, rows_out,
         first_all, extra_all, x_all, normed, pair,
@@ -608,7 +608,7 @@
         out_local, out_ls, out_lr, out_ps, out_pr,
         spread_local, spread_send, spread_recv, hop_send, hop_recv,
         x_local, x_send, x_recv, keep_sem, pair_local, pair_send, pair_recv, late_send, late_recv,
-    ) = refs[8 + 2 * steps :]
+    ) = refs[10 + 2 * steps :]
     bf16, f32 = jnp.bfloat16, jnp.float32
     dp = lax.axis_index("dp")
     core = lax.axis_index("tensor")
@@ -632,15 +632,49 @@
         device_id=mate, device_id_type=MESH)
     shard_rows = lambda j: pl.ds(pl.multiple_of(j * shard, shard), shard)
 
-    def spread(which, bits):
-        there = lax.rem(plane_partner(dp, bits), PLANE)
-        return pltpu.make_async_remote_copy(
-            src_ref=ff_in.at[which, there], dst_ref=own_out.at[which, shard_rows(j_at)],
+    block = own_out.shape[-1]
+    last = gate_in.shape[1] - (PLANE - 1) * block
+
+    def by_width(owner, act):
+        @pl.when(owner < PLANE - 1)
+        def _():
+            act(block)
+
+        @pl.when(owner == PLANE - 1)
+        def _():
+            act(last)
+
+    def piece(which, owner, size):
+        at = pl.ds(pl.multiple_of(owner * block, 128), size)
+        return (gate_in, up_in, down_in)[which].at[:, at], own_out.at[which, shard_rows(j_at), pl.ds(0, size)]
+
+    def spread(which, bits, owner, size):
+        src, dst = piece(which, owner, size)
+        return pltpu.make_async_remote_copy(
+            src_ref=src, dst_ref=dst,
             send_sem=spread_send.at[which, bits - 1], recv_sem=spread_recv.at[which, bits - 1],
             device_id={"dp": plane_partner(dp, bits)}, device_id_type=MESH)
 
-    def spread_keep(which):
-        return pltpu.make_async_copy(ff_in.at[which, j_at], own_out.at[which, shard_rows(j_at)], spread_local.at[which])
+    def spread_start(which):
+        for bits in range(1, PLANE):
+            owner = lax.rem(plane_partner(dp, bits), PLANE)
+            by_width(owner, lambda size: spread(which, bits, owner, size).start())
+
+    def spread_wait_send(which):
+        for bits in range(1, PLANE):
+            owner = lax.rem(plane_partner(dp, bits), PLANE)
+            by_width(owner, lambda size: spread(which, bits, owner, size).wait_send())
+
+    def spread_wait_recv(which):
+        for bits in range(1, PLANE):
+            by_width(j_at, lambda size: spread(which, bits, j_at, size).wait_recv())
+
+    def spread_keep(which, act):
+        def with_size(size):
+            src, dst = piece(which, j_at, size)
+            act(pltpu.make_async_copy(src, dst, spread_local.at[which]))
+
+        by_width(j_at, with_size)
 
     def hop(which, sign, step):
         way = (1 - sign) // 2
@@ -662,19 +696,17 @@
         one.local().start()
     x_keep.start()
     for which in range(3):
-        spread_keep(which).start()
+        spread_keep(which, lambda copy: copy.start())
     greet(dp, core, lines)
     x_copy.start()
     for sign in (1, -1):
         first.line_start(sign, 0)
         extra.line_start(sign, 0)
-    for bits in range(1, PLANE):
-        spread(2, bits).start()
+    spread_start(2)
     first.plane_start_own()
     extra.plane_start_own()
     for which in (0, 1):
-        for bits in range(1, PLANE):
-            spread(which, bits).start()
+        spread_start(which)
 
     x_keep.wait()
     x_copy.wait_recv()
@@ -682,9 +714,8 @@
     scale = lax.rsqrt(jnp.mean(wide * wide, axis=1, keepdims=True) + EPS)
 
     def hop_start(which):
-        spread_keep(which).wait()
-        for bits in range(1, PLANE):
-            spread(which, bits).wait_recv()
+        spread_keep(which, lambda copy: copy.wait())
+        spread_wait_recv(which)
         for sign in (1, -1):
             place = z_at if sign == 1 else lines - 1 - z_at
 
@@ -804,8 +835,7 @@
         if bits:
             pair_copy(bits, True).wait_send()
     for which in range(3):
-        for bits in range(1, PLANE):
-            spread(which, bits).wait_send()
+        spread_wait_send(which)
         for sign in (1, -1):
             for step in range(steps):
                 place = z_at if sign == 1 else lines - 1 - z_at
@@ -815,12 +845,12 @@
                     hop(which, sign, step).wait_send()
 
 
-def front(ff_blocks, first, out_t, extra, x, cosines, sines, lines, members):
+def front(gate, up, down, first, out_t, extra, x, cosines, sines, lines, members):
     bf16, f32 = jnp.bfloat16, jnp.float32
     half, width = x.shape
     local_tok = 2 * half
     shard, columns = first.shape
-    block = ff_blocks.shape[-1]
+    block = -(-gate.shape[1] // (PLANE * 128)) * 128
     q_width = out_t.shape[1]
     count = lines * PLANE
     steps = max(lines - 3, 1)
@@ -841,7 +871,7 @@
             jax.ShapeDtypeStruct((local_tok, width), bf16),
             jax.ShapeDtypeStruct((16, width), f32),
         ),
-        in_specs=[anywhere] * 5 + [inside] * 2,
+        in_specs=[anywhere] * 7 + [inside] * 2,
         out_specs=(anywhere,) * (3 + 2 * steps) + (anywhere, anywhere, inside, anywhere, inside, inside),
         scratch_shapes=[
             pltpu.VMEM((width, columns), bf16), pltpu.VMEM((16 * count, width), bf16),
@@ -857,11 +887,11 @@
         compiler_params=pltpu.CompilerParams(vmem_limit_bytes=56 << 20, collective_id=1, has_side_effects=True),
         name="front",
         cost_estimate=pl.CostEstimate(flops=2 * local_tok * width * columns, bytes_accessed=30 << 20, transcendentals=0),
-    )(ff_blocks, first, out_t, extra, x, cosines, sines)
+    )(gate, up, down, first, out_t, extra, x, cosines, sines)
 
 
 def ff_kernel(
-    *refs, tile_h, tile_n, tile_m, lines,
+    *refs, tile_h, tile_n, tile_m, lines, hidden,
 ):
     early = lines - 3
     x_in, cot_in, cot_came, slab = refs[:4]
@@ -879,7 +909,6 @@
     half = x_in.shape[0]
     width = x_in.shape[1]
     block = gate_w.shape[1]
-    chunk = 2 * half
     dp = lax.axis_index("dp")
     core = lax.axis_index("tensor")
     chip = [None] + [{"dp": plane_partner(dp, bits)} for bits in range(1, PLANE)]
@@ -928,6 +957,13 @@
             @pl.when(place_of(sign) == lines - 1)
             def _():
                 last_hop(which, sign, way).wait_recv()
+
+        last = hidden - (PLANE - 1) * block
+        if last < block:
+
+            @pl.when(lax.rem(dp, PLANE) == PLANE - 1)
+            def _():
+                weights[which][:, last:] = jnp.zeros((width, block - last), bf16)
 
     x_keep = pltpu.make_async_copy(x_in, x_all.at[rows(0, 0)], x_load)
     x_keep.start()
@@ -993,37 +1029,37 @@
         cot_copy(k).wait_recv()
     weight_wait(2)
 
-    @pl.loop(0, PLANE)
+    starts = list(range(0, max(block - 1023, 0), tile_h)) or [0]
+    if block - starts[-1] >= 2 * tile_h:
+        starts.append(starts[-1] + tile_h)
+    cuts = [pl.ds(at, end - at) for at, end in zip(starts, starts[1:] + [block])]
+
+    @pl.loop(0, 2 * PLANE)
     def _(k):
-        at = pl.ds(pl.multiple_of(k * chunk, chunk), chunk)
-
-        @pl.loop(0, block // tile_h)
-        def _(t):
-            cols = pl.ds(pl.multiple_of(t * tile_h, tile_h), tile_h)
+        at = pl.ds(pl.multiple_of(k * half, half), half)
+        for cols in cuts:
             up_g[at, cols] = dot_nn(cot_all[at, :], down_w[:, cols]).astype(bf16)
 
     def gate_part(k):
-        at = rows(k, 0, 2)
-
-        @pl.loop(0, block // tile_h)
-        def _(t):
-            cols = pl.ds(pl.multiple_of(t * tile_h, tile_h), tile_h)
-            gate_g[at, cols] = dot_nn(x_all[at, :], gate_w[:, cols]).astype(bf16)
+        @pl.loop(0, 2)
+        def _(r):
+            at = pl.ds(pl.multiple_of(2 * k * half + r * half, half), half)
+            for cols in cuts:
+                gate_g[at, cols] = dot_nn(x_all[at, :], gate_w[:, cols]).astype(bf16)
 
     def up_part(k):
-        at = rows(k, 0, 2)
-
-        @pl.loop(0, block // tile_h)
-        def _(t):
-            cols = pl.ds(pl.multiple_of(t * tile_h, tile_h), tile_h)
-            up = dot_nn(x_all[at, :], up_w[:, cols])
-            gate = gate_g[at, cols].astype(jnp.float32)
-            pg = up_g[at, cols].astype(jnp.float32)
-            sig = 0.5 * jnp.tanh(0.5 * gate) + 0.5
-            silu = gate * sig
-            prod[at, cols] = (silu * up).astype(bf16)
-            up_g[at, cols] = (pg * silu).astype(bf16)
-            gate_g[at, cols] = (pg * up * (sig + silu * (1.0 - sig))).astype(bf16)
+        @pl.loop(0, 2)
+        def _(r):
+            at = pl.ds(pl.multiple_of(2 * k * half + r * half, half), half)
+            for cols in cuts:
+                up = dot_nn(x_all[at, :], up_w[:, cols])
+                gate = gate_g[at, cols].astype(jnp.float32)
+                pg = up_g[at, cols].astype(jnp.float32)
+                sig = 0.5 * jnp.tanh(0.5 * gate) + 0.5
+                silu = gate * sig
+                prod[at, cols] = (silu * up).astype(bf16)
+                up_g[at, cols] = (pg * silu).astype(bf16)
+                gate_g[at, cols] = (pg * up * (sig + silu * (1.0 - sig))).astype(bf16)
 
     def dx_half(k, r):
         at = rows(k, r)
@@ -1128,6 +1164,7 @@
                 first_hop(which, sign, way).start()
 
     weight_grad(2, cot_all, prod)
+    weight_grad(0, x_all, gate_g)
     dx_first(1)
     dx_first(2)
     dx_second(1)
@@ -1136,7 +1173,6 @@
     dx_first(0)
     dx_second(3)
     dx_second(0)
-    weight_grad(0, x_all, gate_g)
     weight_grad(1, x_all, up_g)
     for k in range(PLANE):
         y_part(k)
@@ -1181,7 +1217,7 @@
         cot_copy(k).wait_send()
 
 
-def feed_forward(x, cot, cot_came, slabs, lines, tile_h=384, tile_n=512, tile_m=256):
+def feed_forward(x, cot, cot_came, slabs, lines, hidden, tile_h=512, tile_n=768, tile_m=256):
     half, width = x.shape
     block = slabs[0].shape[-1]
     slab_rows = width // lines
@@ -1191,7 +1227,7 @@
     dma = pltpu.SemaphoreType.DMA
     slab = jax.ShapeDtypeStruct((3, slab_rows, block), bf16)
     return pl.pallas_call(
-        functools.partial(ff_kernel, tile_h=tile_h, tile_n=tile_n, tile_m=tile_m, lines=lines),
+        functools.partial(ff_kernel, tile_h=tile_h, tile_n=tile_n, tile_m=tile_m, lines=lines, hidden=hidden),
         out_shape=(
             jax.ShapeDtypeStruct((half, width), jnp.float32),
             jax.ShapeDtypeStruct((PLANE, half, width), bf16),
@@ -1478,7 +1514,7 @@
     wide = x_in[...].astype(f32)
     norm = lax.rsqrt(jnp.mean(wide * wide, axis=1, keepdims=True) + EPS)
     z_own = wide * norm
-    w = mine * gain_row_in[...]
+    w = mine * gain_row_in[0:1, :]
     back = norm * (w - z_own * jnp.mean(w * z_own, axis=1, keepdims=True))
     input_grad_out[...] = (middle_grad_in[...] + back).astype(bf16)
     bias = jnp.sum(grads[...].astype(f32), axis=0, keepdims=True)
@@ -1701,7 +1737,6 @@
     per_head = query_bias.shape[1]
     q_width = heads * head_dim
     hidden = gate_weight.shape[1]
-    block = -(-hidden // (PLANE * 128)) * 128
     lines = dp_size // PLANE
     members = TREE_TOK // local_tok
     dp_index = lax.axis_index("dp")
@@ -1721,8 +1756,6 @@
         second = jnp.where(core == 0, other, mine)
         return jnp.concatenate([first, second], axis=0)
 
-    blocked = lambda w: jnp.pad(w, ((0, 0), (0, PLANE * block - hidden))).reshape(shard, PLANE, block).transpose(1, 0, 2)
-    ff_blocks = jnp.stack([blocked(gate_weight), blocked(up_weight), blocked(down_weight.T)])
     first_own = jnp.concatenate([query_weight, key_weight, value_weight], axis=1)
     biases = jnp.concatenate([query_bias, key_bias, value_bias], axis=0)
     bias_row = lax.dynamic_update_slice(
@@ -1737,10 +1770,11 @@
     cosines, sines = rope_tables(positions)
     plan, hot = attention_plan(segment_ids, parent_ids, dp_index, local_tok)
     steps = lines - 3
-    outs = front(ff_blocks, first_own, output_weight.T, extra, layer_input, cosines, sines, lines, members)
+    outs = front(
+        gate_weight, up_weight, down_weight.T, first_own, output_weight.T, extra, layer_input, cosines, sines, lines, members
+    )
     slab, ups, downs = outs[0], list(outs[1 : 1 + steps]), list(outs[1 + steps : 1 + 2 * steps])
     late_up, late_down, first_all, out_t, q_rot, tree, normed, rows = outs[1 + 2 * steps :]
-    gain_one, gain_two = rows[0:1], rows[1:2]
 
     attended, lse, middle, normed_two, other, cot_came, *more = attend(
         plan, hot, q_rot, tree, out_t, layer_input, rows, out_cotangent, ups[-1], downs[-1], late_up, late_down,
@@ -1748,17 +1782,17 @@
     )
 
     normed_two_grad, y_own, y_other, ff_parts, up_first, down_first = feed_forward(
-        normed_two, out_cotangent, cot_came, [slab] + ups + downs + [late_up, late_down] + more, lines
+        normed_two, out_cotangent, cot_came, [slab] + ups + downs + [late_up, late_down] + more, lines, hidden
     )
 
-    ff_parts = ff_parts.reshape(3, lines, width // lines, block)
+    ff_parts = ff_parts.reshape(3, lines, width // lines, ff_parts.shape[-1])
 
     dq, dtree, middle_grad, gain_two_grad, line_o, layer_output, up_next, down_next = attend_back(
         plan, hot, q_rot, attended, lse, tree, other, out_t, normed_two_grad, middle, out_cotangent, rows, cosines, sines,
         y_own, y_other, ff_parts, up_first, down_first, lines, members, scale,
     )
     input_grad, sums, small, ff_sums = finish(
-        dtree, dq, cosines, sines, normed, first_all, line_o, layer_input, gain_two_grad, gain_one,
+        dtree, dq, cosines, sines, normed, first_all, line_o, layer_input, gain_two_grad, rows,
         middle_grad, ff_parts, up_next, down_next, lines, members, scale,
     )
     ff_sums = ff_sums[:, :, :hidden].astype(f32)

time: 580 us -> 571 us (0.984)
  Pallas kernels: 545 us -> 538 us
where the time goes in v5:
time: 571 us; the launch traced here: 562 us
  Pallas kernels  538 us (94%)
  local copies, waits for them, and re-layouts  12.9 us (2%)
  other arithmetic  10.2 us (2%)
    pallas_call x1, Pallas kernels, front(): pl.pallas_call(functools.partial(front_kernel, lines=lines, members=membe...  154 us
    pallas_call x1, Pallas kernels, feed_forward(): pl.pallas_call(functools.partial(ff_kernel, tile_h=tile_h, tile_n=tile_n,...  151 us
    pallas_call x1, Pallas kernels, finish(): pl.pallas_call(functools.partial(back_kernel, lines=lines, members=member...  118 us
    pallas_call x1, Pallas kernels, attend_back(): pl.pallas_call(functools.partial(attend_back_kernel, lines=lines, members...  70.3 us
    pallas_call x1, Pallas kernels, attend(): pl.pallas_call(functools.partial(attend_kernel, lines=lines, members=memb...  44.6 us

profile of v5, /device:TPU:0, one launch (start us, length us, event | category | flops | bytes accessed | tf_op | source)
XLA Modules:
  0.0 562.3 jit_solution(7069773162208269548)
XLA Ops:
  0.7 0.7 pad_maximum_fusion.4
  1.5 0.7 pad_maximum_fusion.3
  2.4 0.7 convert_element_type.8
  3.2 0.7 dynamic_slice.9
  4.1 0.8 select_reduce_fusion.1
  5.5 0.6 reshape.229.info
  6.2 0.6 select_n.167.hot
  6.8 0.7 fusion.4.refs_5_
  7.4 1.6 pad_maximum_fusion.2.refs_3_
  9.1 1.2 fusion
  10.3 1.1 pad_maximum_fusion
  11.4 153.5 %front.1 = (bf16[3,384,1152]{2,1,0:T(8,128)(2,1)}, bf16[3,384,1152]{2,1,0:T(8,128)(2,1)}, bf16[3,384,1152]{2,1,0:T(8,128)(2,1)}, bf16[2,384,1152]{2,1,0:T(8,128)...) custom-call(bf16[96,4480]{1,0:T(8,128)(2,1)} %refs_0_.1, ...), custom_call_target="tpu_custom_call" | custom-call | flops 2013265920 | bytes 31457280 | tf_op jit(solution)/shard_map/front/pallas_call | solution.py:862
  164.9 44.6 %attend.1 = (bf16[640,768]{1,0:T(8,128)(2,1)}, f32[5,8,768]{2,1,0:T(8,128)}, f32[320,1536]{1,0:T(8,128)}, bf16[320,1536]{1,0:T(8,128)(2,1)}, bf16[5,256,256]{2,1...) custom-call(s32[10]{0:T(128)} %reshape.229.info, ...), custom_call_target="tpu_custom_call" | custom-call | flops 4529848320 | bytes 12582912 | tf_op jit(solution)/shard_map/attend/pallas_call | solution.py:225
  209.5 151.0 %feed_forward.1 = (f32[320,1536]{1,0:T(8,128)}, bf16[4,320,1536]{2,1,0:T(8,128)(2,1)}, bf16[4,320,1536]{2,1,0:T(8,128)(2,1)}, bf16[3,1536,1152]{2,1,0:T(8,128)(2...) custom-call(bf16[320,1536]{1,0:T(8,128)(2,1)} %get-tuple-element.64.refs_0_, bf16[320,1536]{1,0:T(8,128)(2,1)} %cot_in.3, ...), custom_call_target="tpu_custom_call" | custom-call | flops 81537269760 | bytes 62914560 | tf_op jit(solution)/shard_map/feed_forward/pallas_call | solution.py:1229
  360.5 70.3 %attend_back.1 = (bf16[640,768]{1,0:T(8,128)(2,1)}, bf16[5120,256]{1,0:T(8,128)(2,1)}, f32[320,1536]{1,0:T(8,128)}, f32[1,1536]{1,0:T(1,128)}, bf16[4,96,768]{2,...) custom-call(s32[10]{0:T(128)} %reshape.229.info, ...), custom_call_target="tpu_custom_call" | custom-call | flops 11324620800 | bytes 31457280 | tf_op jit(solution)/shard_map/attend_back/pallas_call | solution.py:483
  430.9 118.5 %back.1 = (bf16[320,1536]{1,0:T(8,128)(2,1)}, f32[96,1792]{1,0:T(8,128)}, f32[8,1536]{1,0:T(8,128)}, bf16[3,96,4608]{2,1,0:T(8,128)(2,1)}) custom-call(bf16[5120,256]{1,0:T(8,128)(2,1)} %get-tuple-element.79.dkv_in, bf16[640,768]{1,0:T(8,128)(2,1)} %get-tuple-element.80.dq_in, f32[640,128]{1,0:T(8,128)} %get-tuple-element.110.refs_7_.cos_in, ...), custom_call_target="tpu_custom_call" | custom-call | flops 6039797760 | bytes 41943040 | tf_op jit(solution)/shard_map/back/pallas_call | solution.py:1616
  549.3 0.8 slice.56
  550.1 0.8 slice.53
  552.1 1.5 fusion.14
  553.5 1.9 slice_bitcast_fusion.3
  555.4 2.1 slice_convert_fusion
  557.6 2.4 slice_bitcast_fusion
  560.0 0.9 copy.41
  560.9 0.9 copy.42
  (28 shorter events, 2.3 us)
Async XLA Ops:
  551.0 6.5 %copy-start.2 = (f32[8,8]{1,0:T(8,128)}, f32[8,8]{1,0:T(8,128)S(1)}, u32[]{:S(2)}) copy-start(f32[8,8]{1,0:T(8,128)S(1)} %constant_dynamic-slice_fusion) | copy-start | bytes 772
  557.5 2.5 copy-start
  557.5 3.4 copy-start.1

commit v6 on v5

--- a/solution.py
+++ b/solution.py
@@ -785,11 +785,9 @@
         recv_sem=pair_recv.at[0], device_id={"dp": line_partner(dp)}, device_id_type=MESH).wait_recv()
     for bits in range(1, PLANE):
         pair_copy(bits, True).start()
-    for step in range(lines - 1):
-        for sign in (1, -1):
-            outer.arrived(sign, step)
-    for step in range(steps):
-        for which in (2, 0, 1):
+
+    def pass_on(which):
+        for step in range(steps):
             for sign in (1, -1):
                 place = z_at if sign == 1 else lines - 1 - z_at
 
@@ -808,6 +806,12 @@
                         def _():
                             late_hop(LATE.index(which), sign).start()
 
+    pass_on(2)
+    for step in range(lines - 1):
+        for sign in (1, -1):
+            outer.arrived(sign, step)
+    pass_on(0)
+    pass_on(1)
     for bits in range(1, PLANE):
         pair_copy(bits).wait_recv()
         pair_copy(bits, True).wait_recv()
@@ -1533,7 +1537,6 @@
     small_copy.start()
     plane_sum("q")
     plane_sum("kv")
-    line_done(1)
 
     small_copy.wait_recv()
     gain_rows = lax.broadcasted_iota(jnp.int32, (8, width), 0) < 2
@@ -1562,6 +1565,7 @@
     for apart in range(1, lines):
         small_line_copy(apart).start()
     line_sum("o")
+    line_done(1)
     line_sum("q")
     line_sum("kv")
     for apart in range(1, lines):

time: 571 us -> 564 us (0.988)
  Pallas kernels: 538 us -> 531 us
where the time goes in v6:
time: 564 us; the launch traced here: 556 us
  Pallas kernels  531 us (94%)
  local copies, waits for them, and re-layouts  12.9 us (2%)
  other arithmetic  10.2 us (2%)
    pallas_call x1, Pallas kernels, front(): pl.pallas_call(functools.partial(front_kernel, lines=lines, members=membe...  152 us
    pallas_call x1, Pallas kernels, feed_forward(): pl.pallas_call(functools.partial(ff_kernel, tile_h=tile_h, tile_n=tile_n,...  151 us
    pallas_call x1, Pallas kernels, finish(): pl.pallas_call(functools.partial(back_kernel, lines=lines, members=member...  113 us
    pallas_call x1, Pallas kernels, attend_back(): pl.pallas_call(functools.partial(attend_back_kernel, lines=lines, members...  70.4 us
    pallas_call x1, Pallas kernels, attend(): pl.pallas_call(functools.partial(attend_kernel, lines=lines, members=memb...  44.6 us

profile of v6, /device:TPU:0, one launch (start us, length us, event | category | flops | bytes accessed | tf_op | source)
XLA Modules:
  0.0 555.5 jit_solution(5526187896287621190)
XLA Ops:
  0.7 0.7 pad_maximum_fusion.4
  1.5 0.7 pad_maximum_fusion.3
  2.4 0.7 convert_element_type.8
  3.2 0.7 dynamic_slice.9
  4.1 0.8 select_reduce_fusion.1
  5.5 0.6 reshape.229.info
  6.2 0.6 select_n.167.hot
  6.8 0.7 fusion.4.refs_5_
  7.4 1.6 pad_maximum_fusion.2.refs_3_
  9.1 1.2 fusion
  10.3 1.1 pad_maximum_fusion
  11.4 152.2 %front.1 = (bf16[3,384,1152]{2,1,0:T(8,128)(2,1)}, bf16[3,384,1152]{2,1,0:T(8,128)(2,1)}, bf16[3,384,1152]{2,1,0:T(8,128)(2,1)}, bf16[2,384,1152]{2,1,0:T(8,128)...) custom-call(bf16[96,4480]{1,0:T(8,128)(2,1)} %refs_0_.1, ...), custom_call_target="tpu_custom_call" | custom-call | flops 2013265920 | bytes 31457280 | tf_op jit(solution)/shard_map/front/pallas_call | solution.py:866
  163.6 44.6 %attend.1 = (bf16[640,768]{1,0:T(8,128)(2,1)}, f32[5,8,768]{2,1,0:T(8,128)}, f32[320,1536]{1,0:T(8,128)}, bf16[320,1536]{1,0:T(8,128)(2,1)}, bf16[5,256,256]{2,1...) custom-call(s32[10]{0:T(128)} %reshape.229.info, ...), custom_call_target="tpu_custom_call" | custom-call | flops 4529848320 | bytes 12582912 | tf_op jit(solution)/shard_map/attend/pallas_call | solution.py:225
  208.2 151.0 %feed_forward.1 = (f32[320,1536]{1,0:T(8,128)}, bf16[4,320,1536]{2,1,0:T(8,128)(2,1)}, bf16[4,320,1536]{2,1,0:T(8,128)(2,1)}, bf16[3,1536,1152]{2,1,0:T(8,128)(2...) custom-call(bf16[320,1536]{1,0:T(8,128)(2,1)} %get-tuple-element.64.refs_0_, bf16[320,1536]{1,0:T(8,128)(2,1)} %cot_in.3, ...), custom_call_target="tpu_custom_call" | custom-call | flops 81537269760 | bytes 62914560 | tf_op jit(solution)/shard_map/feed_forward/pallas_call | solution.py:1233
  359.2 70.4 %attend_back.1 = (bf16[640,768]{1,0:T(8,128)(2,1)}, bf16[5120,256]{1,0:T(8,128)(2,1)}, f32[320,1536]{1,0:T(8,128)}, f32[1,1536]{1,0:T(1,128)}, bf16[4,96,768]{2,...) custom-call(s32[10]{0:T(128)} %reshape.229.info, ...), custom_call_target="tpu_custom_call" | custom-call | flops 11324620800 | bytes 31457280 | tf_op jit(solution)/shard_map/attend_back/pallas_call | solution.py:483
  429.6 113.0 %back.1 = (bf16[320,1536]{1,0:T(8,128)(2,1)}, f32[96,1792]{1,0:T(8,128)}, f32[8,1536]{1,0:T(8,128)}, bf16[3,96,4608]{2,1,0:T(8,128)(2,1)}) custom-call(bf16[5120,256]{1,0:T(8,128)(2,1)} %get-tuple-element.79.dkv_in, bf16[640,768]{1,0:T(8,128)(2,1)} %get-tuple-element.80.dq_in, f32[640,128]{1,0:T(8,128)} %get-tuple-element.110.refs_7_.cos_in, ...), custom_call_target="tpu_custom_call" | custom-call | flops 6039797760 | bytes 41943040 | tf_op jit(solution)/shard_map/back/pallas_call | solution.py:1620
  542.5 0.8 slice.56
  543.3 0.8 slice.53
  545.3 1.5 fusion.14
  546.7 1.9 slice_bitcast_fusion.3
  548.6 2.1 slice_convert_fusion
  550.7 2.4 slice_bitcast_fusion
  553.2 0.9 copy.41
  554.1 0.9 copy.42
  (28 shorter events, 2.3 us)
Async XLA Ops:
  544.2 6.5 %copy-start.2 = (f32[8,8]{1,0:T(8,128)}, f32[8,8]{1,0:T(8,128)S(1)}, u32[]{:S(2)}) copy-start(f32[8,8]{1,0:T(8,128)S(1)} %constant_dynamic-slice_fusion) | copy-start | bytes 772
  550.7 2.5 copy-start
  550.7 3.4 copy-start.1

commit v7 on v6

--- a/solution.py
+++ b/solution.py
@@ -1068,14 +1068,11 @@
     def dx_half(k, r):
         at = rows(k, r)
 
-        @pl.loop(0, width // tile_n)
-        def _(t):
-            cols = pl.ds(pl.multiple_of(t * tile_n, tile_n), tile_n)
-            part = dot_nt(gate_g[at, :], gate_w[cols, :]) + dot_nt(up_g[at, :], up_w[cols, :])
-            if r:
-                far[k, :, cols] = part.astype(bf16)
-            else:
-                near[k, :, cols] = (part + near[k, :, cols].astype(jnp.float32)).astype(bf16)
+        part = dot_nt(gate_g[at, :], gate_w[...]) + dot_nt(up_g[at, :], up_w[...])
+        if r:
+            far[k] = part.astype(bf16)
+        else:
+            near[k] = (part + near[k].astype(jnp.float32)).astype(bf16)
 
     def dx_first(k):
         dx_half(k, 1)

time: 564 us -> 555 us (0.984)
  Pallas kernels: 531 us -> 523 us
    pallas_call x1, Pallas kernels: 151 us -> 142 us  [feed_forward(): pl.pallas_call(functools.partial(ff_kernel, tile_h=tile_h, tile_n=tile_n,...]
where the time goes in v7:
time: 555 us; the launch traced here: 547 us
  Pallas kernels  523 us (94%)
  local copies, waits for them, and re-layouts  12.9 us (2%)
  other arithmetic  10.2 us (2%)
    pallas_call x1, Pallas kernels, front(): pl.pallas_call(functools.partial(front_kernel, lines=lines, members=membe...  152 us
    pallas_call x1, Pallas kernels, feed_forward(): pl.pallas_call(functools.partial(ff_kernel, tile_h=tile_h, tile_n=tile_n,...  142 us
    pallas_call x1, Pallas kernels, finish(): pl.pallas_call(functools.partial(back_kernel, lines=lines, members=member...  113 us
    pallas_call x1, Pallas kernels, attend_back(): pl.pallas_call(functools.partial(attend_back_kernel, lines=lines, members...  70.8 us
    pallas_call x1, Pallas kernels, attend(): pl.pallas_call(functools.partial(attend_kernel, lines=lines, members=memb...  44.6 us

profile of v7, /device:TPU:0, one launch (start us, length us, event | category | flops | bytes accessed | tf_op | source)
XLA Modules:
  0.0 546.8 jit_solution(2580027465508600158)
XLA Ops:
  0.7 0.7 pad_maximum_fusion.4
  1.5 0.7 pad_maximum_fusion.3
  2.4 0.7 convert_element_type.8
  3.2 0.7 dynamic_slice.9
  4.1 0.8 select_reduce_fusion.1
  5.5 0.6 reshape.229.info
  6.2 0.6 select_n.167.hot
  6.8 0.7 fusion.4.refs_5_
  7.4 1.6 pad_maximum_fusion.2.refs_3_
  9.1 1.2 fusion
  10.3 1.1 pad_maximum_fusion
  11.4 152.2 %front.1 = (bf16[3,384,1152]{2,1,0:T(8,128)(2,1)}, bf16[3,384,1152]{2,1,0:T(8,128)(2,1)}, bf16[3,384,1152]{2,1,0:T(8,128)(2,1)}, bf16[2,384,1152]{2,1,0:T(8,128)...) custom-call(bf16[96,4480]{1,0:T(8,128)(2,1)} %refs_0_.1, ...), custom_call_target="tpu_custom_call" | custom-call | flops 2013265920 | bytes 31457280 | tf_op jit(solution)/shard_map/front/pallas_call | solution.py:866
  163.6 44.6 %attend.1 = (bf16[640,768]{1,0:T(8,128)(2,1)}, f32[5,8,768]{2,1,0:T(8,128)}, f32[320,1536]{1,0:T(8,128)}, bf16[320,1536]{1,0:T(8,128)(2,1)}, bf16[5,256,256]{2,1...) custom-call(s32[10]{0:T(128)} %reshape.229.info, ...), custom_call_target="tpu_custom_call" | custom-call | flops 4529848320 | bytes 12582912 | tf_op jit(solution)/shard_map/attend/pallas_call | solution.py:225
  208.2 141.8 %feed_forward.1 = (f32[320,1536]{1,0:T(8,128)}, bf16[4,320,1536]{2,1,0:T(8,128)(2,1)}, bf16[4,320,1536]{2,1,0:T(8,128)(2,1)}, bf16[3,1536,1152]{2,1,0:T(8,128)(2...) custom-call(bf16[320,1536]{1,0:T(8,128)(2,1)} %get-tuple-element.64.refs_0_, bf16[320,1536]{1,0:T(8,128)(2,1)} %cot_in.3, ...), custom_call_target="tpu_custom_call" | custom-call | flops 81537269760 | bytes 62914560 | tf_op jit(solution)/shard_map/feed_forward/pallas_call | solution.py:1230
  350.0 70.8 %attend_back.1 = (bf16[640,768]{1,0:T(8,128)(2,1)}, bf16[5120,256]{1,0:T(8,128)(2,1)}, f32[320,1536]{1,0:T(8,128)}, f32[1,1536]{1,0:T(1,128)}, bf16[4,96,768]{2,...) custom-call(s32[10]{0:T(128)} %reshape.229.info, ...), custom_call_target="tpu_custom_call" | custom-call | flops 11324620800 | bytes 31457280 | tf_op jit(solution)/shard_map/attend_back/pallas_call | solution.py:483
  420.9 113.2 %back.1 = (bf16[320,1536]{1,0:T(8,128)(2,1)}, f32[96,1792]{1,0:T(8,128)}, f32[8,1536]{1,0:T(8,128)}, bf16[3,96,4608]{2,1,0:T(8,128)(2,1)}) custom-call(bf16[5120,256]{1,0:T(8,128)(2,1)} %get-tuple-element.79.dkv_in, bf16[640,768]{1,0:T(8,128)(2,1)} %get-tuple-element.80.dq_in, f32[640,128]{1,0:T(8,128)} %get-tuple-element.110.refs_7_.cos_in, ...), custom_call_target="tpu_custom_call" | custom-call | flops 6039797760 | bytes 41943040 | tf_op jit(solution)/shard_map/back/pallas_call | solution.py:1617
  534.0 0.8 slice.56
  534.8 0.8 slice.53
  536.8 1.5 fusion.14
  538.3 1.9 slice_bitcast_fusion.3
  540.2 2.1 slice_convert_fusion
  542.3 2.4 slice_bitcast_fusion
  544.7 0.9 copy.41
  545.6 0.9 copy.42
  (28 shorter events, 2.3 us)
Async XLA Ops:
  535.8 6.5 %copy-start.2 = (f32[8,8]{1,0:T(8,128)}, f32[8,8]{1,0:T(8,128)S(1)}, u32[]{:S(2)}) copy-start(f32[8,8]{1,0:T(8,128)S(1)} %constant_dynamic-slice_fusion) | copy-start | bytes 772
  542.2 2.5 copy-start
  542.2 3.4 copy-start.1
